TPU v7x, 256 devices: a whole 4x4x8 slice. The times are simulated.
256 devices in a mesh: blk: 8 (over y_hi, x), branch: 32 (over z, y_lo, core).
Axes of the slice: x: 4, y: 4 (y_hi: 2, y_lo: 2; y = y_hi * 2 + y_lo), z: 8, core: 2. Of those that a mesh axis runs over, the one named last changes fastest.
Arguments:
- counts: int32 [2048, 16384], P('blk', 'branch'), may hold values from 0 to 192, as said below
- totals: int32 [2048], P('blk'), may hold values from 1 to 3145728, as said below
- lengths: int32 [16384], P('branch'), may hold values from 1 to 999
Outputs:
- distances: float32 [2048, 2048], P('blk')
Inputs may be any that keep to these rules, and one draw needn't show every extreme that they name: `counts`: counts_ik is the whole number of reads of sample i below branch k. `totals`: totals_i equals the sum of counts_ik over all 16384 branches.
All inputs are finite; a program needn't handle non-finite values.
Results may differ from a plain program's by a relative error of at most 0.00002.
Values sent between devices are 32-bit elements; how exact they have to be, the bound alone decides.
No kernel may reach another device: no remote copies, remote signals or barrier semaphores. Data moves between devices by JAX's collectives and lax.ppermute only.
A program may use at most 64 MiB of HBM per device.

v0:
```python
import jax
import jax.numpy as jnp
from jax import lax
from jax.experimental import pallas as pl
from jax.experimental.pallas import tpu as pltpu
from jax.sharding import PartitionSpec as P

F32 = jnp.float32
BF16 = jnp.bfloat16
ROWS = 256
KS = 512
BLOCKS = 8
GROUP = 8
PAIRS = GROUP // 2
GROUPS = ROWS // GROUP


def block_at(y, x):
    return (y % 2) * 4 + x % 4


def partner_tables():
    first, second, third, fourth = [], [], [], []
    for b in range(BLOCKS):
        y, x = b // 4, b % 4
        first.append(block_at(y, x + 1))
        second.append(block_at(y + 1, x + 3))
        cycle = {(0, 0): (0, 2), (0, 1): (1, 2), (1, 1): (1, 0), (1, 0): (0, 0)}
        ny, nx = cycle[(y, x // 2)]
        third.append(block_at(ny, nx + x % 2))
        fourth.append(block_at(y + 1, x + 2))
    return [first, second, third, fourth]


PARTNERS = partner_tables()
OWNERS = [[table.index(b) for b in range(BLOCKS)] for table in PARTNERS]


def params():
    return pltpu.CompilerParams(vmem_limit_bytes=56 << 20)


def in_vmem(n):
    return [pl.BlockSpec(memory_space=pltpu.VMEM)] * n


def branch_sums(ref, lane):
    def add(k8, total):
        at = pl.ds(pl.multiple_of(k8 * 8, 8), 8)
        return total + ref[at, lane : lane + 128]

    total = lax.fori_loop(0, KS // 8, add, jnp.zeros((8, 128), F32), unroll=8)
    return jnp.sum(total, axis=0, keepdims=True)


def weigh_kernel(counts_ref, totals_ref, lengths_ref, wt_ref, split_ref, row_ref, col_ref):
    scaled = lengths_ref[...].astype(F32) * 0.001
    wt = (scaled * counts_ref[...].astype(F32)).T / totals_ref[...].astype(F32)
    wt_ref[...] = wt
    for n in range(8):
        x = wt[:, n * 32 : (n + 1) * 32]
        high = x.astype(BF16)
        rest = x - high.astype(F32)
        middle = rest.astype(BF16)
        low = (rest - middle.astype(F32)).astype(BF16)
        split_ref[n] = jnp.concatenate([high, middle, low, jnp.zeros_like(low)], axis=1)
    for h in range(2):
        sums = branch_sums(wt_ref, h * 128)
        row_ref[:, h * 128 : (h + 1) * 128] = jnp.broadcast_to(sums, (8, 128))
        col_ref[h * 128 : (h + 1) * 128, :] = jnp.broadcast_to(sums, (128, 128)).T


def weigh(counts, totals, lengths):
    return pl.pallas_call(
        weigh_kernel,
        out_shape=(
            jax.ShapeDtypeStruct((KS, ROWS), F32),
            jax.ShapeDtypeStruct((8, KS, 128), BF16),
            jax.ShapeDtypeStruct((8, ROWS), F32),
            jax.ShapeDtypeStruct((ROWS, 128), F32),
        ),
        compiler_params=params(),
        name="weigh",
    )(counts, totals.reshape(1, ROWS), lengths.reshape(1, KS))


def spread_call(name, n_blocks, columns, mass_lanes, width):
    def kernel(at_ref, split_ref, col_ref, *refs):
        blocks = refs[:n_blocks]
        out_ref, mass_ref, pick_ref, even_ref, odd_ref = refs[n_blocks:]
        core, y = at_ref[0], at_ref[1]

        part = lax.broadcasted_iota(jnp.int32, (128, 256), 0)
        lane = lax.broadcasted_iota(jnp.int32, (128, 256), 1)
        want = jnp.where(part < 96, part % 32 - lane // 128, -1)
        for p in range(16):
            pick_ref[p] = jnp.where(want == 2 * p, 1.0, 0.0).astype(BF16)

        sums = [branch_sums(blocks[n], lane) for n, lane in mass_lanes]
        block = jnp.concatenate(sums + [jnp.zeros((8 - len(sums), 128), F32)], axis=0)
        mass_ref[...] = block

        def mass_row(n, lane):
            if isinstance(lane, int):
                return sums[mass_lanes.index((n, lane))]
            first = sums[mass_lanes.index((n, 0))]
            return jnp.where(lane == 0, first, sums[mass_lanes.index((n, 128))])

        def broadcast_pair(into, g, q):
            pair = g * PAIRS + q
            into[q] = jnp.dot(
                split_ref[pair // 16], pick_ref[pair % 16], preferred_element_type=F32
            )

        def one_group(g, half, now, later):
            cols = columns(half, y)
            n_cols = len(cols)
            following = jnp.minimum(g + 1, GROUPS - 1)
            for q in range(PAIRS):
                broadcast_pair(later, following, q)
            acc = [jnp.zeros((8, 128), F32)] * (GROUP * n_cols)
            for k8 in range(KS // 8):
                at = slice(k8 * 8, k8 * 8 + 8)
                spans = [
                    blocks[n][at, lane : lane + 128]
                    if isinstance(lane, int)
                    else blocks[n][at, pl.ds(pl.multiple_of(lane, 128), 128)]
                    for n, lane in cols
                ]
                for r in range(GROUP):
                    own = now[r // 2, at, 128 * (r % 2) : 128 * (r % 2) + 128]
                    for j in range(n_cols):
                        acc[r * n_cols + j] += jnp.minimum(own, spans[j])
            side = jnp.where(half == core, 0, 1)
            own_mass = col_ref[pl.ds(pl.multiple_of(g * GROUP, 8), 8), :]
            row = pl.multiple_of((g - half * (GROUPS // 2)) * GROUP, 8)
            for j, (n, lane) in enumerate(cols):
                least = jnp.concatenate(
                    [jnp.sum(acc[r * n_cols + j], axis=0, keepdims=True) for r in range(GROUP)],
                    axis=0,
                )
                out_ref[side, pl.ds(row, 8), 128 * j : 128 * j + 128] = (
                    own_mass + mass_row(n, lane) - 2.0 * least
                )

        for q in range(PAIRS):
            broadcast_pair(even_ref, 0, q)

        for half in range(2):

            def two_groups(t, carry, half=half):
                g = half * (GROUPS // 2) + 2 * t
                one_group(g, half, even_ref, odd_ref)
                one_group(g + 1, half, odd_ref, even_ref)
                return carry

            lax.fori_loop(0, GROUPS // 4, two_groups, 0)

    steps = sum(len(columns(h, 0)) for h in range(2)) * 128 * 128 * KS

    def call(at, split, col, *blocks):
        return pl.pallas_call(
            kernel,
            out_shape=(
                jax.ShapeDtypeStruct((2, 128, width), F32),
                jax.ShapeDtypeStruct((8, 128), F32),
            ),
            in_specs=[pl.BlockSpec(memory_space=pltpu.SMEM)] + in_vmem(2 + n_blocks),
            out_specs=tuple(in_vmem(2)),
            scratch_shapes=[
                pltpu.VMEM((16, 128, 256), BF16),
                pltpu.VMEM((PAIRS, KS, 256), F32),
                pltpu.VMEM((PAIRS, KS, 256), F32),
            ],
            compiler_params=params(),
            cost_estimate=pl.CostEstimate(
                flops=steps * 250, bytes_accessed=4 << 20, transcendentals=0
            ),
            name=name,
        )(at, split, col, *blocks)

    return call


def diagonal_columns(half, y):
    return [(0, 128), (0, 0)][: 2 - half]


def first_columns(half, y):
    return [(0, 0), (0, 128), (1, 0), (1, 128)]


def second_columns(half, y):
    return [(0, 0), (0, 128), (1, (half ^ y) * 128)]


def assemble_kernel(at_ref, own1, other1, own2, other2, out_ref, all_ref):
    core, y = at_ref[0], at_ref[1]
    n1 = own1.shape[2]
    for c, ref1, ref2 in ((core, own1, own2), (1 - core, other1, other2)):
        to = pl.ds(pl.multiple_of(c * 128, 128), 128)
        all_ref[to, 0:n1] = ref1[...].reshape(128, n1)
        all_ref[to, n1:] = ref2[...].reshape(128, all_ref.shape[1] - n1)

    def columns(slot, half=None):
        first = at_ref[2 + slot] * ROWS
        if half is None:
            return pl.ds(pl.multiple_of(first, ROWS), ROWS)
        return pl.ds(pl.multiple_of(first + half * 128, 128), 128)

    upper = all_ref[0:128, 0:128]
    out_ref[0:128, columns(0, 0)] = all_ref[0:128, 128:256]
    out_ref[0:128, columns(0, 1)] = upper
    out_ref[128:256, columns(0, 0)] = upper.T
    out_ref[128:256, columns(0, 1)] = all_ref[128:256, 0:128]
    for slot, lane in ((1, 256), (2, 512), (3, n1)):
        out_ref[:, columns(slot)] = all_ref[:, lane : lane + ROWS]
    for slot, lane in ((5, 768), (6, 1024), (7, n1 + 384)):
        out_ref[:, columns(slot)] = all_ref[:, lane : lane + ROWS].T
    for half in range(2):
        rows = slice(half * 128, half * 128 + 128)
        out_ref[rows, columns(4, half ^ y)] = all_ref[rows, n1 + 256 : n1 + 384]
        to = pl.ds(pl.multiple_of((half ^ (1 - y)) * 128, 128), 128)
        out_ref[to, columns(4, half)] = all_ref[rows, n1 + 640 : n1 + 768].T


def assemble(at, own1, other1, own2, other2):
    return pl.pallas_call(
        assemble_kernel,
        out_shape=jax.ShapeDtypeStruct((ROWS, BLOCKS * ROWS), F32),
        in_specs=[pl.BlockSpec(memory_space=pltpu.SMEM)] + in_vmem(4),
        out_specs=in_vmem(1)[0],
        scratch_shapes=[pltpu.VMEM((ROWS, own1.shape[2] + own2.shape[2]), F32)],
        compiler_params=params(),
        name="assemble",
    )(at, own1, other1, own2, other2)


def on_device(counts, totals, lengths):
    blk = lax.axis_index("blk")
    branch = lax.axis_index("branch")
    core, place = branch % 2, branch // 2
    y_hi = blk // 4
    tables = jnp.array([list(range(BLOCKS))] + PARTNERS + OWNERS[:3], jnp.int32)
    slots = lax.dynamic_index_in_dim(tables, blk, 1, False)
    at = jnp.concatenate([jnp.stack([core, y_hi]).astype(jnp.int32), slots])

    def from_partner(v, n):
        return lax.ppermute(v, "blk", [(PARTNERS[n][b], b) for b in range(BLOCKS)])

    def to_partner(v, n):
        return lax.ppermute(v, "blk", [(b, PARTNERS[n][b]) for b in range(BLOCKS)])

    def other_core(v):
        return lax.ppermute(v, "branch", [(i, i ^ 1) for i in range(32)])

    chips = [[2 * p + c for p in range(16)] for c in range(2)]

    def over_chips(v):
        return lax.all_to_all(v, "branch", 0, 0, axis_index_groups=chips)

    wt, split, mass_row, mass_col = weigh(counts, totals, lengths)
    got = [from_partner(wt, n) for n in range(4)]

    diagonal = spread_call("diagonal", 1, diagonal_columns, [(0, 0), (0, 128)], 256)
    first = spread_call(
        "first", 2, first_columns, [(0, 0), (0, 128), (1, 0), (1, 128)], 512
    )
    second = spread_call(
        "second", 2, second_columns, [(0, 0), (0, 128), (1, 0), (1, 128)], 384
    )

    def on_chip(parts):
        out, mass = parts
        return out[0] + other_core(out[1]), mass + other_core(mass)

    def scatter(tiles, masses):
        tiles = jnp.concatenate(tiles, axis=1).reshape(16, 8, -1)
        masses = jnp.broadcast_to(masses[None], (16, 8, 128))
        shard = jnp.sum(over_chips(jnp.concatenate([tiles, masses], axis=2)), axis=0)
        return shard[:, :-128], shard[:, -128:]

    def gather(pieces):
        mine = jnp.concatenate(pieces, axis=1)
        whole = over_chips(jnp.broadcast_to(mine[None], (16, *mine.shape)))
        return whole, other_core(whole)

    tile0, sums0 = on_chip(diagonal(at, split, mass_col, wt))
    tile1, sums1 = on_chip(first(at, split, mass_col, got[0], got[1]))
    tile2, sums2 = on_chip(second(at, split, mass_col, got[2], got[3]))

    sums = jnp.concatenate([sums0[0:2], sums1[0:4], sums0[6:8]])
    shard, sums = scatter([tile0, tile1], sums)
    own_mass = lax.dynamic_slice_in_dim(
        sums[0:2].reshape(ROWS), core * 128 + place * 8, 8
    )[:, None]
    parts = jnp.concatenate([sums[1], sums[0], sums[2:6].reshape(512)])
    dist1 = shard / (own_mass + parts[None, :])
    swapped1 = [to_partner(dist1[:, 256 * (n + 1) : 256 * (n + 2)], n) for n in range(2)]
    own1, other1 = gather([dist1, *swapped1])

    shard, sums = scatter([tile2], sums2)
    last = jnp.where((core ^ y_hi) == 0, sums[2], sums[3])
    parts = jnp.concatenate([sums[0], sums[1], last])
    dist2 = shard / (own_mass + parts[None, :])
    swapped2 = [to_partner(dist2[:, 0:256], 2), to_partner(dist2[:, 256:384], 3)]
    own2, other2 = gather([dist2, *swapped2])

    return assemble(at, own1, other1, own2, other2)


def solution(mesh):
    placed = (P("blk", "branch"), P("blk"), P("branch"))
    return jax.shard_map(
        on_device, mesh=mesh, in_specs=placed, out_specs=P("blk", None), check_vma=False
    )
```

profile of v0, /device:TPU:1, one launch (start us, length us, event | category | flops | bytes accessed | tf_op | source)
XLA Modules:
  0.0 179.7 jit_solution(2962656766607172088)
XLA Ops:
  0.0 3.4 %weigh.1 = (f32[512,256]{1,0:T(8,128)}, bf16[8,512,128]{2,1,0:T(8,128)(2,1)}, f32[8,256]{1,0:T(8,128)}, f32[256,128]{1,0:T(8,128)}) custom-call(s32[256,512]{1,0:T(8,128)} %counts_ref.1, s32[1,256]{1,0:T(1,128)} %bitcast.39, s32[1,512]{1,0:T(1,128)} %bitcast.38), custom_call_target="tpu_custom_call" | custom-call | tf_op jit(solution)/shard_map/weigh/pallas_call | solution.py:74
  3.4 6.2 %collective-permute-start.10 = (f32[512,256]{1,0:T(8,128)}, f32[512,256]{1,0:T(8,128)S(1)}, u32[]{:S(2)}, u32[]{:S(2)}) collective-permute-start(f32[512,256]{1,0:T(8,128)} %get-tuple-element.16.refs_0_), channel_id=1, source_target_pairs={{192,0},{224,32},{128,64},{160,96},{64,128},{96,160},{0,192},{32,2... | collective-permute-start | bytes 1572872 | tf_op jit(solution)/shard_map/ppermute | solution.py:249
  10.8 1.5 collective-permute-start.1
  13.6 14.4 %diagonal.1 = (f32[2,128,256]{2,1,0:T(8,128)}, f32[8,128]{1,0:T(8,128)}) custom-call(s32[10]{0:T(128)} %pad_add_fusion.at_ref, bf16[8,512,128]{2,1,0:T(8,128)(2,1)} %get-tuple-element.14.split_ref, f32[256,128]{1,0:T(8,128)} %get-tuple-element.15.col_ref, f32[512,256]{1,0:T(8,128)} %get-tuple-element.16.refs_0_), custom_call_target="tpu_custom_call" | custom-call | flops 6291456000 | bytes 4194304 | tf_op jit(solution)/shard_map/diagonal/pallas_call | solution.py:162
  28.0 3.5 %collective-permute-start.4 = (f32[8,128]{1,0:T(8,128)}, f32[8,128]{1,0:T(8,128)S(1)}, u32[]{:S(2)}, u32[]{:S(2)}) collective-permute-start(f32[8,128]{1,0:T(8,128)} %get-tuple-element.19), channel_id=1, source_target_pairs={{0,1},{1,0},{2,3},{3,2},{4,5},{5,4},{6,7},{7,6},{8,9},{9,8},{10,11... | collective-permute-start | bytes 12296 | tf_op jit(solution)/shard_map/ppermute | solution.py:255
  35.2 24.4 %first.1 = (f32[2,128,512]{2,1,0:T(8,128)}, f32[8,128]{1,0:T(8,128)}) custom-call(s32[10]{0:T(128)} %pad_add_fusion.at_ref, bf16[8,512,128]{2,1,0:T(8,128)(2,1)} %get-tuple-element.14.split_ref, f32[256,128]{1,0:T(8,128)} %get-tuple-element.15.col_ref, f32[512,256]{1,0:T(8,128)} %copy-done.8, f32[512,256]{1,0:T(8,128)} %copy-done.7), custom_call_target="tpu_custom_call" | custom-call | flops 16777216000 | bytes 4194304 | tf_op jit(solution)/shard_map/first/pallas_call | solution.py:162
  64.3 9.3 %all-to-all-start = ((f32[16,8,896]{2,1,0:T(8,128)}), f32[16,8,896]{2,1,0:T(8,128)S(1)}, u32[]{:S(2)}, u32[]{:S(2)}) async-start(f32[16,8,896]{2,1,0:T(8,128)} %pad_maximum_fusion), calls=%async_computation | async-start | bytes 917504 | tf_op jit(solution)/shard_map/all_to_all | solution.py:260
  75.2 20.5 %second.1 = (f32[2,128,384]{2,1,0:T(8,128)}, f32[8,128]{1,0:T(8,128)}) custom-call(s32[10]{0:T(128)} %pad_add_fusion.at_ref, bf16[8,512,128]{2,1,0:T(8,128)(2,1)} %get-tuple-element.14.split_ref, f32[256,128]{1,0:T(8,128)} %get-tuple-element.15.col_ref, f32[512,256]{1,0:T(8,128)} %copy-done.6, f32[512,256]{1,0:T(8,128)} %copy-done.5), custom_call_target="tpu_custom_call" | custom-call | flops 12582912000 | bytes 4194304 | tf_op jit(solution)/shard_map/second/pallas_call | solution.py:162
  97.3 1.3 collective-permute-done.12
  100.9 7.8 %all-to-all-start.2 = ((f32[16,8,512]{2,1,0:T(8,128)}), f32[16,8,512]{2,1,0:T(8,128)S(1)}, u32[]{:S(2)}, u32[]{:S(2)}) async-start(f32[16,8,512]{2,1,0:T(8,128)} %pad_maximum_fusion.1), calls=%async_computation.2 | async-start | bytes 524288 | tf_op jit(solution)/shard_map/all_to_all | solution.py:260
  109.0 12.6 %collective-permute-start.6 = (f32[8,256]{1,0:T(8,128)S(1)}, f32[8,256]{1,0:T(8,128)S(1)}, u32[]{:S(2)}, u32[]{:S(2)}) collective-permute-start(f32[8,256]{1,0:T(8,128)S(1)} %get-tuple-element.25), channel_id=1, source_target_pairs={{0,32},{32,64},{64,96},{96,0},{128,160},{160,192},{192,224},{224,1... | collective-permute-start | bytes 24584 | tf_op jit(solution)/shard_map/ppermute | solution.py:252
  121.7 3.8 %collective-permute-start.7 = (f32[8,256]{1,0:T(8,128)S(1)}, f32[8,256]{1,0:T(8,128)S(1)}, u32[]{:S(2)}, u32[]{:S(2)}) collective-permute-start(f32[8,256]{1,0:T(8,128)S(1)} %get-tuple-element.26), channel_id=1, source_target_pairs={{0,224},{32,128},{64,160},{96,192},{128,96},{160,0},{192,32},{224,... | collective-permute-start | bytes 24584 | tf_op jit(solution)/shard_map/ppermute | solution.py:252
  125.4 1.2 collective-permute-done.7
  127.5 7.6 %all-to-all-start.1 = ((f32[16,8,1280]{2,1,0:T(8,128)}), f32[16,8,1280]{2,1,0:T(8,128)S(1)}, u32[]{:S(2)}, u32[]{:S(2)}) async-start(f32[16,8,1280]{2,1,0:T(8,128)} %broadcast_in_dim.9), calls=%async_computation.1 | async-start | bytes 1310720 | tf_op jit(solution)/shard_map/all_to_all | solution.py:260
  135.2 3.3 %collective-permute-start.13 = (f32[8,256]{1,0:T(8,128)S(1)}, f32[8,256]{1,0:T(8,128)S(1)}, u32[]{:S(2)}, u32[]{:S(2)}) collective-permute-start(f32[8,256]{1,0:T(8,128)S(1)} %slice.114), channel_id=1, source_target_pairs={{0,64},{32,96},{64,192},{96,224},{128,0},{160,32},{192,128},{224,1... | collective-permute-start | bytes 24584 | tf_op jit(solution)/shard_map/ppermute | solution.py:252
  138.6 2.6 %collective-permute-start.14 = (f32[8,128]{1,0:T(8,128)S(1)}, f32[8,128]{1,0:T(8,128)S(1)}, u32[]{:S(2)}, u32[]{:S(2)}) collective-permute-start(f32[8,128]{1,0:T(8,128)S(1)} %slice.115), channel_id=1, source_target_pairs={{0,192},{32,224},{64,128},{96,160},{128,64},{160,96},{192,0},{224,... | collective-permute-start | bytes 12296 | tf_op jit(solution)/shard_map/ppermute | solution.py:252
  141.2 3.8 %collective-permute-done.14 = f32[8,128]{1,0:T(8,128)S(1)} collective-permute-done((f32[8,128]{1,0:T(8,128)S(1)}, f32[8,128]{1,0:T(8,128)S(1)}, u32[]{:S(2)}, u32[]{:S(2)}) %collective-permute-start.14) | collective-permute-done | bytes 4128 | tf_op jit(solution)/shard_map/ppermute | solution.py:252
  144.9 7.5 %all-to-all-done.1.own1 = f32[16,8,1280]{2,1,0:T(8,128)S(1)} async-done(((f32[16,8,1280]{2,1,0:T(8,128)}), f32[16,8,1280]{2,1,0:T(8,128)S(1)}, u32[]{:S(2)}, u32[]{:S(2)}) %all-to-all-start.1) | async-done | bytes 655392 | tf_op jit(solution)/shard_map/all_to_all | solution.py:260
  153.3 4.4 %all-to-all-start.3 = ((f32[16,8,768]{2,1,0:T(8,128)}), f32[16,8,768]{2,1,0:T(8,128)S(1)}, u32[]{:S(2)}, u32[]{:S(2)}) async-start(f32[16,8,768]{2,1,0:T(8,128)} %broadcast_in_dim.11), calls=%async_computation.3 | async-start | bytes 786432 | tf_op jit(solution)/shard_map/all_to_all | solution.py:260
  157.7 2.7 %collective-permute-start.8 = (f32[16,8,1280]{2,1,0:T(8,128)S(1)}, f32[16,8,1280]{2,1,0:T(8,128)S(1)}, u32[]{:S(2)}, u32[]{:S(2)}) collective-permute-start(f32[16,8,1280]{2,1,0:T(8,128)S(1)} %all-to-all-done.1.own1), channel_id=1, source_target_pairs={{0,1},{1,0},{2,3},{3,2},{4,5},{5,4},{6,7},{7,6},{8,9},{9,8},{10,11... | collective-permute-start | bytes 1966088 | tf_op jit(solution)/shard_map/ppermute | solution.py:255
  160.4 8.5 %all-to-all-done.3.own2 = f32[16,8,768]{2,1,0:T(8,128)S(1)} async-done(((f32[16,8,768]{2,1,0:T(8,128)}), f32[16,8,768]{2,1,0:T(8,128)S(1)}, u32[]{:S(2)}, u32[]{:S(2)}) %all-to-all-start.3) | async-done | bytes 393248 | tf_op jit(solution)/shard_map/all_to_all | solution.py:260
  168.9 4.4 %collective-permute-start.15 = (f32[16,8,768]{2,1,0:T(8,128)S(1)}, f32[16,8,768]{2,1,0:T(8,128)S(1)}, u32[]{:S(2)}, u32[]{:S(2)}) collective-permute-start(f32[16,8,768]{2,1,0:T(8,128)S(1)} %all-to-all-done.3.own2), channel_id=1, source_target_pairs={{0,1},{1,0},{2,3},{3,2},{4,5},{5,4},{6,7},{7,6},{8,9},{9,8},{10,11... | collective-permute-start | bytes 1179656 | tf_op jit(solution)/shard_map/ppermute | solution.py:255
  173.4 1.3 collective-permute-done.15.other2
  176.3 3.4 %assemble.1 = f32[256,2048]{1,0:T(8,128)} custom-call(s32[10]{0:T(128)} %pad_add_fusion.at_ref, f32[16,8,1280]{2,1,0:T(8,128)} %copy-done, f32[16,8,1280]{2,1,0:T(8,128)} %copy-done.2, f32[16,8,768]{2,1,0:T(8,128)} %copy-done.1, f32[16,8,768]{2,1,0:T(8,128)} %copy-done.3), custom_call_target="tpu_custom_call" | custom-call | tf_op jit(solution)/shard_map/assemble/pallas_call | solution.py:228
  (76 shorter events, 20.1 us)
Async XLA Ops:
  3.4 70.2 %collective-permute-start.10 = (f32[512,256]{1,0:T(8,128)}, f32[512,256]{1,0:T(8,128)S(1)}, u32[]{:S(2)}, u32[]{:S(2)}) collective-permute-start(f32[512,256]{1,0:T(8,128)} %get-tuple-element.16.refs_0_), channel_id=1, source_target_pairs={{192,0},{224,32},{128,64},{160,96},{64,128},{96,160},{0,192},{32,2... | collective-permute-start | bytes 1572872 | tf_op jit(solution)/shard_map/ppermute | solution.py:249
  9.6 64.1 %collective-permute-start.9 = (f32[512,256]{1,0:T(8,128)}, f32[512,256]{1,0:T(8,128)S(1)}, u32[]{:S(2)}, u32[]{:S(2)}) collective-permute-start(f32[512,256]{1,0:T(8,128)} %get-tuple-element.16.refs_0_), channel_id=1, source_target_pairs={{64,0},{96,32},{192,64},{224,96},{0,128},{32,160},{128,192},{160,2... | collective-permute-start | bytes 1572872 | tf_op jit(solution)/shard_map/ppermute | solution.py:249
  9.6 24.0 %collective-permute-start.2 = (f32[512,256]{1,0:T(8,128)}, f32[512,256]{1,0:T(8,128)S(1)}, u32[]{:S(2)}, u32[]{:S(2)}) collective-permute-start(f32[512,256]{1,0:T(8,128)} %get-tuple-element.16.refs_0_), channel_id=1, source_target_pairs={{224,0},{128,32},{160,64},{192,96},{96,128},{0,160},{32,192},{64,2... | collective-permute-start | bytes 1572872 | tf_op jit(solution)/shard_map/ppermute | solution.py:249
  10.8 22.8 %collective-permute-start.1 = (f32[512,256]{1,0:T(8,128)}, f32[512,256]{1,0:T(8,128)S(1)}, u32[]{:S(2)}, u32[]{:S(2)}) collective-permute-start(f32[512,256]{1,0:T(8,128)} %get-tuple-element.16.refs_0_), channel_id=1, source_target_pairs={{32,0},{64,32},{96,64},{0,96},{160,128},{192,160},{224,192},{128,2... | collective-permute-start | bytes 1572872 | tf_op jit(solution)/shard_map/ppermute | solution.py:249
  28.0 4.5 %collective-permute-start.4 = (f32[8,128]{1,0:T(8,128)}, f32[8,128]{1,0:T(8,128)S(1)}, u32[]{:S(2)}, u32[]{:S(2)}) collective-permute-start(f32[8,128]{1,0:T(8,128)} %get-tuple-element.19), channel_id=1, source_target_pairs={{0,1},{1,0},{2,3},{3,2},{4,5},{5,4},{6,7},{7,6},{8,9},{9,8},{10,11... | collective-permute-start | bytes 12296 | tf_op jit(solution)/shard_map/ppermute | solution.py:255
  32.6 28.5 %collective-permute-start = (f32[128,256]{1,0:T(8,128)S(1)}, f32[128,256]{1,0:T(8,128)S(1)}, u32[]{:S(2)}, u32[]{:S(2)}) collective-permute-start(f32[128,256]{1,0:T(8,128)S(1)} %slice_bitcast_fusion.2), channel_id=1, source_target_pairs={{0,1},{1,0},{2,3},{3,2},{4,5},{5,4},{6,7},{7,6},{8,9},{9,8},{10,11... | collective-permute-start | bytes 393224 | tf_op jit(solution)/shard_map/ppermute | solution.py:255
  33.6 27.5 %copy-start.4 = (f32[2,128,256]{2,1,0:T(8,128)S(1)}, f32[2,128,256]{2,1,0:T(8,128)}, u32[]{:S(2)}) copy-start(f32[2,128,256]{2,1,0:T(8,128)} %get-tuple-element.17) | copy-start | bytes 786436
  59.5 1.6 collective-permute-start.5
  60.8 1.6 collective-permute-start.3
  64.3 36.6 %all-to-all-start = ((f32[16,8,896]{2,1,0:T(8,128)}), f32[16,8,896]{2,1,0:T(8,128)S(1)}, u32[]{:S(2)}, u32[]{:S(2)}) async-start(f32[16,8,896]{2,1,0:T(8,128)} %pad_maximum_fusion), calls=%async_computation | async-start | bytes 917504 | tf_op jit(solution)/shard_map/all_to_all | solution.py:260
  96.7 2.6 %collective-permute-start.11 = (f32[128,384]{1,0:T(8,128)S(1)}, f32[128,384]{1,0:T(8,128)S(1)}, u32[]{:S(2)}, u32[]{:S(2)}) collective-permute-start(f32[128,384]{1,0:T(8,128)S(1)} %slice_bitcast_fusion.1), channel_id=1, source_target_pairs={{0,1},{1,0},{2,3},{3,2},{4,5},{5,4},{6,7},{7,6},{8,9},{9,8},{10,11... | collective-permute-start | bytes 589832 | tf_op jit(solution)/shard_map/ppermute | solution.py:255
  97.2 1.4 collective-permute-start.12
  100.9 25.7 %all-to-all-start.2 = ((f32[16,8,512]{2,1,0:T(8,128)}), f32[16,8,512]{2,1,0:T(8,128)S(1)}, u32[]{:S(2)}, u32[]{:S(2)}) async-start(f32[16,8,512]{2,1,0:T(8,128)} %pad_maximum_fusion.1), calls=%async_computation.2 | async-start | bytes 524288 | tf_op jit(solution)/shard_map/all_to_all | solution.py:260
  109.0 16.4 %collective-permute-start.6 = (f32[8,256]{1,0:T(8,128)S(1)}, f32[8,256]{1,0:T(8,128)S(1)}, u32[]{:S(2)}, u32[]{:S(2)}) collective-permute-start(f32[8,256]{1,0:T(8,128)S(1)} %get-tuple-element.25), channel_id=1, source_target_pairs={{0,32},{32,64},{64,96},{96,0},{128,160},{160,192},{192,224},{224,1... | collective-permute-start | bytes 24584 | tf_op jit(solution)/shard_map/ppermute | solution.py:252
  121.7 5.0 %collective-permute-start.7 = (f32[8,256]{1,0:T(8,128)S(1)}, f32[8,256]{1,0:T(8,128)S(1)}, u32[]{:S(2)}, u32[]{:S(2)}) collective-permute-start(f32[8,256]{1,0:T(8,128)S(1)} %get-tuple-element.26), channel_id=1, source_target_pairs={{0,224},{32,128},{64,160},{96,192},{128,96},{160,0},{192,32},{224,... | collective-permute-start | bytes 24584 | tf_op jit(solution)/shard_map/ppermute | solution.py:252
  127.5 24.9 %all-to-all-start.1 = ((f32[16,8,1280]{2,1,0:T(8,128)}), f32[16,8,1280]{2,1,0:T(8,128)S(1)}, u32[]{:S(2)}, u32[]{:S(2)}) async-start(f32[16,8,1280]{2,1,0:T(8,128)} %broadcast_in_dim.9), calls=%async_computation.1 | async-start | bytes 1310720 | tf_op jit(solution)/shard_map/all_to_all | solution.py:260
  135.2 9.7 %collective-permute-start.13 = (f32[8,256]{1,0:T(8,128)S(1)}, f32[8,256]{1,0:T(8,128)S(1)}, u32[]{:S(2)}, u32[]{:S(2)}) collective-permute-start(f32[8,256]{1,0:T(8,128)S(1)} %slice.114), channel_id=1, source_target_pairs={{0,64},{32,96},{64,192},{96,224},{128,0},{160,32},{192,128},{224,1... | collective-permute-start | bytes 24584 | tf_op jit(solution)/shard_map/ppermute | solution.py:252
  138.6 6.4 %collective-permute-start.14 = (f32[8,128]{1,0:T(8,128)S(1)}, f32[8,128]{1,0:T(8,128)S(1)}, u32[]{:S(2)}, u32[]{:S(2)}) collective-permute-start(f32[8,128]{1,0:T(8,128)S(1)} %slice.115), channel_id=1, source_target_pairs={{0,192},{32,224},{64,128},{96,160},{128,64},{160,96},{192,0},{224,... | collective-permute-start | bytes 12296 | tf_op jit(solution)/shard_map/ppermute | solution.py:252
  152.4 22.3 %copy-start = (f32[16,8,1280]{2,1,0:T(8,128)}, f32[16,8,1280]{2,1,0:T(8,128)S(1)}, u32[]{:S(2)}) copy-start(f32[16,8,1280]{2,1,0:T(8,128)S(1)} %all-to-all-done.1.own1) | copy-start | bytes 1966084
  153.3 15.7 %all-to-all-start.3 = ((f32[16,8,768]{2,1,0:T(8,128)}), f32[16,8,768]{2,1,0:T(8,128)S(1)}, u32[]{:S(2)}, u32[]{:S(2)}) async-start(f32[16,8,768]{2,1,0:T(8,128)} %broadcast_in_dim.11), calls=%async_computation.3 | async-start | bytes 786432 | tf_op jit(solution)/shard_map/all_to_all | solution.py:260
  157.7 17.0 %collective-permute-start.8 = (f32[16,8,1280]{2,1,0:T(8,128)S(1)}, f32[16,8,1280]{2,1,0:T(8,128)S(1)}, u32[]{:S(2)}, u32[]{:S(2)}) collective-permute-start(f32[16,8,1280]{2,1,0:T(8,128)S(1)} %all-to-all-done.1.own1), channel_id=1, source_target_pairs={{0,1},{1,0},{2,3},{3,2},{4,5},{5,4},{6,7},{7,6},{8,9},{9,8},{10,11... | collective-permute-start | bytes 1966088 | tf_op jit(solution)/shard_map/ppermute | solution.py:255
  168.9 5.8 %copy-start.1 = (f32[16,8,768]{2,1,0:T(8,128)}, f32[16,8,768]{2,1,0:T(8,128)S(1)}, u32[]{:S(2)}) copy-start(f32[16,8,768]{2,1,0:T(8,128)S(1)} %all-to-all-done.3.own2) | copy-start | bytes 1179652
  168.9 5.8 %collective-permute-start.15 = (f32[16,8,768]{2,1,0:T(8,128)S(1)}, f32[16,8,768]{2,1,0:T(8,128)S(1)}, u32[]{:S(2)}, u32[]{:S(2)}) collective-permute-start(f32[16,8,768]{2,1,0:T(8,128)S(1)} %all-to-all-done.3.own2), channel_id=1, source_target_pairs={{0,1},{1,0},{2,3},{3,2},{4,5},{5,4},{6,7},{7,6},{8,9},{9,8},{10,11... | collective-permute-start | bytes 1179656 | tf_op jit(solution)/shard_map/ppermute | solution.py:255
  175.5 0.9 copy-start.2
  (5 other events, 3.9 us)
where the time goes:
time: 181 us; the launch traced here: 180 us
  starting transfers between devices  72.6 us (40%)
  Pallas kernels  66 us (36%)
  waiting for transfers between devices  24.3 us (13%)
  local copies, waits for them, and re-layouts  10.1 us (6%)
  other arithmetic  6.5 us (4%)
    pallas_call x3, Pallas kernels, call(): pl.pallas_call(kernel, out_shape=(jax.ShapeDtypeStruct((2, 128, width), F...  59.2 us
    all_to_all x4, starting transfers between devices, over_chips(): return lax.all_to_all(v, 'branch', 0, 0, axis_index_groups=chips)  29.1 us
    ppermute x4, starting transfers between devices, to_partner(): return lax.ppermute(v, 'blk', [(b, PARTNERS[n][b]) for b in range(BLOCKS)])  22.3 us
    all_to_all x4, waiting for transfers between devices, over_chips(): return lax.all_to_all(v, 'branch', 0, 0, axis_index_groups=chips)  16 us
    ppermute x8, starting transfers between devices, other_core(): return lax.ppermute(v, 'branch', [(i, i ^ 1) for i in range(32)])  12.2 us
    ppermute x4, starting transfers between devices, from_partner(): return lax.ppermute(v, 'blk', [(PARTNERS[n][b], b) for b in range(BLOCKS)])  8.91 us
    ppermute x4, waiting for transfers between devices, to_partner(): return lax.ppermute(v, 'blk', [(b, PARTNERS[n][b]) for b in range(BLOCKS)])  4.95 us
    unnamed x18, local copies, waits for them, and re-layouts  4.75 us
  transfers between devices with their start and end apart: 20, of which 8 were waited for; matrix products, arithmetic and copies ran while one was open for 6% of the time, Pallas kernels for 33%

commit v1 on v0

v1 whole, which is shorter than its diff:
```python
import jax
import jax.numpy as jnp
from jax import lax
from jax.experimental import pallas as pl
from jax.experimental.pallas import tpu as pltpu
from jax.sharding import PartitionSpec as P

F32 = jnp.float32
BF16 = jnp.bfloat16
ROWS = 256
KS = 512
BLOCKS = 8
GROUP = 8
PAIRS = GROUP // 2
GROUPS = ROWS // GROUP


def block_at(y, x):
    return (y % 2) * 4 + x % 4


def partner_tables():
    first, second, third, fourth = [], [], [], []
    for b in range(BLOCKS):
        y, x = b // 4, b % 4
        first.append(block_at(y, x + 1))
        second.append(block_at(y + 1, x + 3))
        cycle = {(0, 0): (0, 2), (0, 1): (1, 2), (1, 1): (1, 0), (1, 0): (0, 0)}
        ny, nx = cycle[(y, x // 2)]
        third.append(block_at(ny, nx + x % 2))
        fourth.append(block_at(y + 1, x + 2))
    return [first, second, third, fourth]


PARTNERS = partner_tables()
OWNERS = [[table.index(b) for b in range(BLOCKS)] for table in PARTNERS]


def params():
    return pltpu.CompilerParams(vmem_limit_bytes=56 << 20)


def in_vmem(n):
    return [pl.BlockSpec(memory_space=pltpu.VMEM)] * n


def branch_sums(ref, lane):
    def add(k8, total):
        at = pl.ds(pl.multiple_of(k8 * 8, 8), 8)
        return total + ref[at, lane : lane + 128]

    total = lax.fori_loop(0, KS // 8, add, jnp.zeros((8, 128), F32), unroll=8)
    return jnp.sum(total, axis=0, keepdims=True)


def weigh_kernel(counts_ref, totals_ref, lengths_ref, wt_ref, split_ref, row_ref, col_ref):
    scaled = lengths_ref[...].astype(F32) * 0.001
    wt = (scaled * counts_ref[...].astype(F32)).T / totals_ref[...].astype(F32)
    wt_ref[...] = wt
    for n in range(8):
        x = wt[:, n * 32 : (n + 1) * 32]
        high = x.astype(BF16)
        rest = x - high.astype(F32)
        middle = rest.astype(BF16)
        low = (rest - middle.astype(F32)).astype(BF16)
        split_ref[n] = jnp.concatenate([high, middle, low, jnp.zeros_like(low)], axis=1)
    for h in range(2):
        sums = branch_sums(wt_ref, h * 128)
        row_ref[:, h * 128 : (h + 1) * 128] = jnp.broadcast_to(sums, (8, 128))
        col_ref[h * 128 : (h + 1) * 128, :] = jnp.broadcast_to(sums, (128, 128)).T


def weigh(counts, totals, lengths):
    return pl.pallas_call(
        weigh_kernel,
        out_shape=(
            jax.ShapeDtypeStruct((KS, ROWS), F32),
            jax.ShapeDtypeStruct((8, KS, 128), BF16),
            jax.ShapeDtypeStruct((8, ROWS), F32),
            jax.ShapeDtypeStruct((ROWS, 128), F32),
        ),
        compiler_params=params(),
        name="weigh",
    )(counts, totals.reshape(1, ROWS), lengths.reshape(1, KS))


def spread_call(name, n_blocks, columns, sides, width, group=8, mass_row=0):
    pairs = group // 2
    groups = ROWS // 2 // group

    def kernel(split_ref, col_ref, *refs):
        blocks = refs[:n_blocks]
        outs = refs[n_blocks : n_blocks + len(sides)]
        pick_ref, even_ref, odd_ref = refs[n_blocks + len(sides) :]
        core = lax.axis_index("branch") % 2
        y = lax.axis_index("blk") // 4

        part = lax.broadcasted_iota(jnp.int32, (128, 256), 0)
        lane = lax.broadcasted_iota(jnp.int32, (128, 256), 1)
        want = jnp.where(part < 96, part % 32 - lane // 128, -1)
        for p in range(16):
            pick_ref[p] = jnp.where(want == 2 * p, 1.0, 0.0).astype(BF16)

        def span(n, lane, at):
            if isinstance(lane, int):
                return blocks[n][at, lane : lane + 128]
            return blocks[n][at, pl.ds(pl.multiple_of(lane, 128), 128)]

        def broadcast_pair(into, g, q, at=slice(0, KS)):
            pair = g * pairs + q
            into[q, at] = jnp.dot(
                split_ref[pair // 16, at], pick_ref[pair % 16], preferred_element_type=F32
            )

        def one_group(g, base, out_ref, cols, sums, now, later):
            n_cols = len(cols)
            following = jnp.minimum(base + g + 1, ROWS // group - 1)
            steps = []
            if group == 8:
                for q in range(pairs):
                    broadcast_pair(later, following, q)
            else:
                steps = [(q, slice(k, k + 128)) for k in range(0, KS, 128) for q in range(pairs)]
            acc = [jnp.zeros((8, 128), F32)] * (group * n_cols)
            for k8 in range(KS // 8):
                if steps and k8 % 2 == 0:
                    q, at = steps[k8 // 2]
                    broadcast_pair(later, following, q, at)
                at = slice(k8 * 8, k8 * 8 + 8)
                spans = [span(n, lane, at) for n, lane in cols]
                for r in range(group):
                    own = now[r // 2, at, 128 * (r % 2) : 128 * (r % 2) + 128]
                    for j in range(n_cols):
                        acc[r * n_cols + j] += jnp.minimum(own, spans[j])
            for r0 in range(0, group, 8):
                row = pl.multiple_of(g * group + r0, 8)
                own_mass = col_ref[pl.ds(pl.multiple_of(base * group + row, 8), 8), :]
                for j in range(n_cols):
                    least = jnp.concatenate(
                        [
                            jnp.sum(acc[(r0 + r) * n_cols + j], axis=0, keepdims=True)
                            for r in range(8)
                        ],
                        axis=0,
                    )
                    out_ref[pl.ds(row, 8), 128 * j : 128 * j + 128] = (
                        own_mass + sums[j] - 2.0 * least
                    )

        def one_side(out_ref, half, cols):
            base = half * groups
            sums = []
            for n, lane in cols:
                total = jnp.zeros((8, 128), F32)
                for k8 in range(KS // 8):
                    total = total + span(n, lane, slice(k8 * 8, k8 * 8 + 8))
                sums.append(jnp.sum(total, axis=0, keepdims=True))
            zeros = jnp.zeros((1, 128), F32)
            below = [zeros] * mass_row + sums
            below = below + [zeros] * (8 - len(below))
            out_ref[128:136, 0:128] = jnp.concatenate(below, axis=0)
            for q in range(pairs):
                broadcast_pair(even_ref, base, q)

            def two_groups(t, carry):
                one_group(2 * t, base, out_ref, cols, sums, even_ref, odd_ref)
                one_group(2 * t + 1, base, out_ref, cols, sums, odd_ref, even_ref)
                return carry

            lax.fori_loop(0, groups // 2, two_groups, 0)

        for side, out_ref in zip(sides, outs, strict=True):
            half = core if side == 0 else 1 - core
            if isinstance(columns, tuple):
                for value, cols in enumerate(columns):
                    pl.when(half == value)(
                        lambda out_ref=out_ref, half=half, cols=cols: one_side(out_ref, half, cols)
                    )
            else:
                one_side(out_ref, half, columns(half, y))

    steps = width * 128 * KS * len(sides)

    def call(split, col, *blocks):
        return pl.pallas_call(
            kernel,
            out_shape=tuple(jax.ShapeDtypeStruct((136, width), F32) for _ in sides),
            in_specs=in_vmem(2 + n_blocks),
            out_specs=tuple(in_vmem(len(sides))),
            scratch_shapes=[
                pltpu.VMEM((16, 128, 256), BF16),
                pltpu.VMEM((pairs, KS, 256), F32),
                pltpu.VMEM((pairs, KS, 256), F32),
            ],
            compiler_params=params(),
            cost_estimate=pl.CostEstimate(
                flops=steps * 250, bytes_accessed=4 << 20, transcendentals=0
            ),
            name=name,
        )(split, col, *blocks)

    return call


DIAGONAL = ([(0, 128), (0, 0)], [(0, 128)])


def first_columns(half, y):
    return [(0, 0), (0, 128), (1, 0), (1, 128)]


def second_columns(half, y):
    return [(0, 0), (0, 128), (1, (half ^ y) * 128)]


def block_partner(b, slot):
    y, x = b // 4, b % 4
    if slot == 0:
        return b
    if slot == 1:
        return y * 4 + (x + 1) % 4
    if slot == 2:
        return (1 - y) * 4 + (x + 3) % 4
    if slot == 4:
        return (1 - y) * 4 + (x + 2) % 4
    if slot == 5:
        return y * 4 + (x + 3) % 4
    if slot == 6:
        return (1 - y) * 4 + (x + 1) % 4
    far = x // 2
    keep_y = (far == y) if slot == 3 else (far != y)
    return jnp.where(keep_y, y * 4 + (x + 2) % 4, (1 - y) * 4 + x)


def assemble_kernel(own1, other1, own2, other2, out_ref, all_ref):
    core = lax.axis_index("branch") % 2
    b = lax.axis_index("blk")
    y = b // 4
    n1 = own1.shape[2]
    for c, ref1, ref2 in ((core, own1, own2), (1 - core, other1, other2)):
        to = pl.ds(pl.multiple_of(c * 128, 128), 128)
        all_ref[to, 0:n1] = ref1[...].reshape(128, n1)
        all_ref[to, n1:] = ref2[...].reshape(128, all_ref.shape[1] - n1)

    def columns(slot, half=None):
        first = block_partner(b, slot) * ROWS
        if half is None:
            return pl.ds(pl.multiple_of(first, ROWS), ROWS)
        return pl.ds(pl.multiple_of(first + half * 128, 128), 128)

    upper = all_ref[0:128, 0:128]
    out_ref[0:128, columns(0, 0)] = all_ref[0:128, 128:256]
    out_ref[0:128, columns(0, 1)] = upper
    out_ref[128:256, columns(0, 0)] = upper.T
    out_ref[128:256, columns(0, 1)] = all_ref[128:256, 0:128]
    for slot, lane in ((1, 256), (2, 512), (3, n1)):
        out_ref[:, columns(slot)] = all_ref[:, lane : lane + ROWS]
    for slot, lane in ((5, 768), (6, 1024), (7, n1 + 384)):
        out_ref[:, columns(slot)] = all_ref[:, lane : lane + ROWS].T
    for half in range(2):
        rows = slice(half * 128, half * 128 + 128)
        out_ref[rows, columns(4, half ^ y)] = all_ref[rows, n1 + 256 : n1 + 384]
        to = pl.ds(pl.multiple_of((half ^ (1 - y)) * 128, 128), 128)
        out_ref[to, columns(4, half)] = all_ref[rows, n1 + 640 : n1 + 768].T


def assemble(own1, other1, own2, other2):
    return pl.pallas_call(
        assemble_kernel,
        out_shape=jax.ShapeDtypeStruct((ROWS, BLOCKS * ROWS), F32),
        in_specs=in_vmem(4),
        out_specs=in_vmem(1)[0],
        scratch_shapes=[pltpu.VMEM((ROWS, own1.shape[2] + own2.shape[2]), F32)],
        compiler_params=params(),
        name="assemble",
    )(own1, other1, own2, other2)


def on_device(counts, totals, lengths):
    branch = lax.axis_index("branch")
    place = branch // 2

    def from_partner(v, n):
        return lax.ppermute(v, "blk", [(PARTNERS[n][b], b) for b in range(BLOCKS)])

    def to_partner(v, n):
        return lax.ppermute(v, "blk", [(b, PARTNERS[n][b]) for b in range(BLOCKS)])

    def other_core(v):
        return lax.ppermute(v, "branch", [(i, i ^ 1) for i in range(32)])

    chips = [[2 * p + c for p in range(16)] for c in range(2)]

    def over_chips(v):
        return lax.all_to_all(v, "branch", 0, 0, axis_index_groups=chips)

    def scatter(kept, received):
        tiles = jnp.concatenate(
            [(k[:128] + r[:128]).reshape(16, 8, -1) for k, r in zip(kept, received, strict=True)],
            axis=2,
        )
        masses = sum(k[128:, :128] + r[128:, :128] for k, r in zip(kept, received, strict=True))
        masses = jnp.broadcast_to(masses[None], (16, 8, 128))
        shard = jnp.sum(over_chips(jnp.concatenate([tiles, masses], axis=2)), axis=0)
        return shard[:, :-128], shard[:, -128:]

    def gather(pieces):
        mine = jnp.concatenate(pieces, axis=1)
        whole = over_chips(jnp.broadcast_to(mine[None], (16, *mine.shape)))
        return whole, other_core(whole)

    wt, split, mass_row, mass_col = weigh(counts, totals, lengths)
    got = [from_partner(wt, n) for n in range(2)]
    diagonal = spread_call("diagonal", 1, DIAGONAL, (1, 0), 256, group=16, mass_row=4)
    first = spread_call("first", 2, first_columns, (1, 0), 512)
    second = [spread_call(f"second{s}", 2, second_columns, (s,), 384) for s in range(2)]

    send0, keep0 = diagonal(split, mass_col, wt)
    later, keep0 = lax.optimization_barrier((wt, keep0))
    got += [from_partner(later, n) for n in (2, 3)]
    send1, keep1 = first(split, mass_col, got[0], got[1])
    shard, sums = scatter([keep0, keep1], [other_core(send0), other_core(send1)])
    (send2,) = second[1](split, mass_col, got[2], got[3])
    (keep2,) = second[0](split, mass_col, got[2], got[3])

    own_lower = sums[5]
    own_half = jnp.where(branch % 2 == 0, own_lower, sums[4])
    own_mass = lax.dynamic_slice_in_dim(own_half, place * 8, 8)[:, None]
    parts = jnp.concatenate([sums[4:5], sums[5:6], sums[0:4]]).reshape(768)
    dist1 = shard / (own_mass + parts[None, :])
    swapped1 = [to_partner(dist1[:, 256 * (n + 1) : 256 * (n + 2)], n) for n in range(2)]
    own1, other1 = gather([dist1, *swapped1])

    shard, sums = scatter([keep2], [other_core(send2)])
    dist2 = shard / (own_mass + sums[0:3].reshape(384)[None, :])
    swapped2 = [to_partner(dist2[:, 0:256], 2), to_partner(dist2[:, 256:384], 3)]
    own2, other2 = gather([dist2, *swapped2])

    return assemble(own1, other1, own2, other2)


def solution(mesh):
    placed = (P("blk", "branch"), P("blk"), P("branch"))
    return jax.shard_map(
        on_device, mesh=mesh, in_specs=placed, out_specs=P("blk", None), check_vma=False
    )
```

time: 181 us -> 164 us (0.906)
  starting transfers between devices: 72.6 us -> 48.7 us
  waiting for transfers between devices: 24.3 us -> 34.1 us
  local copies, waits for them, and re-layouts: 10.1 us -> 6.66 us
  Pallas kernels: 66 us -> 69 us
    ppermute x4, starting transfers between devices: 22.3 us -> 7 us  [to_partner(): return lax.ppermute(v, 'blk', [(b, PARTNERS[n][b]) for b in range(BLOCKS)])]
    all_to_all x4, waiting for transfers between devices: 16 us -> 26.9 us  [over_chips(): return lax.all_to_all(v, 'branch', 0, 0, axis_index_groups=chips)]
    all_to_all x4, starting transfers between devices: 29.1 us -> 23.1 us  [over_chips(): return lax.all_to_all(v, 'branch', 0, 0, axis_index_groups=chips)]
    ppermute x8 -> x5, starting transfers between devices: 12.2 us -> 8.22 us  [other_core(): return lax.ppermute(v, 'branch', [(i, i ^ 1) for i in range(32)])]
    squeeze x5 -> x0, local copies, waits for them, and re-layouts: 3.52 us -> none  [the longest x3 2.82 us: on_chip(): return (out[0] + other_core(out[1]), mass + other_core(mass))]
    pallas_call x3 -> x4, Pallas kernels: 59.2 us -> 62.1 us  [call(): pl.pallas_call(kernel, out_shape=tuple((jax.ShapeDtypeStruct((136, width)...]
    ppermute x8 -> x5, waiting for transfers between devices: 3.35 us -> 1.36 us  [other_core(): return lax.ppermute(v, 'branch', [(i, i ^ 1) for i in range(32)])]
    unnamed x18 -> x20, local copies, waits for them, and re-layouts: 4.75 us -> 4.83 us
  transfers between devices with their start and end apart: 20 -> 17, of which waited for: 8 -> 7; matrix products, arithmetic and copies ran while one was open for 6% -> 3% of each run, Pallas kernels for 33% -> 38%
where the time goes in v1:
time: 164 us
  Pallas kernels  69 us (42%)
  starting transfers between devices  48.7 us (30%)
  waiting for transfers between devices  34.1 us (21%)
  local copies, waits for them, and re-layouts  6.66 us (4%)
  other arithmetic  5.04 us (3%)
    pallas_call x4, Pallas kernels, call(): pl.pallas_call(kernel, out_shape=tuple((jax.ShapeDtypeStruct((136, width)...  62.1 us
    all_to_all x4, waiting for transfers between devices, over_chips(): return lax.all_to_all(v, 'branch', 0, 0, axis_index_groups=chips)  26.9 us
    all_to_all x4, starting transfers between devices, over_chips(): return lax.all_to_all(v, 'branch', 0, 0, axis_index_groups=chips)  23.1 us
    ppermute x4, starting transfers between devices, from_partner(): return lax.ppermute(v, 'blk', [(PARTNERS[n][b], b) for b in range(BLOCKS)])  10.4 us
    ppermute x5, starting transfers between devices, other_core(): return lax.ppermute(v, 'branch', [(i, i ^ 1) for i in range(32)])  8.22 us
    ppermute x4, starting transfers between devices, to_partner(): return lax.ppermute(v, 'blk', [(b, PARTNERS[n][b]) for b in range(BLOCKS)])  7 us
    ppermute x4, waiting for transfers between devices, to_partner(): return lax.ppermute(v, 'blk', [(b, PARTNERS[n][b]) for b in range(BLOCKS)])  5.84 us
    unnamed x20, local copies, waits for them, and re-layouts  4.83 us
  transfers between devices with their start and end apart: 17, of which 7 were waited for; matrix products, arithmetic and copies ran while one was open for 3% of the time, Pallas kernels for 38%

profile of v1, /device:TPU:1, one launch (start us, length us, event | category | flops | bytes accessed | tf_op | source)
XLA Modules:
  0.0 163.7 jit_solution(17789333580869555664)
XLA Ops:
  0.0 3.4 %weigh.1 = (f32[512,256]{1,0:T(8,128)}, bf16[8,512,128]{2,1,0:T(8,128)(2,1)}, f32[8,256]{1,0:T(8,128)}, f32[256,128]{1,0:T(8,128)}) custom-call(s32[256,512]{1,0:T(8,128)} %counts_ref.1, s32[1,256]{1,0:T(1,128)} %bitcast.15, s32[1,512]{1,0:T(1,128)} %bitcast.14), custom_call_target="tpu_custom_call" | custom-call | tf_op jit(solution)/shard_map/weigh/pallas_call | solution.py:74
  3.4 4.7 %collective-permute-start.2 = (f32[512,256]{1,0:T(8,128)}, f32[512,256]{1,0:T(8,128)S(1)}, u32[]{:S(2)}, u32[]{:S(2)}) collective-permute-start(f32[512,256]{1,0:T(8,128)} %get-tuple-element.22.refs_0_), channel_id=1, source_target_pairs={{224,0},{128,32},{160,64},{192,96},{96,128},{0,160},{32,192},{64,2... | collective-permute-start | bytes 1572872 | tf_op jit(solution)/shard_map/ppermute | solution.py:284
  8.1 1.5 collective-permute-start.1
  9.5 14.9 %diagonal.1 = (f32[136,256]{1,0:T(8,128)}, f32[136,256]{1,0:T(8,128)}) custom-call(bf16[8,512,128]{2,1,0:T(8,128)(2,1)} %get-tuple-element.15.split_ref, f32[256,128]{1,0:T(8,128)} %get-tuple-element.16.col_ref, f32[512,256]{1,0:T(8,128)} %get-tuple-element.22.refs_0_), custom_call_target="tpu_custom_call" | custom-call | flops 8388608000 | bytes 4194304 | tf_op jit(solution)/shard_map/diagonal/pallas_call | solution.py:185
  25.6 1.3 collective-permute-start.8
  27.0 2.9 %collective-permute-start.7 = (f32[512,256]{1,0:T(8,128)S(1)}, f32[512,256]{1,0:T(8,128)S(1)}, u32[]{:S(2)}, u32[]{:S(2)}) collective-permute-start(f32[512,256]{1,0:T(8,128)S(1)} %copy-done.7), channel_id=1, source_target_pairs={{64,0},{96,32},{192,64},{224,96},{0,128},{32,160},{128,192},{160,2... | collective-permute-start | bytes 1572872 | tf_op jit(solution)/shard_map/ppermute | solution.py:284
  32.4 24.3 %first.1 = (f32[136,512]{1,0:T(8,128)}, f32[136,512]{1,0:T(8,128)}) custom-call(bf16[8,512,128]{2,1,0:T(8,128)(2,1)} %get-tuple-element.15.split_ref, f32[256,128]{1,0:T(8,128)} %get-tuple-element.16.col_ref, f32[512,256]{1,0:T(8,128)} %copy-done.9, f32[512,256]{1,0:T(8,128)} %copy-done.8), custom_call_target="tpu_custom_call" | custom-call | flops 16777216000 | bytes 4194304 | tf_op jit(solution)/shard_map/first/pallas_call | solution.py:185
  59.0 11.2 %second1.1 = f32[136,384]{1,0:T(8,128)} custom-call(bf16[8,512,128]{2,1,0:T(8,128)(2,1)} %get-tuple-element.15.split_ref, f32[256,128]{1,0:T(8,128)} %get-tuple-element.16.col_ref, f32[512,256]{1,0:T(8,128)} %copy-done.6, f32[512,256]{1,0:T(8,128)} %copy-done.5), custom_call_target="tpu_custom_call" | custom-call | flops 6291456000 | bytes 4194304 | tf_op jit(solution)/shard_map/second1/pallas_call | solution.py:185
  72.3 8.4 %all-to-all-start = ((f32[16,8,896]{2,1,0:T(8,128)}), f32[16,8,896]{2,1,0:T(8,128)S(1)}, u32[]{:S(2)}, u32[]{:S(2)}) async-start(f32[16,8,896]{2,1,0:T(8,128)} %pad_maximum_fusion), calls=%async_computation | async-start | bytes 917504 | tf_op jit(solution)/shard_map/all_to_all | solution.py:295
  80.7 11.6 %second0.1 = f32[136,384]{1,0:T(8,128)} custom-call(bf16[8,512,128]{2,1,0:T(8,128)(2,1)} %get-tuple-element.15.split_ref, f32[256,128]{1,0:T(8,128)} %get-tuple-element.16.col_ref, f32[512,256]{1,0:T(8,128)} %copy-done.6, f32[512,256]{1,0:T(8,128)} %copy-done.5), custom_call_target="tpu_custom_call" | custom-call | flops 6291456000 | bytes 4194304 | tf_op jit(solution)/shard_map/second0/pallas_call | solution.py:185
  95.7 6.5 %all-to-all-start.2 = ((f32[16,8,512]{2,1,0:T(8,128)}), f32[16,8,512]{2,1,0:T(8,128)S(1)}, u32[]{:S(2)}, u32[]{:S(2)}) async-start(f32[16,8,512]{2,1,0:T(8,128)} %pad_maximum_fusion.1), calls=%async_computation.2 | async-start | bytes 524288 | tf_op jit(solution)/shard_map/all_to_all | solution.py:295
  102.9 3.7 %collective-permute-start.5 = (f32[8,256]{1,0:T(8,128)S(1)}, f32[8,256]{1,0:T(8,128)S(1)}, u32[]{:S(2)}, u32[]{:S(2)}) collective-permute-start(f32[8,256]{1,0:T(8,128)S(1)} %get-tuple-element.24), channel_id=1, source_target_pairs={{0,224},{32,128},{64,160},{96,192},{128,96},{160,0},{192,32},{224,... | collective-permute-start | bytes 24584 | tf_op jit(solution)/shard_map/ppermute | solution.py:287
  106.6 1.4 collective-permute-done.5
  108.0 5.5 %all-to-all-done.2 = f32[16,8,512]{2,1,0:T(8,128)S(1)} async-done(((f32[16,8,512]{2,1,0:T(8,128)}), f32[16,8,512]{2,1,0:T(8,128)S(1)}, u32[]{:S(2)}, u32[]{:S(2)}) %all-to-all-start.2) | async-done | bytes 262176 | tf_op jit(solution)/shard_map/all_to_all | solution.py:295
  114.4 3.6 %all-to-all-start.1 = ((f32[16,8,1280]{2,1,0:T(8,128)}), f32[16,8,1280]{2,1,0:T(8,128)S(1)}, u32[]{:S(2)}, u32[]{:S(2)}) async-start(f32[16,8,1280]{2,1,0:T(8,128)} %broadcast_in_dim.9), calls=%async_computation.1 | async-start | bytes 1310720 | tf_op jit(solution)/shard_map/all_to_all | solution.py:295
  119.1 1.9 %collective-permute-start.11 = (f32[8,128]{1,0:T(8,128)S(1)}, f32[8,128]{1,0:T(8,128)S(1)}, u32[]{:S(2)}, u32[]{:S(2)}) collective-permute-start(f32[8,128]{1,0:T(8,128)S(1)} %slice.118), channel_id=1, source_target_pairs={{0,192},{32,224},{64,128},{96,160},{128,64},{160,96},{192,0},{224,... | collective-permute-start | bytes 12296 | tf_op jit(solution)/shard_map/ppermute | solution.py:287
  121.1 4.4 %collective-permute-done.11 = f32[8,128]{1,0:T(8,128)S(1)} collective-permute-done((f32[8,128]{1,0:T(8,128)S(1)}, f32[8,128]{1,0:T(8,128)S(1)}, u32[]{:S(2)}, u32[]{:S(2)}) %collective-permute-start.11) | collective-permute-done | bytes 4128 | tf_op jit(solution)/shard_map/ppermute | solution.py:287
  125.5 10.6 %all-to-all-done.1.own1 = f32[16,8,1280]{2,1,0:T(8,128)S(1)} async-done(((f32[16,8,1280]{2,1,0:T(8,128)}), f32[16,8,1280]{2,1,0:T(8,128)S(1)}, u32[]{:S(2)}, u32[]{:S(2)}) %all-to-all-start.1) | async-done | bytes 655392 | tf_op jit(solution)/shard_map/all_to_all | solution.py:295
  136.9 4.6 %all-to-all-start.3 = ((f32[16,8,768]{2,1,0:T(8,128)}), f32[16,8,768]{2,1,0:T(8,128)S(1)}, u32[]{:S(2)}, u32[]{:S(2)}) async-start(f32[16,8,768]{2,1,0:T(8,128)} %broadcast_in_dim.11), calls=%async_computation.3 | async-start | bytes 786432 | tf_op jit(solution)/shard_map/all_to_all | solution.py:295
  141.5 2.2 %collective-permute-start.6 = (f32[16,8,1280]{2,1,0:T(8,128)S(1)}, f32[16,8,1280]{2,1,0:T(8,128)S(1)}, u32[]{:S(2)}, u32[]{:S(2)}) collective-permute-start(f32[16,8,1280]{2,1,0:T(8,128)S(1)} %all-to-all-done.1.own1), channel_id=1, source_target_pairs={{0,1},{1,0},{2,3},{3,2},{4,5},{5,4},{6,7},{7,6},{8,9},{9,8},{10,11... | collective-permute-start | bytes 1966088 | tf_op jit(solution)/shard_map/ppermute | solution.py:290
  143.8 9.7 %all-to-all-done.3.own2 = f32[16,8,768]{2,1,0:T(8,128)S(1)} async-done(((f32[16,8,768]{2,1,0:T(8,128)}), f32[16,8,768]{2,1,0:T(8,128)S(1)}, u32[]{:S(2)}, u32[]{:S(2)}) %all-to-all-start.3) | async-done | bytes 393248 | tf_op jit(solution)/shard_map/all_to_all | solution.py:295
  153.5 3.7 %collective-permute-start.12 = (f32[16,8,768]{2,1,0:T(8,128)S(1)}, f32[16,8,768]{2,1,0:T(8,128)S(1)}, u32[]{:S(2)}, u32[]{:S(2)}) collective-permute-start(f32[16,8,768]{2,1,0:T(8,128)S(1)} %all-to-all-done.3.own2), channel_id=1, source_target_pairs={{0,1},{1,0},{2,3},{3,2},{4,5},{5,4},{6,7},{7,6},{8,9},{9,8},{10,11... | collective-permute-start | bytes 1179656 | tf_op jit(solution)/shard_map/ppermute | solution.py:290
  157.2 1.3 collective-permute-done.12.other2
  160.1 3.5 %assemble.1 = f32[256,2048]{1,0:T(8,128)} custom-call(f32[16,8,1280]{2,1,0:T(8,128)} %copy-done, f32[16,8,1280]{2,1,0:T(8,128)} %copy-done.2, f32[16,8,768]{2,1,0:T(8,128)} %copy-done.1, f32[16,8,768]{2,1,0:T(8,128)} %copy-done.3), custom_call_target="tpu_custom_call" | custom-call | tf_op jit(solution)/shard_map/assemble/pallas_call | solution.py:268
  (62 shorter events, 16.4 us)
Async XLA Ops:
  3.4 27.4 %collective-permute-start.2 = (f32[512,256]{1,0:T(8,128)}, f32[512,256]{1,0:T(8,128)S(1)}, u32[]{:S(2)}, u32[]{:S(2)}) collective-permute-start(f32[512,256]{1,0:T(8,128)} %get-tuple-element.22.refs_0_), channel_id=1, source_target_pairs={{224,0},{128,32},{160,64},{192,96},{96,128},{0,160},{32,192},{64,2... | collective-permute-start | bytes 1572872 | tf_op jit(solution)/shard_map/ppermute | solution.py:284
  8.1 22.8 %collective-permute-start.1 = (f32[512,256]{1,0:T(8,128)}, f32[512,256]{1,0:T(8,128)S(1)}, u32[]{:S(2)}, u32[]{:S(2)}) collective-permute-start(f32[512,256]{1,0:T(8,128)} %get-tuple-element.22.refs_0_), channel_id=1, source_target_pairs={{32,0},{64,32},{96,64},{0,96},{160,128},{192,160},{224,192},{128,2... | collective-permute-start | bytes 1572872 | tf_op jit(solution)/shard_map/ppermute | solution.py:284
  9.5 16.1 %copy-start.7 = (f32[512,256]{1,0:T(8,128)S(1)}, f32[512,256]{1,0:T(8,128)}, u32[]{:S(2)}) copy-start(f32[512,256]{1,0:T(8,128)} %get-tuple-element.22.refs_0_) | copy-start | bytes 1572868
  24.4 5.5 %collective-permute-start = (f32[136,256]{1,0:T(8,128)}, f32[136,256]{1,0:T(8,128)S(1)}, u32[]{:S(2)}, u32[]{:S(2)}) collective-permute-start(f32[136,256]{1,0:T(8,128)} %get-tuple-element.19), channel_id=1, source_target_pairs={{0,1},{1,0},{2,3},{3,2},{4,5},{5,4},{6,7},{7,6},{8,9},{9,8},{10,11... | collective-permute-start | bytes 417800 | tf_op jit(solution)/shard_map/ppermute | solution.py:290
  25.6 31.8 %collective-permute-start.8 = (f32[512,256]{1,0:T(8,128)S(1)}, f32[512,256]{1,0:T(8,128)S(1)}, u32[]{:S(2)}, u32[]{:S(2)}) collective-permute-start(f32[512,256]{1,0:T(8,128)S(1)} %copy-done.7), channel_id=1, source_target_pairs={{192,0},{224,32},{128,64},{160,96},{64,128},{96,160},{0,192},{32,2... | collective-permute-start | bytes 1572872 | tf_op jit(solution)/shard_map/ppermute | solution.py:284
  27.0 30.5 %collective-permute-start.7 = (f32[512,256]{1,0:T(8,128)S(1)}, f32[512,256]{1,0:T(8,128)S(1)}, u32[]{:S(2)}, u32[]{:S(2)}) collective-permute-start(f32[512,256]{1,0:T(8,128)S(1)} %copy-done.7), channel_id=1, source_target_pairs={{64,0},{96,32},{192,64},{224,96},{0,128},{32,160},{128,192},{160,2... | collective-permute-start | bytes 1572872 | tf_op jit(solution)/shard_map/ppermute | solution.py:284
  30.8 0.8 copy-start.8
  56.8 13.9 %copy-start.4 = (f32[136,512]{1,0:T(8,128)S(1)}, f32[136,512]{1,0:T(8,128)}, u32[]{:S(2)}) copy-start(f32[136,512]{1,0:T(8,128)} %get-tuple-element.20) | copy-start | bytes 835588
  56.8 13.9 %collective-permute-start.3 = (f32[136,512]{1,0:T(8,128)}, f32[136,512]{1,0:T(8,128)S(1)}, u32[]{:S(2)}, u32[]{:S(2)}) collective-permute-start(f32[136,512]{1,0:T(8,128)} %get-tuple-element.21), channel_id=1, source_target_pairs={{0,1},{1,0},{2,3},{3,2},{4,5},{5,4},{6,7},{7,6},{8,9},{9,8},{10,11... | collective-permute-start | bytes 835592 | tf_op jit(solution)/shard_map/ppermute | solution.py:290
  57.4 0.8 copy-start.5
  70.3 22.1 %collective-permute-start.9 = (f32[136,384]{1,0:T(8,128)}, f32[136,384]{1,0:T(8,128)S(1)}, u32[]{:S(2)}, u32[]{:S(2)}) collective-permute-start(f32[136,384]{1,0:T(8,128)} %second1.1), channel_id=1, source_target_pairs={{0,1},{1,0},{2,3},{3,2},{4,5},{5,4},{6,7},{7,6},{8,9},{9,8},{10,11... | collective-permute-start | bytes 626696 | tf_op jit(solution)/shard_map/ppermute | solution.py:290
  72.3 23.5 %all-to-all-start = ((f32[16,8,896]{2,1,0:T(8,128)}), f32[16,8,896]{2,1,0:T(8,128)S(1)}, u32[]{:S(2)}, u32[]{:S(2)}) async-start(f32[16,8,896]{2,1,0:T(8,128)} %pad_maximum_fusion), calls=%async_computation | async-start | bytes 917504 | tf_op jit(solution)/shard_map/all_to_all | solution.py:295
  95.7 17.8 %all-to-all-start.2 = ((f32[16,8,512]{2,1,0:T(8,128)}), f32[16,8,512]{2,1,0:T(8,128)S(1)}, u32[]{:S(2)}, u32[]{:S(2)}) async-start(f32[16,8,512]{2,1,0:T(8,128)} %pad_maximum_fusion.1), calls=%async_computation.2 | async-start | bytes 524288 | tf_op jit(solution)/shard_map/all_to_all | solution.py:295
  102.5 4.1 %collective-permute-start.4 = (f32[8,256]{1,0:T(8,128)S(1)}, f32[8,256]{1,0:T(8,128)S(1)}, u32[]{:S(2)}, u32[]{:S(2)}) collective-permute-start(f32[8,256]{1,0:T(8,128)S(1)} %get-tuple-element.23), channel_id=1, source_target_pairs={{0,32},{32,64},{64,96},{96,0},{128,160},{160,192},{192,224},{224,1... | collective-permute-start | bytes 24584 | tf_op jit(solution)/shard_map/ppermute | solution.py:287
  102.9 5.1 %collective-permute-start.5 = (f32[8,256]{1,0:T(8,128)S(1)}, f32[8,256]{1,0:T(8,128)S(1)}, u32[]{:S(2)}, u32[]{:S(2)}) collective-permute-start(f32[8,256]{1,0:T(8,128)S(1)} %get-tuple-element.24), channel_id=1, source_target_pairs={{0,224},{32,128},{64,160},{96,192},{128,96},{160,0},{192,32},{224,... | collective-permute-start | bytes 24584 | tf_op jit(solution)/shard_map/ppermute | solution.py:287
  114.4 21.7 %all-to-all-start.1 = ((f32[16,8,1280]{2,1,0:T(8,128)}), f32[16,8,1280]{2,1,0:T(8,128)S(1)}, u32[]{:S(2)}, u32[]{:S(2)}) async-start(f32[16,8,1280]{2,1,0:T(8,128)} %broadcast_in_dim.9), calls=%async_computation.1 | async-start | bytes 1310720 | tf_op jit(solution)/shard_map/all_to_all | solution.py:295
  118.1 7.4 %collective-permute-start.10 = (f32[8,256]{1,0:T(8,128)S(1)}, f32[8,256]{1,0:T(8,128)S(1)}, u32[]{:S(2)}, u32[]{:S(2)}) collective-permute-start(f32[8,256]{1,0:T(8,128)S(1)} %slice.117), channel_id=1, source_target_pairs={{0,64},{32,96},{64,192},{96,224},{128,0},{160,32},{192,128},{224,1... | collective-permute-start | bytes 24584 | tf_op jit(solution)/shard_map/ppermute | solution.py:287
  119.1 6.4 %collective-permute-start.11 = (f32[8,128]{1,0:T(8,128)S(1)}, f32[8,128]{1,0:T(8,128)S(1)}, u32[]{:S(2)}, u32[]{:S(2)}) collective-permute-start(f32[8,128]{1,0:T(8,128)S(1)} %slice.118), channel_id=1, source_target_pairs={{0,192},{32,224},{64,128},{96,160},{128,64},{160,96},{192,0},{224,... | collective-permute-start | bytes 12296 | tf_op jit(solution)/shard_map/ppermute | solution.py:287
  136.1 22.4 %copy-start = (f32[16,8,1280]{2,1,0:T(8,128)}, f32[16,8,1280]{2,1,0:T(8,128)S(1)}, u32[]{:S(2)}) copy-start(f32[16,8,1280]{2,1,0:T(8,128)S(1)} %all-to-all-done.1.own1) | copy-start | bytes 1966084
  136.9 16.6 %all-to-all-start.3 = ((f32[16,8,768]{2,1,0:T(8,128)}), f32[16,8,768]{2,1,0:T(8,128)S(1)}, u32[]{:S(2)}, u32[]{:S(2)}) async-start(f32[16,8,768]{2,1,0:T(8,128)} %broadcast_in_dim.11), calls=%async_computation.3 | async-start | bytes 786432 | tf_op jit(solution)/shard_map/all_to_all | solution.py:295
  141.5 17.0 %collective-permute-start.6 = (f32[16,8,1280]{2,1,0:T(8,128)S(1)}, f32[16,8,1280]{2,1,0:T(8,128)S(1)}, u32[]{:S(2)}, u32[]{:S(2)}) collective-permute-start(f32[16,8,1280]{2,1,0:T(8,128)S(1)} %all-to-all-done.1.own1), channel_id=1, source_target_pairs={{0,1},{1,0},{2,3},{3,2},{4,5},{5,4},{6,7},{7,6},{8,9},{9,8},{10,11... | collective-permute-start | bytes 1966088 | tf_op jit(solution)/shard_map/ppermute | solution.py:290
  153.5 5.0 %copy-start.1 = (f32[16,8,768]{2,1,0:T(8,128)}, f32[16,8,768]{2,1,0:T(8,128)S(1)}, u32[]{:S(2)}) copy-start(f32[16,8,768]{2,1,0:T(8,128)S(1)} %all-to-all-done.3.own2) | copy-start | bytes 1179652
  153.5 5.0 %collective-permute-start.12 = (f32[16,8,768]{2,1,0:T(8,128)S(1)}, f32[16,8,768]{2,1,0:T(8,128)S(1)}, u32[]{:S(2)}, u32[]{:S(2)}) collective-permute-start(f32[16,8,768]{2,1,0:T(8,128)S(1)} %all-to-all-done.3.own2), channel_id=1, source_target_pairs={{0,1},{1,0},{2,3},{3,2},{4,5},{5,4},{6,7},{7,6},{8,9},{9,8},{10,11... | collective-permute-start | bytes 1179656 | tf_op jit(solution)/shard_map/ppermute | solution.py:290
  159.3 0.9 copy-start.2
  (3 other events, 2.4 us)

commit v2 on v1

v2 whole, which is shorter than its diff:
```python
import jax
import jax.numpy as jnp
from jax import lax
from jax.experimental import pallas as pl
from jax.experimental.pallas import tpu as pltpu
from jax.sharding import PartitionSpec as P

F32 = jnp.float32
BF16 = jnp.bfloat16
ROWS = 256
KS = 512
BLOCKS = 8
GROUP = 8
PAIRS = GROUP // 2
GROUPS = ROWS // GROUP


def block_at(y, x):
    return (y % 2) * 4 + x % 4


def partner_tables():
    first, second, third, fourth = [], [], [], []
    for b in range(BLOCKS):
        y, x = b // 4, b % 4
        first.append(block_at(y, x + 1))
        second.append(block_at(y + 1, x + 3))
        cycle = {(0, 0): (0, 2), (0, 1): (1, 2), (1, 1): (1, 0), (1, 0): (0, 0)}
        ny, nx = cycle[(y, x // 2)]
        third.append(block_at(ny, nx + x % 2))
        fourth.append(block_at(y + 1, x + 2))
    return [first, second, third, fourth]


PARTNERS = partner_tables()
OWNERS = [[table.index(b) for b in range(BLOCKS)] for table in PARTNERS]


def params():
    return pltpu.CompilerParams(vmem_limit_bytes=56 << 20)


def in_vmem(n):
    return [pl.BlockSpec(memory_space=pltpu.VMEM)] * n


def branch_sums(ref, lane):
    def add(k8, total):
        at = pl.ds(pl.multiple_of(k8 * 8, 8), 8)
        return total + ref[at, lane : lane + 128]

    total = lax.fori_loop(0, KS // 8, add, jnp.zeros((8, 128), F32), unroll=8)
    return jnp.sum(total, axis=0, keepdims=True)


def weigh_kernel(counts_ref, totals_ref, lengths_ref, wt_ref, split_ref, row_ref, col_ref):
    scaled = lengths_ref[...].astype(F32) * 0.001
    wt = (scaled * counts_ref[...].astype(F32)).T / totals_ref[...].astype(F32)
    wt_ref[...] = wt
    for n in range(8):
        x = wt[:, n * 32 : (n + 1) * 32]
        high = x.astype(BF16)
        rest = x - high.astype(F32)
        middle = rest.astype(BF16)
        low = (rest - middle.astype(F32)).astype(BF16)
        split_ref[n] = jnp.concatenate([high, middle, low, jnp.zeros_like(low)], axis=1)
    for h in range(2):
        sums = branch_sums(wt_ref, h * 128)
        row_ref[:, h * 128 : (h + 1) * 128] = jnp.broadcast_to(sums, (8, 128))
        col_ref[h * 128 : (h + 1) * 128, :] = jnp.broadcast_to(sums, (128, 128)).T


def weigh(counts, totals, lengths):
    return pl.pallas_call(
        weigh_kernel,
        out_shape=(
            jax.ShapeDtypeStruct((KS, ROWS), F32),
            jax.ShapeDtypeStruct((8, KS, 128), BF16),
            jax.ShapeDtypeStruct((8, ROWS), F32),
            jax.ShapeDtypeStruct((ROWS, 128), F32),
        ),
        compiler_params=params(),
        name="weigh",
    )(counts, totals.reshape(1, ROWS), lengths.reshape(1, KS))


def spread_call(name, n_blocks, columns, width, group, mass_row):
    pairs = group // 2
    groups = ROWS // group

    def kernel(split_ref, col_ref, *refs):
        sources = refs[:n_blocks]
        out_ref = refs[n_blocks]
        block_ref, pick_ref, even_ref, odd_ref, sems = refs[n_blocks + 1 :]
        y = lax.axis_index("blk") // 4

        loads = [
            pltpu.make_async_copy(src, block_ref.at[n], sems.at[n])
            for n, src in enumerate(sources)
        ]
        for load in loads:
            load.start()

        part = lax.broadcasted_iota(jnp.int32, (128, 256), 0)
        lane = lax.broadcasted_iota(jnp.int32, (128, 256), 1)
        want = jnp.where(part < 96, part % 32 - lane // 128, -1)
        for p in range(16):
            pick_ref[p] = jnp.where(want == 2 * p, 1.0, 0.0).astype(BF16)

        def broadcast_pair(into, g, q, at=slice(0, KS)):
            pair = g * pairs + q
            into[q, at] = jnp.dot(
                split_ref[pair // 16, at], pick_ref[pair % 16], preferred_element_type=F32
            )

        for q in range(pairs):
            broadcast_pair(even_ref, 0, q)
        for load in loads:
            load.wait()

        def span(n, lane, at):
            if isinstance(lane, int):
                return block_ref[n, at, lane : lane + 128]
            return block_ref[n, at, pl.ds(pl.multiple_of(lane, 128), 128)]

        for half in range(2):
            below = [jnp.zeros((1, 128), F32)] * mass_row
            for n, lane in columns(half, y):
                total = jnp.zeros((8, 128), F32)
                for k8 in range(KS // 8):
                    total = total + span(n, lane, slice(k8 * 8, k8 * 8 + 8))
                below.append(jnp.sum(total, axis=0, keepdims=True))
            below += [jnp.zeros((1, 128), F32)] * (8 - len(below))
            out_ref[half, 128:136, 0:128] = jnp.concatenate(below, axis=0)

        def one_group(g, now, later):
            half = g // (groups // 2)
            cols = columns(half, y)
            n_cols = len(cols)
            following = jnp.minimum(g + 1, groups - 1)
            steps = []
            if group == 8:
                for q in range(pairs):
                    broadcast_pair(later, following, q)
            else:
                steps = [(q, slice(k, k + 128)) for k in range(0, KS, 128) for q in range(pairs)]
            acc = [jnp.zeros((8, 128), F32)] * (group * n_cols)
            for k8 in range(KS // 8):
                if steps and k8 % 2 == 0:
                    q, at = steps[k8 // 2]
                    broadcast_pair(later, following, q, at)
                at = slice(k8 * 8, k8 * 8 + 8)
                spans = [span(n, lane, at) for n, lane in cols]
                for r in range(group):
                    own = now[r // 2, at, 128 * (r % 2) : 128 * (r % 2) + 128]
                    for j in range(n_cols):
                        acc[r * n_cols + j] += jnp.minimum(own, spans[j])
            for r0 in range(0, group, 8):
                first = pl.multiple_of(g * group + r0, 8)
                row = pl.multiple_of(first - half * 128, 8)
                own_mass = col_ref[pl.ds(first, 8), :]
                for j in range(n_cols):
                    mass = out_ref[half, 128 + mass_row + j : 129 + mass_row + j, 0:128]
                    least = jnp.concatenate(
                        [
                            jnp.sum(acc[(r0 + r) * n_cols + j], axis=0, keepdims=True)
                            for r in range(8)
                        ],
                        axis=0,
                    )
                    out_ref[half, pl.ds(row, 8), 128 * j : 128 * j + 128] = (
                        own_mass + mass - 2.0 * least
                    )

        def two_groups(t, carry):
            one_group(2 * t, even_ref, odd_ref)
            one_group(2 * t + 1, odd_ref, even_ref)
            return carry

        lax.fori_loop(0, groups // 2, two_groups, 0)

    def call(split, col, *blocks):
        return pl.pallas_call(
            kernel,
            out_shape=jax.ShapeDtypeStruct((2, 136, width), F32),
            in_specs=in_vmem(2) + [pl.BlockSpec(memory_space=pl.ANY)] * n_blocks,
            out_specs=in_vmem(1)[0],
            scratch_shapes=[
                pltpu.VMEM((n_blocks, KS, ROWS), F32),
                pltpu.VMEM((16, 128, 256), BF16),
                pltpu.VMEM((pairs, KS, 256), F32),
                pltpu.VMEM((pairs, KS, 256), F32),
                pltpu.SemaphoreType.DMA((n_blocks,)),
            ],
            compiler_params=params(),
            cost_estimate=pl.CostEstimate(
                flops=width * ROWS * KS * 250, bytes_accessed=4 << 20, transcendentals=0
            ),
            name=name,
        )(split, col, *blocks)

    return call


def diagonal_columns(half, y):
    return [(0, 128), (0, 0)]


def first_columns(half, y):
    return [(0, 0), (0, 128), (1, 0), (1, 128)]


def second_columns(half, y):
    return [(0, 0), (0, 128), (1, (half ^ y) * 128)]


def block_partner(b, slot):
    y, x = b // 4, b % 4
    if slot == 0:
        return b
    if slot == 1:
        return y * 4 + (x + 1) % 4
    if slot == 2:
        return (1 - y) * 4 + (x + 3) % 4
    if slot == 4:
        return (1 - y) * 4 + (x + 2) % 4
    if slot == 5:
        return y * 4 + (x + 3) % 4
    if slot == 6:
        return (1 - y) * 4 + (x + 1) % 4
    far = x // 2
    keep_y = (far == y) if slot == 3 else (far != y)
    return jnp.where(keep_y, y * 4 + (x + 2) % 4, (1 - y) * 4 + x)


DIRECT = 1152
SWAPPED = 896


def assemble_kernel(own1, other1, own2, other2, out_ref, all_ref, turned_ref, sems, out_sems):
    core = lax.axis_index("branch") % 2
    b = lax.axis_index("blk")
    y = b // 4
    loads = []
    for n, (ref, c, lane) in enumerate(
        ((own2, core, DIRECT), (other2, 1 - core, DIRECT), (own1, core, 0), (other1, 1 - core, 0))
    ):
        to = pl.ds(pl.multiple_of(c * 128, 128), 128)
        into = all_ref.at[to, lane : lane + ref.shape[1]]
        loads.append(pltpu.make_async_copy(ref, into, sems.at[n]))
    for load in loads:
        load.start()

    def columns(slot, half=None):
        first = block_partner(b, slot) * ROWS
        if half is None:
            return pl.ds(pl.multiple_of(first, ROWS), ROWS)
        return pl.ds(pl.multiple_of(first + half * 128, 128), 128)

    stores = []

    def store(src, rows, cols):
        copy = pltpu.make_async_copy(src, out_ref.at[rows, cols], out_sems.at[len(stores)])
        copy.start()
        stores.append(copy)

    every = slice(0, ROWS)
    for load in loads:
        load.wait()
    for slot, lane in ((1, 256), (2, 512), (3, 768)):
        store(all_ref.at[:, lane : lane + ROWS], every, columns(slot))
    for half in range(2):
        rows = slice(half * 128, half * 128 + 128)
        store(all_ref.at[rows, 1024:1152], rows, columns(4, half ^ y))
        store(all_ref.at[:, 128 - half * 128 : 256 - half * 128], every, columns(0, half))
    for n, slot in enumerate((5, 6, 7)):
        lane = DIRECT + n * ROWS
        turned_ref[n] = all_ref[:, lane : lane + ROWS].T
        store(turned_ref.at[n], every, columns(slot))
    for half in range(2):
        at = slice(half * 128, half * 128 + 128)
        turned_ref[3, 0:128, at] = all_ref[at, DIRECT + 768 : DIRECT + 896].T
        to = pl.ds(pl.multiple_of((half ^ (1 - y)) * 128, 128), 128)
        store(turned_ref.at[3, 0:128, at], to, columns(4, half))
    for copy in stores:
        copy.wait()


def assemble(*pieces):
    anywhere = pl.BlockSpec(memory_space=pl.ANY)
    return pl.pallas_call(
        assemble_kernel,
        out_shape=jax.ShapeDtypeStruct((ROWS, BLOCKS * ROWS), F32),
        in_specs=[anywhere] * 4,
        out_specs=anywhere,
        scratch_shapes=[
            pltpu.VMEM((ROWS, DIRECT + SWAPPED), F32),
            pltpu.VMEM((4, ROWS, ROWS), F32),
            pltpu.SemaphoreType.DMA((4,)),
            pltpu.SemaphoreType.DMA((12,)),
        ],
        compiler_params=params(),
        name="assemble",
    )(*[p.reshape(128, p.shape[2]) for p in pieces])


def on_device(counts, totals, lengths):
    branch = lax.axis_index("branch")
    place = branch // 2

    def from_partner(v, n):
        return lax.ppermute(v, "blk", [(PARTNERS[n][b], b) for b in range(BLOCKS)])

    def to_partner(v, n):
        return lax.ppermute(v, "blk", [(b, PARTNERS[n][b]) for b in range(BLOCKS)])

    def other_core(v):
        return lax.ppermute(v, "branch", [(i, i ^ 1) for i in range(32)])

    chips = [[2 * p + c for p in range(16)] for c in range(2)]

    def over_chips(v):
        return lax.all_to_all(v, "branch", 0, 0, axis_index_groups=chips)

    def gather(pieces):
        mine = jnp.concatenate(pieces, axis=1)
        whole = over_chips(jnp.broadcast_to(mine[None], (16, *mine.shape)))
        return whole, other_core(whole)

    wt, split, mass_row, mass_col = weigh(counts, totals, lengths)
    got = [from_partner(wt, n) for n in range(2)]
    diagonal = spread_call("diagonal", 1, diagonal_columns, 256, 16, 0)
    first = spread_call("first", 2, first_columns, 512, 8, 2)
    second = spread_call("second", 2, second_columns, 384, 8, 0)

    part0 = diagonal(split, mass_col, wt)
    later, part0 = lax.optimization_barrier((wt, part0))
    got += [from_partner(later, n) for n in (2, 3)]
    part1 = first(split, mass_col, got[0], got[1])
    part2 = second(split, mass_col, got[2], got[3])

    def on_chip(part):
        both = part + other_core(part)
        return lax.dynamic_index_in_dim(both, branch % 2, 0, False)

    parts = [on_chip(part) for part in (part0, part1, part2)]
    tiles = [p[:128].reshape(16, 8, -1) for p in parts]
    masses = [
        jnp.broadcast_to(m[None], (16, 8, 128))
        for m in (parts[0][128:, :128] + parts[1][128:, :128], parts[2][128:, :128])
    ]
    shard = jnp.sum(over_chips(jnp.concatenate(tiles + masses, axis=2)), axis=0)

    mass = shard[:, DIRECT : DIRECT + 128]
    own_half = jnp.where(branch % 2 == 0, mass[1], mass[0])
    own_mass = lax.dynamic_slice_in_dim(own_half, place * 8, 8)[:, None]
    parts = jnp.concatenate([mass[0:6], shard[0:3, DIRECT + 128 :]]).reshape(DIRECT)
    dist = shard[:, :DIRECT] / (own_mass + parts[None, :])
    swapped = [
        to_partner(dist[:, 256 * (n + 1) : min(256 * (n + 2), DIRECT)], n) for n in range(4)
    ]
    own1, other1 = gather([dist])
    own2, other2 = gather(swapped)
    return assemble(own1, other1, own2, other2)


def solution(mesh):
    placed = (P("blk", "branch"), P("blk"), P("branch"))
    return jax.shard_map(
        on_device, mesh=mesh, in_specs=placed, out_specs=P("blk", None), check_vma=False
    )
```

time: 164 us -> 164 us (level)
  waiting for transfers between devices: 34.1 us -> 41.1 us
  starting transfers between devices: 48.7 us -> 44.8 us
  other arithmetic: 5.04 us -> 1.17 us
  local copies, waits for them, and re-layouts: 6.66 us -> 9.35 us
  Pallas kernels: 69 us -> 66.6 us
    all_to_all x4 -> x3, waiting for transfers between devices: 26.9 us -> 35 us  [over_chips(): return lax.all_to_all(v, 'branch', 0, 0, axis_index_groups=chips)]
    all_to_all x4 -> x3, starting transfers between devices: 23.1 us -> 17.8 us  [over_chips(): return lax.all_to_all(v, 'branch', 0, 0, axis_index_groups=chips)]
    ppermute x4, waiting for transfers between devices: 5.84 us -> 3.72 us  [to_partner(): return lax.ppermute(v, 'blk', [(b, PARTNERS[n][b]) for b in range(BLOCKS)])]
    unnamed x20 -> x26, local copies, waits for them, and re-layouts: 4.83 us -> 6.93 us
    reshape x3 -> x0, other arithmetic: 1.91 us -> none  [scatter(): (k[:128] + r[:128]).reshape(16, 8, -1)]
    pallas_call x4 -> x3, Pallas kernels: 62.1 us -> 60.3 us  [call(): pl.pallas_call(kernel, out_shape=jax.ShapeDtypeStruct((2, 136, width), F3...]
  transfers between devices with their start and end apart: 17 -> 16, of which waited for: 7 -> 6; matrix products, arithmetic and copies ran while one was open for 3% -> 1% of each run, Pallas kernels for 38% -> 37%
where the time goes in v2:
time: 164 us; the launch traced here: 163 us
  Pallas kernels  66.6 us (41%)
  starting transfers between devices  44.8 us (27%)
  waiting for transfers between devices  41.1 us (25%)
  local copies, waits for them, and re-layouts  9.35 us (6%)
    pallas_call x3, Pallas kernels, call(): pl.pallas_call(kernel, out_shape=jax.ShapeDtypeStruct((2, 136, width), F3...  60.3 us
    all_to_all x3, waiting for transfers between devices, over_chips(): return lax.all_to_all(v, 'branch', 0, 0, axis_index_groups=chips)  35 us
    all_to_all x3, starting transfers between devices, over_chips(): return lax.all_to_all(v, 'branch', 0, 0, axis_index_groups=chips)  17.8 us
    ppermute x4, starting transfers between devices, from_partner(): return lax.ppermute(v, 'blk', [(PARTNERS[n][b], b) for b in range(BLOCKS)])  10.4 us
    ppermute x5, starting transfers between devices, other_core(): return lax.ppermute(v, 'branch', [(i, i ^ 1) for i in range(32)])  9.03 us
    ppermute x4, starting transfers between devices, to_partner(): return lax.ppermute(v, 'blk', [(b, PARTNERS[n][b]) for b in range(BLOCKS)])  7.52 us
    unnamed x26, local copies, waits for them, and re-layouts  6.93 us
    ppermute x4, waiting for transfers between devices, to_partner(): return lax.ppermute(v, 'blk', [(b, PARTNERS[n][b]) for b in range(BLOCKS)])  3.72 us
  transfers between devices with their start and end apart: 16, of which 6 were waited for; matrix products, arithmetic and copies ran while one was open for 1% of the time, Pallas kernels for 37%

profile of v2, /device:TPU:1, one launch (start us, length us, event | category | flops | bytes accessed | tf_op | source)
XLA Modules:
  0.0 163.5 jit_solution(1013840648971065564)
XLA Ops:
  0.0 3.4 %weigh.1 = (f32[512,256]{1,0:T(8,128)}, bf16[8,512,128]{2,1,0:T(8,128)(2,1)}, f32[8,256]{1,0:T(8,128)}, f32[256,128]{1,0:T(8,128)}) custom-call(s32[256,512]{1,0:T(8,128)} %counts_ref.1, s32[1,256]{1,0:T(1,128)} %bitcast.33, s32[1,512]{1,0:T(1,128)} %bitcast.32), custom_call_target="tpu_custom_call" | custom-call | tf_op jit(solution)/shard_map/weigh/pallas_call | solution.py:74
  3.4 4.7 %collective-permute-start.2 = (f32[512,256]{1,0:T(8,128)}, f32[512,256]{1,0:T(8,128)S(1)}, u32[]{:S(2)}, u32[]{:S(2)}) collective-permute-start(f32[512,256]{1,0:T(8,128)} %get-tuple-element.14.refs_0_), channel_id=1, source_target_pairs={{224,0},{128,32},{160,64},{192,96},{96,128},{0,160},{32,192},{64,2... | collective-permute-start | bytes 1572872 | tf_op jit(solution)/shard_map/ppermute | solution.py:312
  8.0 1.5 collective-permute-start.1
  9.5 14.8 %diagonal.1 = f32[2,136,256]{2,1,0:T(8,128)} custom-call(bf16[8,512,128]{2,1,0:T(8,128)(2,1)} %get-tuple-element.11.split_ref, f32[256,128]{1,0:T(8,128)} %get-tuple-element.12.col_ref, f32[512,256]{1,0:T(8,128)} %get-tuple-element.14.refs_0_), custom_call_target="tpu_custom_call" | custom-call | flops 8388608000 | bytes 4194304 | tf_op jit(solution)/shard_map/diagonal/pallas_call | solution.py:183
  24.3 1.4 collective-permute-start.5
  25.7 2.9 %collective-permute-start.4 = (f32[512,256]{1,0:T(8,128)S(1)}, f32[512,256]{1,0:T(8,128)S(1)}, u32[]{:S(2)}, u32[]{:S(2)}) collective-permute-start(f32[512,256]{1,0:T(8,128)S(1)} %copy-done.6), channel_id=1, source_target_pairs={{64,0},{96,32},{192,64},{224,96},{0,128},{32,160},{128,192},{160,2... | collective-permute-start | bytes 1572872 | tf_op jit(solution)/shard_map/ppermute | solution.py:312
  28.6 1.8 %collective-permute-start = (f32[2,136,256]{2,1,0:T(8,128)}, f32[2,136,256]{2,1,0:T(8,128)S(1)}, u32[]{:S(2)}, u32[]{:S(2)}) collective-permute-start(f32[2,136,256]{2,1,0:T(8,128)} %diagonal.1), channel_id=1, source_target_pairs={{0,1},{1,0},{2,3},{3,2},{4,5},{5,4},{6,7},{7,6},{8,9},{9,8},{10,11... | collective-permute-start | bytes 835592 | tf_op jit(solution)/shard_map/ppermute | solution.py:318
  32.1 24.8 %first.1 = f32[2,136,512]{2,1,0:T(8,128)} custom-call(bf16[8,512,128]{2,1,0:T(8,128)(2,1)} %get-tuple-element.11.split_ref, f32[256,128]{1,0:T(8,128)} %get-tuple-element.12.col_ref, f32[512,256]{1,0:T(8,128)} %copy-done.10, f32[512,256]{1,0:T(8,128)} %copy-done.9), custom_call_target="tpu_custom_call" | custom-call | flops 16777216000 | bytes 4194304 | tf_op jit(solution)/shard_map/first/pallas_call | solution.py:183
  58.6 20.7 %second.1 = f32[2,136,384]{2,1,0:T(8,128)} custom-call(bf16[8,512,128]{2,1,0:T(8,128)(2,1)} %get-tuple-element.11.split_ref, f32[256,128]{1,0:T(8,128)} %get-tuple-element.12.col_ref, f32[512,256]{1,0:T(8,128)} %copy-done.8, f32[512,256]{1,0:T(8,128)} %copy-done.7), custom_call_target="tpu_custom_call" | custom-call | flops 12582912000 | bytes 4194304 | tf_op jit(solution)/shard_map/second/pallas_call | solution.py:183
  81.5 1.0 dynamic-slice_add_fusion.1
  85.2 8.4 %all-to-all-start = ((f32[16,8,1408]{2,1,0:T(8,128)}), f32[16,8,1408]{2,1,0:T(8,128)S(1)}, u32[]{:S(2)}, u32[]{:S(2)}) async-start(f32[16,8,1408]{2,1,0:T(8,128)} %broadcast_dynamic-update-slice_fusion), calls=%async_computation | async-start | bytes 1441792 | tf_op jit(solution)/shard_map/all_to_all | solution.py:323
  93.6 19.6 %all-to-all-done = f32[16,8,1408]{2,1,0:T(8,128)S(1)} async-done(((f32[16,8,1408]{2,1,0:T(8,128)}), f32[16,8,1408]{2,1,0:T(8,128)S(1)}, u32[]{:S(2)}, u32[]{:S(2)}) %all-to-all-start) | async-done | bytes 720928 | tf_op jit(solution)/shard_map/all_to_all | solution.py:323
  114.3 5.0 %all-to-all-start.1 = ((f32[16,8,1152]{2,1,0:T(8,128)}), f32[16,8,1152]{2,1,0:T(8,128)S(1)}, u32[]{:S(2)}, u32[]{:S(2)}) async-start(f32[16,8,1152]{2,1,0:T(8,128)} %broadcast_in_dim.10), calls=%async_computation.1 | async-start | bytes 1179648 | tf_op jit(solution)/shard_map/all_to_all | solution.py:323
  119.8 1.6 collective-permute-start.10
  121.3 2.9 %collective-permute-start.9 = (f32[8,256]{1,0:T(8,128)S(1)}, f32[8,256]{1,0:T(8,128)S(1)}, u32[]{:S(2)}, u32[]{:S(2)}) collective-permute-start(f32[8,256]{1,0:T(8,128)S(1)} %get-tuple-element.17), channel_id=1, source_target_pairs={{0,224},{32,128},{64,160},{96,192},{128,96},{160,0},{192,32},{224,... | collective-permute-start | bytes 24584 | tf_op jit(solution)/shard_map/ppermute | solution.py:315
  124.2 2.7 %collective-permute-start.11 = (f32[8,128]{1,0:T(8,128)S(1)}, f32[8,128]{1,0:T(8,128)S(1)}, u32[]{:S(2)}, u32[]{:S(2)}) collective-permute-start(f32[8,128]{1,0:T(8,128)S(1)} %slice.81), channel_id=1, source_target_pairs={{0,192},{32,224},{64,128},{96,160},{128,64},{160,96},{192,0},{224,... | collective-permute-start | bytes 12296 | tf_op jit(solution)/shard_map/ppermute | solution.py:315
  126.9 3.7 %collective-permute-done.11 = f32[8,128]{1,0:T(8,128)S(1)} collective-permute-done((f32[8,128]{1,0:T(8,128)S(1)}, f32[8,128]{1,0:T(8,128)S(1)}, u32[]{:S(2)}, u32[]{:S(2)}) %collective-permute-start.11) | collective-permute-done | bytes 4128 | tf_op jit(solution)/shard_map/ppermute | solution.py:315
  130.6 5.1 %all-to-all-done.1 = f32[16,8,1152]{2,1,0:T(8,128)S(1)} async-done(((f32[16,8,1152]{2,1,0:T(8,128)}), f32[16,8,1152]{2,1,0:T(8,128)S(1)}, u32[]{:S(2)}, u32[]{:S(2)}) %all-to-all-start.1) | async-done | bytes 589856 | tf_op jit(solution)/shard_map/all_to_all | solution.py:323
  136.6 4.4 %all-to-all-start.2 = ((f32[16,8,896]{2,1,0:T(8,128)}), f32[16,8,896]{2,1,0:T(8,128)S(1)}, u32[]{:S(2)}, u32[]{:S(2)}) async-start(f32[16,8,896]{2,1,0:T(8,128)} %broadcast_in_dim.11), calls=%async_computation.2 | async-start | bytes 917504 | tf_op jit(solution)/shard_map/all_to_all | solution.py:323
  141.0 2.4 %collective-permute-start.7 = (f32[16,8,1152]{2,1,0:T(8,128)S(1)}, f32[16,8,1152]{2,1,0:T(8,128)S(1)}, u32[]{:S(2)}, u32[]{:S(2)}) collective-permute-start(f32[16,8,1152]{2,1,0:T(8,128)S(1)} %all-to-all-done.1), channel_id=1, source_target_pairs={{0,1},{1,0},{2,3},{3,2},{4,5},{5,4},{6,7},{7,6},{8,9},{9,8},{10,11... | collective-permute-start | bytes 1769480 | tf_op jit(solution)/shard_map/ppermute | solution.py:318
  143.4 10.3 %all-to-all-done.2 = f32[16,8,896]{2,1,0:T(8,128)S(1)} async-done(((f32[16,8,896]{2,1,0:T(8,128)}), f32[16,8,896]{2,1,0:T(8,128)S(1)}, u32[]{:S(2)}, u32[]{:S(2)}) %all-to-all-start.2) | async-done | bytes 458784 | tf_op jit(solution)/shard_map/all_to_all | solution.py:323
  153.7 4.2 %collective-permute-start.12 = (f32[16,8,896]{2,1,0:T(8,128)S(1)}, f32[16,8,896]{2,1,0:T(8,128)S(1)}, u32[]{:S(2)}, u32[]{:S(2)}) collective-permute-start(f32[16,8,896]{2,1,0:T(8,128)S(1)} %all-to-all-done.2), channel_id=1, source_target_pairs={{0,1},{1,0},{2,3},{3,2},{4,5},{5,4},{6,7},{7,6},{8,9},{9,8},{10,11... | collective-permute-start | bytes 1376264 | tf_op jit(solution)/shard_map/ppermute | solution.py:318
  157.9 1.4 collective-permute-done.12
  160.3 3.0 %assemble.1 = f32[256,2048]{1,0:T(8,128)} custom-call(f32[128,1152]{1,0:T(8,128)} %bitcast.25, f32[128,1152]{1,0:T(8,128)} %bitcast.29, f32[128,896]{1,0:T(8,128)} %bitcast.26, f32[128,896]{1,0:T(8,128)} %bitcast.31), custom_call_target="tpu_custom_call" | custom-call | tf_op jit(solution)/shard_map/assemble/pallas_call | solution.py:291
  (57 shorter events, 11.5 us)
Async XLA Ops:
  3.4 27.0 %collective-permute-start.2 = (f32[512,256]{1,0:T(8,128)}, f32[512,256]{1,0:T(8,128)S(1)}, u32[]{:S(2)}, u32[]{:S(2)}) collective-permute-start(f32[512,256]{1,0:T(8,128)} %get-tuple-element.14.refs_0_), channel_id=1, source_target_pairs={{224,0},{128,32},{160,64},{192,96},{96,128},{0,160},{32,192},{64,2... | collective-permute-start | bytes 1572872 | tf_op jit(solution)/shard_map/ppermute | solution.py:312
  8.0 22.4 %collective-permute-start.1 = (f32[512,256]{1,0:T(8,128)}, f32[512,256]{1,0:T(8,128)S(1)}, u32[]{:S(2)}, u32[]{:S(2)}) collective-permute-start(f32[512,256]{1,0:T(8,128)} %get-tuple-element.14.refs_0_), channel_id=1, source_target_pairs={{32,0},{64,32},{96,64},{0,96},{160,128},{192,160},{224,192},{128,2... | collective-permute-start | bytes 1572872 | tf_op jit(solution)/shard_map/ppermute | solution.py:312
  9.5 14.8 %copy-start.6 = (f32[512,256]{1,0:T(8,128)S(1)}, f32[512,256]{1,0:T(8,128)}, u32[]{:S(2)}) copy-start(f32[512,256]{1,0:T(8,128)} %get-tuple-element.14.refs_0_) | copy-start | bytes 1572868
  24.3 32.6 %collective-permute-start.5 = (f32[512,256]{1,0:T(8,128)S(1)}, f32[512,256]{1,0:T(8,128)S(1)}, u32[]{:S(2)}, u32[]{:S(2)}) collective-permute-start(f32[512,256]{1,0:T(8,128)S(1)} %copy-done.6), channel_id=1, source_target_pairs={{192,0},{224,32},{128,64},{160,96},{64,128},{96,160},{0,192},{32,2... | collective-permute-start | bytes 1572872 | tf_op jit(solution)/shard_map/ppermute | solution.py:312
  25.7 31.3 %collective-permute-start.4 = (f32[512,256]{1,0:T(8,128)S(1)}, f32[512,256]{1,0:T(8,128)S(1)}, u32[]{:S(2)}, u32[]{:S(2)}) collective-permute-start(f32[512,256]{1,0:T(8,128)S(1)} %copy-done.6), channel_id=1, source_target_pairs={{64,0},{96,32},{192,64},{224,96},{0,128},{32,160},{128,192},{160,2... | collective-permute-start | bytes 1572872 | tf_op jit(solution)/shard_map/ppermute | solution.py:312
  28.6 51.2 %collective-permute-start = (f32[2,136,256]{2,1,0:T(8,128)}, f32[2,136,256]{2,1,0:T(8,128)S(1)}, u32[]{:S(2)}, u32[]{:S(2)}) collective-permute-start(f32[2,136,256]{2,1,0:T(8,128)} %diagonal.1), channel_id=1, source_target_pairs={{0,1},{1,0},{2,3},{3,2},{4,5},{5,4},{6,7},{7,6},{8,9},{9,8},{10,11... | collective-permute-start | bytes 835592 | tf_op jit(solution)/shard_map/ppermute | solution.py:318
  30.4 0.8 copy-start.9
  56.8 23.0 %copy-start.5 = (f32[2,136,256]{2,1,0:T(8,128)S(1)}, f32[2,136,256]{2,1,0:T(8,128)}, u32[]{:S(2)}) copy-start(f32[2,136,256]{2,1,0:T(8,128)} %diagonal.1) | copy-start | bytes 835588
  56.8 25.6 %copy-start.4 = (f32[2,136,512]{2,1,0:T(8,128)S(1)}, f32[2,136,512]{2,1,0:T(8,128)}, u32[]{:S(2)}) copy-start(f32[2,136,512]{2,1,0:T(8,128)} %first.1) | copy-start | bytes 1671172
  56.8 25.6 %collective-permute-start.3 = (f32[2,136,512]{2,1,0:T(8,128)}, f32[2,136,512]{2,1,0:T(8,128)S(1)}, u32[]{:S(2)}, u32[]{:S(2)}) collective-permute-start(f32[2,136,512]{2,1,0:T(8,128)} %first.1), channel_id=1, source_target_pairs={{0,1},{1,0},{2,3},{3,2},{4,5},{5,4},{6,7},{7,6},{8,9},{9,8},{10,11... | collective-permute-start | bytes 1671176 | tf_op jit(solution)/shard_map/ppermute | solution.py:318
  57.8 0.8 copy-start.8
  79.3 2.2 %collective-permute-start.6 = (f32[2,136,384]{2,1,0:T(8,128)}, f32[2,136,384]{2,1,0:T(8,128)S(1)}, u32[]{:S(2)}, u32[]{:S(2)}) collective-permute-start(f32[2,136,384]{2,1,0:T(8,128)} %second.1), channel_id=1, source_target_pairs={{0,1},{1,0},{2,3},{3,2},{4,5},{5,4},{6,7},{7,6},{8,9},{9,8},{10,11... | collective-permute-start | bytes 1253384 | tf_op jit(solution)/shard_map/ppermute | solution.py:318
  85.2 28.0 %all-to-all-start = ((f32[16,8,1408]{2,1,0:T(8,128)}), f32[16,8,1408]{2,1,0:T(8,128)S(1)}, u32[]{:S(2)}, u32[]{:S(2)}) async-start(f32[16,8,1408]{2,1,0:T(8,128)} %broadcast_dynamic-update-slice_fusion), calls=%async_computation | async-start | bytes 1441792 | tf_op jit(solution)/shard_map/all_to_all | solution.py:323
  114.3 21.5 %all-to-all-start.1 = ((f32[16,8,1152]{2,1,0:T(8,128)}), f32[16,8,1152]{2,1,0:T(8,128)S(1)}, u32[]{:S(2)}, u32[]{:S(2)}) async-start(f32[16,8,1152]{2,1,0:T(8,128)} %broadcast_in_dim.10), calls=%async_computation.1 | async-start | bytes 1179648 | tf_op jit(solution)/shard_map/all_to_all | solution.py:323
  119.4 11.2 %collective-permute-start.8 = (f32[8,256]{1,0:T(8,128)S(1)}, f32[8,256]{1,0:T(8,128)S(1)}, u32[]{:S(2)}, u32[]{:S(2)}) collective-permute-start(f32[8,256]{1,0:T(8,128)S(1)} %get-tuple-element.15), channel_id=1, source_target_pairs={{0,32},{32,64},{64,96},{96,0},{128,160},{160,192},{192,224},{224,1... | collective-permute-start | bytes 24584 | tf_op jit(solution)/shard_map/ppermute | solution.py:315
  119.8 10.9 %collective-permute-start.10 = (f32[8,256]{1,0:T(8,128)S(1)}, f32[8,256]{1,0:T(8,128)S(1)}, u32[]{:S(2)}, u32[]{:S(2)}) collective-permute-start(f32[8,256]{1,0:T(8,128)S(1)} %get-tuple-element.16), channel_id=1, source_target_pairs={{0,64},{32,96},{64,192},{96,224},{128,0},{160,32},{192,128},{224,1... | collective-permute-start | bytes 24584 | tf_op jit(solution)/shard_map/ppermute | solution.py:315
  121.3 9.3 %collective-permute-start.9 = (f32[8,256]{1,0:T(8,128)S(1)}, f32[8,256]{1,0:T(8,128)S(1)}, u32[]{:S(2)}, u32[]{:S(2)}) collective-permute-start(f32[8,256]{1,0:T(8,128)S(1)} %get-tuple-element.17), channel_id=1, source_target_pairs={{0,224},{32,128},{64,160},{96,192},{128,96},{160,0},{192,32},{224,... | collective-permute-start | bytes 24584 | tf_op jit(solution)/shard_map/ppermute | solution.py:315
  124.2 6.4 %collective-permute-start.11 = (f32[8,128]{1,0:T(8,128)S(1)}, f32[8,128]{1,0:T(8,128)S(1)}, u32[]{:S(2)}, u32[]{:S(2)}) collective-permute-start(f32[8,128]{1,0:T(8,128)S(1)} %slice.81), channel_id=1, source_target_pairs={{0,192},{32,224},{64,128},{96,160},{128,64},{160,96},{192,0},{224,... | collective-permute-start | bytes 12296 | tf_op jit(solution)/shard_map/ppermute | solution.py:315
  135.8 23.6 %copy-start = (f32[16,8,1152]{2,1,0:T(8,128)}, f32[16,8,1152]{2,1,0:T(8,128)S(1)}, u32[]{:S(2)}) copy-start(f32[16,8,1152]{2,1,0:T(8,128)S(1)} %all-to-all-done.1) | copy-start | bytes 1769476
  136.6 17.1 %all-to-all-start.2 = ((f32[16,8,896]{2,1,0:T(8,128)}), f32[16,8,896]{2,1,0:T(8,128)S(1)}, u32[]{:S(2)}, u32[]{:S(2)}) async-start(f32[16,8,896]{2,1,0:T(8,128)} %broadcast_in_dim.11), calls=%async_computation.2 | async-start | bytes 917504 | tf_op jit(solution)/shard_map/all_to_all | solution.py:323
  141.0 18.3 %collective-permute-start.7 = (f32[16,8,1152]{2,1,0:T(8,128)S(1)}, f32[16,8,1152]{2,1,0:T(8,128)S(1)}, u32[]{:S(2)}, u32[]{:S(2)}) collective-permute-start(f32[16,8,1152]{2,1,0:T(8,128)S(1)} %all-to-all-done.1), channel_id=1, source_target_pairs={{0,1},{1,0},{2,3},{3,2},{4,5},{5,4},{6,7},{7,6},{8,9},{9,8},{10,11... | collective-permute-start | bytes 1769480 | tf_op jit(solution)/shard_map/ppermute | solution.py:318
  153.7 5.7 %copy-start.1 = (f32[16,8,896]{2,1,0:T(8,128)}, f32[16,8,896]{2,1,0:T(8,128)S(1)}, u32[]{:S(2)}) copy-start(f32[16,8,896]{2,1,0:T(8,128)S(1)} %all-to-all-done.2) | copy-start | bytes 1376260
  153.7 5.6 %collective-permute-start.12 = (f32[16,8,896]{2,1,0:T(8,128)S(1)}, f32[16,8,896]{2,1,0:T(8,128)S(1)}, u32[]{:S(2)}, u32[]{:S(2)}) collective-permute-start(f32[16,8,896]{2,1,0:T(8,128)S(1)} %all-to-all-done.2), channel_id=1, source_target_pairs={{0,1},{1,0},{2,3},{3,2},{4,5},{5,4},{6,7},{7,6},{8,9},{9,8},{10,11... | collective-permute-start | bytes 1376264 | tf_op jit(solution)/shard_map/ppermute | solution.py:318
  159.4 1.0 copy-start.2
  (3 other events, 2.4 us)

commit v3 on v2

v3 whole, which is shorter than its diff:
```python
import jax
import jax.numpy as jnp
from jax import lax
from jax.experimental import pallas as pl
from jax.experimental.pallas import tpu as pltpu
from jax.sharding import PartitionSpec as P

F32 = jnp.float32
BF16 = jnp.bfloat16
ROWS = 256
KS = 512
BLOCKS = 8
GROUP = 8
PAIRS = GROUP // 2
GROUPS = ROWS // GROUP


def block_at(y, x):
    return (y % 2) * 4 + x % 4


def partner_tables():
    first, second, third, fourth = [], [], [], []
    for b in range(BLOCKS):
        y, x = b // 4, b % 4
        first.append(block_at(y, x + 1))
        second.append(block_at(y + 1, x + 3))
        cycle = {(0, 0): (0, 2), (0, 1): (1, 2), (1, 1): (1, 0), (1, 0): (0, 0)}
        ny, nx = cycle[(y, x // 2)]
        third.append(block_at(ny, nx + x % 2))
        fourth.append(block_at(y + 1, x + 2))
    return [first, second, third, fourth]


PARTNERS = partner_tables()
OWNERS = [[table.index(b) for b in range(BLOCKS)] for table in PARTNERS]


def params():
    return pltpu.CompilerParams(vmem_limit_bytes=24 << 20)


def in_vmem(n):
    return [pl.BlockSpec(memory_space=pltpu.VMEM)] * n


def branch_sums(ref, lane):
    def add(k8, total):
        at = pl.ds(pl.multiple_of(k8 * 8, 8), 8)
        return total + ref[at, lane : lane + 128]

    total = lax.fori_loop(0, KS // 8, add, jnp.zeros((8, 128), F32), unroll=8)
    return jnp.sum(total, axis=0, keepdims=True)


def weigh_kernel(counts_ref, totals_ref, lengths_ref, wt_ref, split_ref, row_ref, col_ref):
    scaled = lengths_ref[...].astype(F32) * 0.001
    wt = (scaled * counts_ref[...].astype(F32)).T / totals_ref[...].astype(F32)
    wt_ref[...] = wt
    for n in range(8):
        x = wt[:, n * 32 : (n + 1) * 32]
        high = x.astype(BF16)
        rest = x - high.astype(F32)
        middle = rest.astype(BF16)
        low = (rest - middle.astype(F32)).astype(BF16)
        split_ref[n] = jnp.concatenate([high, middle, low, jnp.zeros_like(low)], axis=1)
    for h in range(2):
        sums = branch_sums(wt_ref, h * 128)
        row_ref[:, h * 128 : (h + 1) * 128] = jnp.broadcast_to(sums, (8, 128))
        col_ref[h * 128 : (h + 1) * 128, :] = jnp.broadcast_to(sums, (128, 128)).T


def weigh(counts, totals, lengths):
    return pl.pallas_call(
        weigh_kernel,
        out_shape=(
            jax.ShapeDtypeStruct((KS, ROWS), F32),
            jax.ShapeDtypeStruct((8, KS, 128), BF16),
            jax.ShapeDtypeStruct((8, ROWS), F32),
            jax.ShapeDtypeStruct((ROWS, 128), F32),
        ),
        compiler_params=params(),
        name="weigh",
    )(counts, totals.reshape(1, ROWS), lengths.reshape(1, KS))


def spread_call(name, n_blocks, columns, width, group, mass_row, side=None):
    pairs = group // 2
    halves = 2 if side is None else 1
    groups = halves * ROWS // 2 // group

    def kernel(split_ref, col_ref, *refs):
        blocks = refs[:n_blocks]
        out_ref, pick_ref, even_ref, odd_ref = refs[n_blocks:]
        core = lax.axis_index("branch") % 2
        y = lax.axis_index("blk") // 4
        if side is None:
            base = 0
        else:
            base = (core if side == 0 else 1 - core) * groups

        part = lax.broadcasted_iota(jnp.int32, (128, 256), 0)
        lane = lax.broadcasted_iota(jnp.int32, (128, 256), 1)
        want = jnp.where(part < 96, part % 32 - lane // 128, -1)
        for p in range(16):
            pick_ref[p] = jnp.where(want == 2 * p, 1.0, 0.0).astype(BF16)

        def broadcast_pair(into, g, q, at=slice(0, KS)):
            pair = g * pairs + q
            into[q, at] = jnp.dot(
                split_ref[pair // 16, at], pick_ref[pair % 16], preferred_element_type=F32
            )

        def span(n, lane, at):
            if isinstance(lane, int):
                return blocks[n][at, lane : lane + 128]
            return blocks[n][at, pl.ds(pl.multiple_of(lane, 128), 128)]

        def columns_at(h):
            return columns(h if side is None else base // groups, y)

        for h in range(halves):
            below = [jnp.zeros((1, 128), F32)] * mass_row
            for n, lane in columns_at(h):
                total = jnp.zeros((8, 128), F32)
                for k8 in range(KS // 8):
                    total = total + span(n, lane, slice(k8 * 8, k8 * 8 + 8))
                below.append(jnp.sum(total, axis=0, keepdims=True))
            below += [jnp.zeros((1, 128), F32)] * (8 - len(below))
            out_ref[h, 128:136, 0:128] = jnp.concatenate(below, axis=0)

        for q in range(pairs):
            broadcast_pair(even_ref, base, q)

        def one_group(g, now, later):
            h = g * group // 128
            cols = columns_at(h)
            n_cols = len(cols)
            following = base + jnp.minimum(g + 1, groups - 1)
            steps = []
            if group == 8:
                for q in range(pairs):
                    broadcast_pair(later, following, q)
            else:
                steps = [(q, slice(k, k + 128)) for k in range(0, KS, 128) for q in range(pairs)]
            acc = [jnp.zeros((8, 128), F32)] * (group * n_cols)
            for k8 in range(KS // 8):
                if steps and k8 % 2 == 0:
                    q, at = steps[k8 // 2]
                    broadcast_pair(later, following, q, at)
                at = slice(k8 * 8, k8 * 8 + 8)
                spans = [span(n, lane, at) for n, lane in cols]
                for r in range(group):
                    own = now[r // 2, at, 128 * (r % 2) : 128 * (r % 2) + 128]
                    for j in range(n_cols):
                        acc[r * n_cols + j] += jnp.minimum(own, spans[j])
            for r0 in range(0, group, 8):
                row = pl.multiple_of(g * group + r0 - h * 128, 8)
                first = pl.multiple_of((base + g) * group + r0, 8)
                own_mass = col_ref[pl.ds(first, 8), :]
                for j in range(n_cols):
                    mass = out_ref[h, 128 + mass_row + j : 129 + mass_row + j, 0:128]
                    least = jnp.concatenate(
                        [
                            jnp.sum(acc[(r0 + r) * n_cols + j], axis=0, keepdims=True)
                            for r in range(8)
                        ],
                        axis=0,
                    )
                    out_ref[h, pl.ds(row, 8), 128 * j : 128 * j + 128] = (
                        own_mass + mass - 2.0 * least
                    )

        def two_groups(t, carry):
            one_group(2 * t, even_ref, odd_ref)
            one_group(2 * t + 1, odd_ref, even_ref)
            return carry

        lax.fori_loop(0, groups // 2, two_groups, 0)

    def call(split, col, *blocks):
        return pl.pallas_call(
            kernel,
            out_shape=jax.ShapeDtypeStruct((halves, 136, width), F32),
            in_specs=in_vmem(2 + n_blocks),
            out_specs=in_vmem(1)[0],
            scratch_shapes=[
                pltpu.VMEM((16, 128, 256), BF16),
                pltpu.VMEM((pairs, KS, 256), F32),
                pltpu.VMEM((pairs, KS, 256), F32),
            ],
            compiler_params=params(),
            cost_estimate=pl.CostEstimate(
                flops=halves * width * 128 * KS * 250, bytes_accessed=4 << 20, transcendentals=0
            ),
            name=name,
        )(split, col, *blocks)

    return call


def diagonal_columns(half, y):
    return [(0, 0), (0, 128)]


def first_columns(half, y):
    return [(0, 0), (0, 128), (1, 0), (1, 128)]


def second_columns(half, y):
    return [(0, 0), (0, 128), (1, (half ^ y) * 128)]


def pack_kernel(*refs):
    out_ref = refs[-1]
    core = lax.axis_index("branch") % 2
    lane = 0
    masses = jnp.zeros((8, 128), F32)
    for own, got in zip(refs[:-1:2], refs[1:-1:2], strict=True):
        half = core if own.shape[0] == 2 else 0
        width = own.shape[2]
        both = own[half, 0:128, :] + got[half, 0:128, :]
        out_ref[:, :, lane : lane + width] = both.reshape(16, 8, width)
        masses = masses + own[half, 128:136, 0:128] + got[half, 128:136, 0:128]
        lane += width
    out_ref[:, :, lane:] = jnp.broadcast_to(masses[None], (16, 8, 128))


def pack(*parts):
    width = sum(p.shape[2] for p in parts[::2]) + 128
    return pl.pallas_call(
        pack_kernel,
        out_shape=jax.ShapeDtypeStruct((16, 8, width), F32),
        in_specs=in_vmem(len(parts)),
        out_specs=in_vmem(1)[0],
        compiler_params=params(),
        name="pack",
    )(*parts)


def block_partner(b, slot):
    y, x = b // 4, b % 4
    if slot == 0:
        return b
    if slot == 1:
        return y * 4 + (x + 1) % 4
    if slot == 2:
        return (1 - y) * 4 + (x + 3) % 4
    if slot == 4:
        return (1 - y) * 4 + (x + 2) % 4
    if slot == 5:
        return y * 4 + (x + 3) % 4
    if slot == 6:
        return (1 - y) * 4 + (x + 1) % 4
    far = x // 2
    keep_y = (far == y) if slot == 3 else (far != y)
    return jnp.where(keep_y, y * 4 + (x + 2) % 4, (1 - y) * 4 + x)


def assemble_kernel(own1, other1, own2, other2, out_ref, turned_ref, sems):
    core = lax.axis_index("branch") % 2
    b = lax.axis_index("blk")
    y = b // 4
    stores = []

    def store(src, rows, cols):
        copy = pltpu.make_async_copy(src, out_ref.at[rows, cols], sems.at[len(stores)])
        copy.start()
        stores.append(copy)

    def rows_of(half):
        return pl.ds(pl.multiple_of(half * 128, 128), 128)

    def columns(slot, half=None):
        first = block_partner(b, slot) * ROWS
        if half is None:
            return pl.ds(pl.multiple_of(first, ROWS), ROWS)
        return pl.ds(pl.multiple_of(first + half * 128, 128), 128)

    both = ((0, core, own1, own2), (1, 1 - core, other1, other2))
    for _, half, ref1, ref2 in both:
        rows = rows_of(half)
        for slot, ref, lane in ((0, ref1, 0), (1, ref1, 256), (2, ref1, 512), (3, ref2, 0)):
            store(ref.at[:, lane : lane + ROWS], rows, columns(slot))
        store(ref2.at[:, 256:384], rows, columns(4, half ^ y))
    for side, half, ref1, ref2 in both:
        for n, (slot, ref, lane) in enumerate(((5, ref1, 768), (6, ref1, 1024), (7, ref2, 384))):
            turned_ref[side, n] = ref[:, lane : lane + ROWS].T
            store(turned_ref.at[side, n], slice(0, ROWS), columns(slot, half))
        turned_ref[side, 3, 0:128] = ref2[:, 640:768].T
        store(turned_ref.at[side, 3, 0:128], rows_of(half ^ (1 - y)), columns(4, half))
    for copy in stores:
        copy.wait()


def assemble(*pieces):
    return pl.pallas_call(
        assemble_kernel,
        out_shape=jax.ShapeDtypeStruct((ROWS, BLOCKS * ROWS), F32),
        in_specs=in_vmem(4),
        out_specs=pl.BlockSpec(memory_space=pl.ANY),
        scratch_shapes=[
            pltpu.VMEM((2, 4, ROWS, 128), F32),
            pltpu.SemaphoreType.DMA((18,)),
        ],
        compiler_params=params(),
        name="assemble",
    )(*[p.reshape(128, p.shape[2]) for p in pieces])


def on_device(counts, totals, lengths):
    branch = lax.axis_index("branch")
    place = branch // 2

    def from_partner(v, n):
        return lax.ppermute(v, "blk", [(PARTNERS[n][b], b) for b in range(BLOCKS)])

    def to_partner(v, n):
        return lax.ppermute(v, "blk", [(b, PARTNERS[n][b]) for b in range(BLOCKS)])

    def other_core(v):
        return lax.ppermute(v, "branch", [(i, i ^ 1) for i in range(32)])

    chips = [[2 * p + c for p in range(16)] for c in range(2)]

    def over_chips(v):
        return lax.all_to_all(v, "branch", 0, 0, axis_index_groups=chips)

    def gather(pieces):
        mine = jnp.concatenate(pieces, axis=1)
        whole = over_chips(jnp.broadcast_to(mine[None], (16, *mine.shape)))
        return whole, other_core(whole)

    def tied(v, *others):
        return lax.optimization_barrier((v, *others))[0]

    wt, split, mass_row, mass_col = weigh(counts, totals, lengths)
    got = [from_partner(wt, n) for n in range(2)]
    diagonal = spread_call("diagonal", 1, diagonal_columns, 256, 16, 0)
    first = [spread_call(f"first{s}", 2, first_columns, 512, 8, 2, s) for s in range(2)]
    second = [spread_call(f"second{s}", 2, second_columns, 384, 8, 0, s) for s in range(2)]

    part0 = diagonal(split, mass_col, wt)
    later = tied(wt, part0)
    got += [from_partner(later, n) for n in (2, 3)]
    received0 = other_core(part0)
    received1 = other_core(first[1](split, mass_col, got[0], got[1]))
    kept1 = first[0](split, mass_col, got[0], got[1])
    payload1 = pack(part0, received0, kept1, received1)
    shard = jnp.sum(over_chips(payload1), axis=0)

    third = tied(got[2], payload1)
    received2 = other_core(second[1](split, mass_col, third, got[3]))

    mass = shard[:, 768:]
    own_half = jnp.where(branch % 2 == 0, mass[0], mass[1])
    own_mass = lax.dynamic_slice_in_dim(own_half, place * 8, 8)[:, None]
    dist1 = shard[:, :768] / (own_mass + mass[0:6].reshape(768)[None, :])
    swapped1 = [to_partner(dist1[:, 256 * (n + 1) : 256 * (n + 2)], n) for n in range(2)]

    third = tied(third, dist1, received2)
    kept2 = second[0](split, mass_col, third, got[3])
    payload2 = pack(kept2, received2)
    shard = jnp.sum(over_chips(payload2), axis=0)
    dist2 = shard[:, :384] / (own_mass + shard[0:3, 384:].reshape(384)[None, :])
    swapped2 = [to_partner(dist2[:, 0:256], 2), to_partner(dist2[:, 256:384], 3)]

    own1, other1 = gather([tied(dist1, payload2), *swapped1])
    own2, other2 = gather([dist2, *swapped2])
    return assemble(own1, other1, own2, other2)


def solution(mesh):
    placed = (P("blk", "branch"), P("blk"), P("branch"))
    return jax.shard_map(
        on_device, mesh=mesh, in_specs=placed, out_specs=P("blk", None), check_vma=False
    )
```

time: 164 us -> 148 us (0.902)
  waiting for transfers between devices: 41.1 us -> 31.1 us
  Pallas kernels: 66.6 us -> 60.5 us
  starting transfers between devices: 44.8 us -> 50.7 us
  local copies, waits for them, and re-layouts: 9.35 us -> 4.14 us
    all_to_all x3 -> x4, waiting for transfers between devices: 35 us -> 21.7 us  [over_chips(): return lax.all_to_all(v, 'branch', 0, 0, axis_index_groups=chips)]
    unnamed x26 -> x6, local copies, waits for them, and re-layouts: 6.93 us -> 2.4 us
    ppermute x4, waiting for transfers between devices: 3.72 us -> 8.01 us  [to_partner(): return lax.ppermute(v, 'blk', [(b, PARTNERS[n][b]) for b in range(BLOCKS)])]
    ppermute x5, starting transfers between devices: 9.03 us -> 12.8 us  [other_core(): return lax.ppermute(v, 'branch', [(i, i ^ 1) for i in range(32)])]
    all_to_all x3 -> x4, starting transfers between devices: 17.8 us -> 21.4 us  [over_chips(): return lax.all_to_all(v, 'branch', 0, 0, axis_index_groups=chips)]
    pallas_call x3 -> x7, Pallas kernels: 60.3 us -> 57.3 us  [the longest x5 55.8 us: call(): pl.pallas_call(kernel, out_shape=jax.ShapeDtypeStruct((halves, 136, width...]
  transfers between devices with their start and end apart: 16 -> 17, of which waited for: 6 -> 8; matrix products, arithmetic and copies ran while one was open for 1% -> 0% of each run, Pallas kernels for 37% -> 32%
where the time goes in v3:
time: 148 us; the launch traced here: 147 us
  Pallas kernels  60.5 us (41%)
  starting transfers between devices  50.7 us (34%)
  waiting for transfers between devices  31.1 us (21%)
  local copies, waits for them, and re-layouts  4.14 us (3%)
    pallas_call x5, Pallas kernels, call(): pl.pallas_call(kernel, out_shape=jax.ShapeDtypeStruct((halves, 136, width...  55.8 us
    all_to_all x4, waiting for transfers between devices, over_chips(): return lax.all_to_all(v, 'branch', 0, 0, axis_index_groups=chips)  21.7 us
    all_to_all x4, starting transfers between devices, over_chips(): return lax.all_to_all(v, 'branch', 0, 0, axis_index_groups=chips)  21.4 us
    ppermute x5, starting transfers between devices, other_core(): return lax.ppermute(v, 'branch', [(i, i ^ 1) for i in range(32)])  12.8 us
    ppermute x4, starting transfers between devices, from_partner(): return lax.ppermute(v, 'blk', [(PARTNERS[n][b], b) for b in range(BLOCKS)])  10.4 us
    ppermute x4, waiting for transfers between devices, to_partner(): return lax.ppermute(v, 'blk', [(b, PARTNERS[n][b]) for b in range(BLOCKS)])  8.01 us
    ppermute x4, starting transfers between devices, to_partner(): return lax.ppermute(v, 'blk', [(b, PARTNERS[n][b]) for b in range(BLOCKS)])  6.2 us
  transfers between devices with their start and end apart: 17, of which 8 were waited for; matrix products, arithmetic and copies ran while one was open for 0% of the time, Pallas kernels for 32%

profile of v3, /device:TPU:1, one launch (start us, length us, event | category | flops | bytes accessed | tf_op | source)
XLA Modules:
  0.0 147.0 jit_solution(7699073964169165815)
XLA Ops:
  2.4 1.7 %weigh.1 = (f32[512,256]{1,0:T(8,128)S(1)}, bf16[8,512,128]{2,1,0:T(8,128)(2,1)S(1)}, f32[8,256]{1,0:T(8,128)}, f32[256,128]{1,0:T(8,128)S(1)}) custom-call(s32[256,512]{1,0:T(8,128)S(1)} %copy-done, s32[1,256]{1,0:T(1,128)S(1)} %bitcast.17, s32[1,512]{1,0:T(1,128)S(1)} %bitcast.16), custom_call_target="tpu_custom_call" | custom-call | tf_op jit(solution)/shard_map/weigh/pallas_call | solution.py:74
  4.1 3.3 %collective-permute-start.1 = (f32[512,256]{1,0:T(8,128)S(1)}, f32[512,256]{1,0:T(8,128)S(1)}, u32[]{:S(2)}, u32[]{:S(2)}) collective-permute-start(f32[512,256]{1,0:T(8,128)S(1)} %get-tuple-element.15.refs_0_), channel_id=1, source_target_pairs={{32,0},{64,32},{96,64},{0,96},{160,128},{192,160},{224,192},{128,2... | collective-permute-start | bytes 1572872 | tf_op jit(solution)/shard_map/ppermute | solution.py:316
  7.5 1.6 %collective-permute-start.2 = (f32[512,256]{1,0:T(8,128)S(1)}, f32[512,256]{1,0:T(8,128)S(1)}, u32[]{:S(2)}, u32[]{:S(2)}) collective-permute-start(f32[512,256]{1,0:T(8,128)S(1)} %get-tuple-element.15.refs_0_), channel_id=1, source_target_pairs={{224,0},{128,32},{160,64},{192,96},{96,128},{0,160},{32,192},{64,2... | collective-permute-start | bytes 1572872 | tf_op jit(solution)/shard_map/ppermute | solution.py:316
  9.1 13.4 %diagonal.1.refs_0_ = f32[2,136,256]{2,1,0:T(8,128)S(1)} custom-call(bf16[8,512,128]{2,1,0:T(8,128)(2,1)S(1)} %get-tuple-element.12.split_ref, f32[256,128]{1,0:T(8,128)S(1)} %get-tuple-element.13.col_ref, f32[512,256]{1,0:T(8,128)S(1)} %get-tuple-element.15.refs_0_), custom_call_target="tpu_custom_call" | custom-call | flops 8388608000 | bytes 4194304 | tf_op jit(solution)/shard_map/diagonal/pallas_call | solution.py:182
  23.8 1.8 %collective-permute-start.4 = (f32[512,256]{1,0:T(8,128)S(1)}, f32[512,256]{1,0:T(8,128)S(1)}, u32[]{:S(2)}, u32[]{:S(2)}) collective-permute-start(f32[512,256]{1,0:T(8,128)S(1)} %get-tuple-element.15.refs_0_), channel_id=1, source_target_pairs={{64,0},{96,32},{192,64},{224,96},{0,128},{32,160},{128,192},{160,2... | collective-permute-start | bytes 1572872 | tf_op jit(solution)/shard_map/ppermute | solution.py:316
  25.6 3.6 %collective-permute-start.5 = (f32[512,256]{1,0:T(8,128)S(1)}, f32[512,256]{1,0:T(8,128)S(1)}, u32[]{:S(2)}, u32[]{:S(2)}) collective-permute-start(f32[512,256]{1,0:T(8,128)S(1)} %get-tuple-element.15.refs_0_), channel_id=1, source_target_pairs={{192,0},{224,32},{128,64},{160,96},{64,128},{96,160},{0,192},{32,2... | collective-permute-start | bytes 1572872 | tf_op jit(solution)/shard_map/ppermute | solution.py:316
  29.2 11.3 %first1.1 = f32[1,136,512]{2,1,0:T(8,128)S(1)} custom-call(bf16[8,512,128]{2,1,0:T(8,128)(2,1)S(1)} %get-tuple-element.12.split_ref, f32[256,128]{1,0:T(8,128)S(1)} %get-tuple-element.13.col_ref, f32[512,256]{1,0:T(8,128)S(1)} %collective-permute-done.1.refs_0_, f32[512,256]{1,0:T(8,128)S(1)} %collective-permute-done.2.refs_1_), custom_call_target="tpu_custom_call" | custom-call | flops 8388608000 | bytes 4194304 | tf_op jit(solution)/shard_map/first1/pallas_call | solution.py:182
  41.3 11.3 %first0.1.refs_2_ = f32[1,136,512]{2,1,0:T(8,128)S(1)} custom-call(bf16[8,512,128]{2,1,0:T(8,128)(2,1)S(1)} %get-tuple-element.12.split_ref, f32[256,128]{1,0:T(8,128)S(1)} %get-tuple-element.13.col_ref, f32[512,256]{1,0:T(8,128)S(1)} %collective-permute-done.1.refs_0_, f32[512,256]{1,0:T(8,128)S(1)} %collective-permute-done.2.refs_1_), custom_call_target="tpu_custom_call" | custom-call | flops 8388608000 | bytes 4194304 | tf_op jit(solution)/shard_map/first0/pallas_call | solution.py:182
  53.5 8.4 %all-to-all-start = ((f32[16,8,896]{2,1,0:T(8,128)}), f32[16,8,896]{2,1,0:T(8,128)S(1)}, u32[]{:S(2)}, u32[]{:S(2)}) async-start(f32[16,8,896]{2,1,0:T(8,128)} %pack.2), calls=%async_computation | async-start | bytes 917504 | tf_op jit(solution)/shard_map/all_to_all | solution.py:327
  62.0 9.8 %second1.1 = f32[1,136,384]{2,1,0:T(8,128)S(1)} custom-call(bf16[8,512,128]{2,1,0:T(8,128)(2,1)S(1)} %get-tuple-element.12.split_ref, f32[256,128]{1,0:T(8,128)S(1)} %get-tuple-element.13.col_ref, f32[512,256]{1,0:T(8,128)S(1)} %collective-permute-done.4.refs_0_, f32[512,256]{1,0:T(8,128)S(1)} %collective-permute-done.5.refs_1_), custom_call_target="tpu_custom_call" | custom-call | flops 6291456000 | bytes 4194304 | tf_op jit(solution)/shard_map/second1/pallas_call | solution.py:182
  72.3 4.8 %all-to-all-done = f32[16,8,896]{2,1,0:T(8,128)S(1)} async-done(((f32[16,8,896]{2,1,0:T(8,128)}), f32[16,8,896]{2,1,0:T(8,128)S(1)}, u32[]{:S(2)}, u32[]{:S(2)}) %all-to-all-start) | async-done | bytes 458784 | tf_op jit(solution)/shard_map/all_to_all | solution.py:327
  77.3 9.9 %second0.1.refs_0_ = f32[1,136,384]{2,1,0:T(8,128)S(1)} custom-call(bf16[8,512,128]{2,1,0:T(8,128)(2,1)S(1)} %get-tuple-element.12.split_ref, f32[256,128]{1,0:T(8,128)S(1)} %get-tuple-element.13.col_ref, f32[512,256]{1,0:T(8,128)S(1)} %collective-permute-done.4.refs_0_, f32[512,256]{1,0:T(8,128)S(1)} %collective-permute-done.5.refs_1_), custom_call_target="tpu_custom_call" | custom-call | flops 6291456000 | bytes 4194304 | tf_op jit(solution)/shard_map/second0/pallas_call | solution.py:182
  87.9 3.9 %all-to-all-start.2 = ((f32[16,8,512]{2,1,0:T(8,128)}), f32[16,8,512]{2,1,0:T(8,128)S(1)}, u32[]{:S(2)}, u32[]{:S(2)}) async-start(f32[16,8,512]{2,1,0:T(8,128)} %pack.3), calls=%async_computation.2 | async-start | bytes 524288 | tf_op jit(solution)/shard_map/all_to_all | solution.py:327
  93.4 1.6 %collective-permute-start.8 = (f32[8,256]{1,0:T(8,128)S(1)}, f32[8,256]{1,0:T(8,128)S(1)}, u32[]{:S(2)}, u32[]{:S(2)}) collective-permute-start(f32[8,256]{1,0:T(8,128)S(1)} %get-tuple-element.20), channel_id=1, source_target_pairs={{0,224},{32,128},{64,160},{96,192},{128,96},{160,0},{192,32},{224,... | collective-permute-start | bytes 24584 | tf_op jit(solution)/shard_map/ppermute | solution.py:319
  95.6 2.7 %collective-permute-done.8 = f32[8,256]{1,0:T(8,128)S(1)} collective-permute-done((f32[8,256]{1,0:T(8,128)S(1)}, f32[8,256]{1,0:T(8,128)S(1)}, u32[]{:S(2)}, u32[]{:S(2)}) %collective-permute-start.8) | collective-permute-done | bytes 8224 | tf_op jit(solution)/shard_map/ppermute | solution.py:319
  98.3 3.2 %all-to-all-done.2 = f32[16,8,512]{2,1,0:T(8,128)S(1)} async-done(((f32[16,8,512]{2,1,0:T(8,128)}), f32[16,8,512]{2,1,0:T(8,128)S(1)}, u32[]{:S(2)}, u32[]{:S(2)}) %all-to-all-start.2) | async-done | bytes 262176 | tf_op jit(solution)/shard_map/all_to_all | solution.py:327
  102.4 4.6 %all-to-all-start.1 = ((f32[16,8,1280]{2,1,0:T(8,128)}), f32[16,8,1280]{2,1,0:T(8,128)S(1)}, u32[]{:S(2)}, u32[]{:S(2)}) async-start(f32[16,8,1280]{2,1,0:T(8,128)} %broadcast_in_dim.4), calls=%async_computation.1 | async-start | bytes 1310720 | tf_op jit(solution)/shard_map/all_to_all | solution.py:327
  108.5 1.7 %collective-permute-start.11 = (f32[8,128]{1,0:T(8,128)S(1)}, f32[8,128]{1,0:T(8,128)S(1)}, u32[]{:S(2)}, u32[]{:S(2)}) collective-permute-start(f32[8,128]{1,0:T(8,128)S(1)} %slice.53), channel_id=1, source_target_pairs={{0,192},{32,224},{64,128},{96,160},{128,64},{160,96},{192,0},{224,... | collective-permute-start | bytes 12296 | tf_op jit(solution)/shard_map/ppermute | solution.py:319
  110.2 4.7 %collective-permute-done.11 = f32[8,128]{1,0:T(8,128)S(1)} collective-permute-done((f32[8,128]{1,0:T(8,128)S(1)}, f32[8,128]{1,0:T(8,128)S(1)}, u32[]{:S(2)}, u32[]{:S(2)}) %collective-permute-start.11) | collective-permute-done | bytes 4128 | tf_op jit(solution)/shard_map/ppermute | solution.py:319
  114.9 7.5 %all-to-all-done.1 = f32[16,8,1280]{2,1,0:T(8,128)S(1)} async-done(((f32[16,8,1280]{2,1,0:T(8,128)}), f32[16,8,1280]{2,1,0:T(8,128)S(1)}, u32[]{:S(2)}, u32[]{:S(2)}) %all-to-all-start.1) | async-done | bytes 655392 | tf_op jit(solution)/shard_map/all_to_all | solution.py:327
  123.1 4.4 %all-to-all-start.3 = ((f32[16,8,768]{2,1,0:T(8,128)}), f32[16,8,768]{2,1,0:T(8,128)S(1)}, u32[]{:S(2)}, u32[]{:S(2)}) async-start(f32[16,8,768]{2,1,0:T(8,128)} %broadcast_in_dim.5), calls=%async_computation.3 | async-start | bytes 786432 | tf_op jit(solution)/shard_map/all_to_all | solution.py:327
  127.6 4.6 %collective-permute-start.9 = (f32[16,8,1280]{2,1,0:T(8,128)S(1)}, f32[16,8,1280]{2,1,0:T(8,128)S(1)}, u32[]{:S(2)}, u32[]{:S(2)}) collective-permute-start(f32[16,8,1280]{2,1,0:T(8,128)S(1)} %all-to-all-done.1), channel_id=1, source_target_pairs={{0,1},{1,0},{2,3},{3,2},{4,5},{5,4},{6,7},{7,6},{8,9},{9,8},{10,11... | collective-permute-start | bytes 1966088 | tf_op jit(solution)/shard_map/ppermute | solution.py:322
  132.2 6.2 %all-to-all-done.3 = f32[16,8,768]{2,1,0:T(8,128)S(1)} async-done(((f32[16,8,768]{2,1,0:T(8,128)}), f32[16,8,768]{2,1,0:T(8,128)S(1)}, u32[]{:S(2)}, u32[]{:S(2)}) %all-to-all-start.3) | async-done | bytes 393248 | tf_op jit(solution)/shard_map/all_to_all | solution.py:327
  138.5 5.6 %collective-permute-start.12 = (f32[16,8,768]{2,1,0:T(8,128)S(1)}, f32[16,8,768]{2,1,0:T(8,128)S(1)}, u32[]{:S(2)}, u32[]{:S(2)}) collective-permute-start(f32[16,8,768]{2,1,0:T(8,128)S(1)} %all-to-all-done.3), channel_id=1, source_target_pairs={{0,1},{1,0},{2,3},{3,2},{4,5},{5,4},{6,7},{7,6},{8,9},{9,8},{10,11... | collective-permute-start | bytes 1179656 | tf_op jit(solution)/shard_map/ppermute | solution.py:322
  (40 shorter events, 14.8 us)
Async XLA Ops:
  0.0 1.0 copy-start
  1.0 0.7 copy-start.1
  1.7 0.7 copy-start.2
  4.1 25.1 %collective-permute-start.1 = (f32[512,256]{1,0:T(8,128)S(1)}, f32[512,256]{1,0:T(8,128)S(1)}, u32[]{:S(2)}, u32[]{:S(2)}) collective-permute-start(f32[512,256]{1,0:T(8,128)S(1)} %get-tuple-element.15.refs_0_), channel_id=1, source_target_pairs={{32,0},{64,32},{96,64},{0,96},{160,128},{192,160},{224,192},{128,2... | collective-permute-start | bytes 1572872 | tf_op jit(solution)/shard_map/ppermute | solution.py:316
  7.5 21.8 %collective-permute-start.2 = (f32[512,256]{1,0:T(8,128)S(1)}, f32[512,256]{1,0:T(8,128)S(1)}, u32[]{:S(2)}, u32[]{:S(2)}) collective-permute-start(f32[512,256]{1,0:T(8,128)S(1)} %get-tuple-element.15.refs_0_), channel_id=1, source_target_pairs={{224,0},{128,32},{160,64},{192,96},{96,128},{0,160},{32,192},{64,2... | collective-permute-start | bytes 1572872 | tf_op jit(solution)/shard_map/ppermute | solution.py:316
  22.5 30.2 %collective-permute-start = (f32[2,136,256]{2,1,0:T(8,128)S(1)}, f32[2,136,256]{2,1,0:T(8,128)S(1)}, u32[]{:S(2)}, u32[]{:S(2)}) collective-permute-start(f32[2,136,256]{2,1,0:T(8,128)S(1)} %diagonal.1.refs_0_), channel_id=1, source_target_pairs={{0,1},{1,0},{2,3},{3,2},{4,5},{5,4},{6,7},{7,6},{8,9},{9,8},{10,11... | collective-permute-start | bytes 835592 | tf_op jit(solution)/shard_map/ppermute | solution.py:322
  23.8 38.2 %collective-permute-start.4 = (f32[512,256]{1,0:T(8,128)S(1)}, f32[512,256]{1,0:T(8,128)S(1)}, u32[]{:S(2)}, u32[]{:S(2)}) collective-permute-start(f32[512,256]{1,0:T(8,128)S(1)} %get-tuple-element.15.refs_0_), channel_id=1, source_target_pairs={{64,0},{96,32},{192,64},{224,96},{0,128},{32,160},{128,192},{160,2... | collective-permute-start | bytes 1572872 | tf_op jit(solution)/shard_map/ppermute | solution.py:316
  25.6 36.4 %collective-permute-start.5 = (f32[512,256]{1,0:T(8,128)S(1)}, f32[512,256]{1,0:T(8,128)S(1)}, u32[]{:S(2)}, u32[]{:S(2)}) collective-permute-start(f32[512,256]{1,0:T(8,128)S(1)} %get-tuple-element.15.refs_0_), channel_id=1, source_target_pairs={{192,0},{224,32},{128,64},{160,96},{64,128},{96,160},{0,192},{32,2... | collective-permute-start | bytes 1572872 | tf_op jit(solution)/shard_map/ppermute | solution.py:316
  40.6 12.1 %collective-permute-start.3 = (f32[1,136,512]{2,1,0:T(8,128)S(1)}, f32[1,136,512]{2,1,0:T(8,128)S(1)}, u32[]{:S(2)}, u32[]{:S(2)}) collective-permute-start(f32[1,136,512]{2,1,0:T(8,128)S(1)} %first1.1), channel_id=1, source_target_pairs={{0,1},{1,0},{2,3},{3,2},{4,5},{5,4},{6,7},{7,6},{8,9},{9,8},{10,11... | collective-permute-start | bytes 835592 | tf_op jit(solution)/shard_map/ppermute | solution.py:322
  53.5 23.5 %all-to-all-start = ((f32[16,8,896]{2,1,0:T(8,128)}), f32[16,8,896]{2,1,0:T(8,128)S(1)}, u32[]{:S(2)}, u32[]{:S(2)}) async-start(f32[16,8,896]{2,1,0:T(8,128)} %pack.2), calls=%async_computation | async-start | bytes 917504 | tf_op jit(solution)/shard_map/all_to_all | solution.py:327
  71.8 5.5 %collective-permute-start.6 = (f32[1,136,384]{2,1,0:T(8,128)S(1)}, f32[1,136,384]{2,1,0:T(8,128)S(1)}, u32[]{:S(2)}, u32[]{:S(2)}) collective-permute-start(f32[1,136,384]{2,1,0:T(8,128)S(1)} %second1.1), channel_id=1, source_target_pairs={{0,1},{1,0},{2,3},{3,2},{4,5},{5,4},{6,7},{7,6},{8,9},{9,8},{10,11... | collective-permute-start | bytes 626696 | tf_op jit(solution)/shard_map/ppermute | solution.py:322
  87.9 13.7 %all-to-all-start.2 = ((f32[16,8,512]{2,1,0:T(8,128)}), f32[16,8,512]{2,1,0:T(8,128)S(1)}, u32[]{:S(2)}, u32[]{:S(2)}) async-start(f32[16,8,512]{2,1,0:T(8,128)} %pack.3), calls=%async_computation.2 | async-start | bytes 524288 | tf_op jit(solution)/shard_map/all_to_all | solution.py:327
  91.8 3.8 %collective-permute-start.7 = (f32[8,256]{1,0:T(8,128)S(1)}, f32[8,256]{1,0:T(8,128)S(1)}, u32[]{:S(2)}, u32[]{:S(2)}) collective-permute-start(f32[8,256]{1,0:T(8,128)S(1)} %get-tuple-element.19), channel_id=1, source_target_pairs={{0,32},{32,64},{64,96},{96,0},{128,160},{160,192},{192,224},{224,1... | collective-permute-start | bytes 24584 | tf_op jit(solution)/shard_map/ppermute | solution.py:319
  93.4 4.9 %collective-permute-start.8 = (f32[8,256]{1,0:T(8,128)S(1)}, f32[8,256]{1,0:T(8,128)S(1)}, u32[]{:S(2)}, u32[]{:S(2)}) collective-permute-start(f32[8,256]{1,0:T(8,128)S(1)} %get-tuple-element.20), channel_id=1, source_target_pairs={{0,224},{32,128},{64,160},{96,192},{128,96},{160,0},{192,32},{224,... | collective-permute-start | bytes 24584 | tf_op jit(solution)/shard_map/ppermute | solution.py:319
  102.4 20.0 %all-to-all-start.1 = ((f32[16,8,1280]{2,1,0:T(8,128)}), f32[16,8,1280]{2,1,0:T(8,128)S(1)}, u32[]{:S(2)}, u32[]{:S(2)}) async-start(f32[16,8,1280]{2,1,0:T(8,128)} %broadcast_in_dim.4), calls=%async_computation.1 | async-start | bytes 1310720 | tf_op jit(solution)/shard_map/all_to_all | solution.py:327
  107.2 7.7 %collective-permute-start.10 = (f32[8,256]{1,0:T(8,128)S(1)}, f32[8,256]{1,0:T(8,128)S(1)}, u32[]{:S(2)}, u32[]{:S(2)}) collective-permute-start(f32[8,256]{1,0:T(8,128)S(1)} %slice.52), channel_id=1, source_target_pairs={{0,64},{32,96},{64,192},{96,224},{128,0},{160,32},{192,128},{224,1... | collective-permute-start | bytes 24584 | tf_op jit(solution)/shard_map/ppermute | solution.py:319
  108.5 6.4 %collective-permute-start.11 = (f32[8,128]{1,0:T(8,128)S(1)}, f32[8,128]{1,0:T(8,128)S(1)}, u32[]{:S(2)}, u32[]{:S(2)}) collective-permute-start(f32[8,128]{1,0:T(8,128)S(1)} %slice.53), channel_id=1, source_target_pairs={{0,192},{32,224},{64,128},{96,160},{128,64},{160,96},{192,0},{224,... | collective-permute-start | bytes 12296 | tf_op jit(solution)/shard_map/ppermute | solution.py:319
  123.1 15.3 %all-to-all-start.3 = ((f32[16,8,768]{2,1,0:T(8,128)}), f32[16,8,768]{2,1,0:T(8,128)S(1)}, u32[]{:S(2)}, u32[]{:S(2)}) async-start(f32[16,8,768]{2,1,0:T(8,128)} %broadcast_in_dim.5), calls=%async_computation.3 | async-start | bytes 786432 | tf_op jit(solution)/shard_map/all_to_all | solution.py:327
  127.6 17.8 %collective-permute-start.9 = (f32[16,8,1280]{2,1,0:T(8,128)S(1)}, f32[16,8,1280]{2,1,0:T(8,128)S(1)}, u32[]{:S(2)}, u32[]{:S(2)}) collective-permute-start(f32[16,8,1280]{2,1,0:T(8,128)S(1)} %all-to-all-done.1), channel_id=1, source_target_pairs={{0,1},{1,0},{2,3},{3,2},{4,5},{5,4},{6,7},{7,6},{8,9},{9,8},{10,11... | collective-permute-start | bytes 1966088 | tf_op jit(solution)/shard_map/ppermute | solution.py:322
  138.5 6.9 %collective-permute-start.12 = (f32[16,8,768]{2,1,0:T(8,128)S(1)}, f32[16,8,768]{2,1,0:T(8,128)S(1)}, u32[]{:S(2)}, u32[]{:S(2)}) collective-permute-start(f32[16,8,768]{2,1,0:T(8,128)S(1)} %all-to-all-done.3), channel_id=1, source_target_pairs={{0,1},{1,0},{2,3},{3,2},{4,5},{5,4},{6,7},{7,6},{8,9},{9,8},{10,11... | collective-permute-start | bytes 1179656 | tf_op jit(solution)/shard_map/ppermute | solution.py:322

commit v4 on v3

--- a/solution.py
+++ b/solution.py
@@ -53,7 +53,18 @@
     return jnp.sum(total, axis=0, keepdims=True)
 
 
-def weigh_kernel(counts_ref, totals_ref, lengths_ref, wt_ref, split_ref, row_ref, col_ref):
+def weigh_kernel(counts_hbm, totals_hbm, lengths_hbm, wt_ref, split_ref, col_ref, *scratch):
+    counts_ref, totals_ref, lengths_ref, sems = scratch
+    loads = [
+        pltpu.make_async_copy(src, dst, sems.at[n])
+        for n, (src, dst) in enumerate(
+            ((counts_hbm, counts_ref), (totals_hbm, totals_ref), (lengths_hbm, lengths_ref))
+        )
+    ]
+    for load in loads:
+        load.start()
+    for load in loads:
+        load.wait()
     scaled = lengths_ref[...].astype(F32) * 0.001
     wt = (scaled * counts_ref[...].astype(F32)).T / totals_ref[...].astype(F32)
     wt_ref[...] = wt
@@ -66,7 +77,6 @@
         split_ref[n] = jnp.concatenate([high, middle, low, jnp.zeros_like(low)], axis=1)
     for h in range(2):
         sums = branch_sums(wt_ref, h * 128)
-        row_ref[:, h * 128 : (h + 1) * 128] = jnp.broadcast_to(sums, (8, 128))
         col_ref[h * 128 : (h + 1) * 128, :] = jnp.broadcast_to(sums, (128, 128)).T
 
 
@@ -76,9 +86,16 @@
         out_shape=(
             jax.ShapeDtypeStruct((KS, ROWS), F32),
             jax.ShapeDtypeStruct((8, KS, 128), BF16),
-            jax.ShapeDtypeStruct((8, ROWS), F32),
             jax.ShapeDtypeStruct((ROWS, 128), F32),
         ),
+        in_specs=[pl.BlockSpec(memory_space=pltpu.HBM)] * 3,
+        out_specs=tuple(in_vmem(3)),
+        scratch_shapes=[
+            pltpu.VMEM((ROWS, KS), jnp.int32),
+            pltpu.VMEM((1, ROWS), jnp.int32),
+            pltpu.VMEM((1, KS), jnp.int32),
+            pltpu.SemaphoreType.DMA((3,)),
+        ],
         compiler_params=params(),
         name="weigh",
     )(counts, totals.reshape(1, ROWS), lengths.reshape(1, KS))
@@ -257,7 +274,7 @@
     return jnp.where(keep_y, y * 4 + (x + 2) % 4, (1 - y) * 4 + x)
 
 
-def assemble_kernel(own1, other1, own2, other2, out_ref, turned_ref, sems):
+def assemble_kernel(own, other, out_ref, turned_ref, sems):
     core = lax.axis_index("branch") % 2
     b = lax.axis_index("blk")
     y = b // 4
@@ -277,17 +294,18 @@
             return pl.ds(pl.multiple_of(first, ROWS), ROWS)
         return pl.ds(pl.multiple_of(first + half * 128, 128), 128)
 
-    both = ((0, core, own1, own2), (1, 1 - core, other1, other2))
-    for _, half, ref1, ref2 in both:
+    both = ((0, core, own), (1, 1 - core, other))
+    for _, half, ref in both:
         rows = rows_of(half)
-        for slot, ref, lane in ((0, ref1, 0), (1, ref1, 256), (2, ref1, 512), (3, ref2, 0)):
+        for slot, lane in ((0, 0), (1, 256), (2, 512), (3, 768)):
             store(ref.at[:, lane : lane + ROWS], rows, columns(slot))
-        store(ref2.at[:, 256:384], rows, columns(4, half ^ y))
-    for side, half, ref1, ref2 in both:
-        for n, (slot, ref, lane) in enumerate(((5, ref1, 768), (6, ref1, 1024), (7, ref2, 384))):
+        store(ref.at[:, 1024:1152], rows, columns(4, half ^ y))
+    for side, half, ref in both:
+        for n, slot in enumerate((5, 6, 7)):
+            lane = 1152 + n * ROWS
             turned_ref[side, n] = ref[:, lane : lane + ROWS].T
             store(turned_ref.at[side, n], slice(0, ROWS), columns(slot, half))
-        turned_ref[side, 3, 0:128] = ref2[:, 640:768].T
+        turned_ref[side, 3, 0:128] = ref[:, 1920:2048].T
         store(turned_ref.at[side, 3, 0:128], rows_of(half ^ (1 - y)), columns(4, half))
     for copy in stores:
         copy.wait()
@@ -297,7 +315,7 @@
     return pl.pallas_call(
         assemble_kernel,
         out_shape=jax.ShapeDtypeStruct((ROWS, BLOCKS * ROWS), F32),
-        in_specs=in_vmem(4),
+        in_specs=in_vmem(2),
         out_specs=pl.BlockSpec(memory_space=pl.ANY),
         scratch_shapes=[
             pltpu.VMEM((2, 4, ROWS, 128), F32),
@@ -334,7 +352,7 @@
     def tied(v, *others):
         return lax.optimization_barrier((v, *others))[0]
 
-    wt, split, mass_row, mass_col = weigh(counts, totals, lengths)
+    wt, split, mass_col = weigh(counts, totals, lengths)
     got = [from_partner(wt, n) for n in range(2)]
     diagonal = spread_call("diagonal", 1, diagonal_columns, 256, 16, 0)
     first = [spread_call(f"first{s}", 2, first_columns, 512, 8, 2, s) for s in range(2)]
@@ -360,14 +378,12 @@
 
     third = tied(third, dist1, received2)
     kept2 = second[0](split, mass_col, third, got[3])
-    payload2 = pack(kept2, received2)
+    payload2 = pack(tied(kept2, *swapped1), received2)
     shard = jnp.sum(over_chips(payload2), axis=0)
     dist2 = shard[:, :384] / (own_mass + shard[0:3, 384:].reshape(384)[None, :])
     swapped2 = [to_partner(dist2[:, 0:256], 2), to_partner(dist2[:, 256:384], 3)]
 
-    own1, other1 = gather([tied(dist1, payload2), *swapped1])
-    own2, other2 = gather([dist2, *swapped2])
-    return assemble(own1, other1, own2, other2)
+    return assemble(*gather([dist1, dist2, *swapped1, *swapped2]))
 
 
 def solution(mesh):

time: 148 us -> 148 us (level)
  blocking collectives: 0 us -> 40.8 us
  waiting for transfers between devices: 31.1 us -> 8.55 us
  starting transfers between devices: 50.7 us -> 35.8 us
  local copies, waits for them, and re-layouts: 4.14 us -> 2.6 us
    all_to_all x0 -> x2, blocking collectives: none -> 40.8 us  [over_chips(): return lax.all_to_all(v, 'branch', 0, 0, axis_index_groups=chips)]
    all_to_all x4 -> x1, waiting for transfers between devices: 21.7 us -> 4.78 us  [over_chips(): return lax.all_to_all(v, 'branch', 0, 0, axis_index_groups=chips)]
    all_to_all x4 -> x1, starting transfers between devices: 21.4 us -> 8.42 us  [over_chips(): return lax.all_to_all(v, 'branch', 0, 0, axis_index_groups=chips)]
    ppermute x4, waiting for transfers between devices: 8.01 us -> 1.47 us  [to_partner(): return lax.ppermute(v, 'blk', [(b, PARTNERS[n][b]) for b in range(BLOCKS)])]
    ppermute x5 -> x4, starting transfers between devices: 12.8 us -> 7.99 us  [other_core(): return lax.ppermute(v, 'branch', [(i, i ^ 1) for i in range(32)])]
    ppermute x4, starting transfers between devices: 6.2 us -> 8.9 us  [to_partner(): return lax.ppermute(v, 'blk', [(b, PARTNERS[n][b]) for b in range(BLOCKS)])]
    broadcast_in_dim x2 -> x1, local copies, waits for them, and re-layouts: 1.65 us -> 0.09 us  [gather(): whole = over_chips(jnp.broadcast_to(mine[None], (16, *mine.shape)))]
  transfers between devices with their start and end apart: 17 -> 13, of which waited for: 8 -> 3; matrix products, arithmetic and copies ran while one was open for 0% -> 0% of each run, Pallas kernels for 32% -> 38%
where the time goes in v4:
time: 148 us
  Pallas kernels  59.4 us (40%)
  blocking collectives  40.8 us (28%)
  starting transfers between devices  35.8 us (24%)
  waiting for transfers between devices  8.55 us (6%)
  local copies, waits for them, and re-layouts  2.6 us (2%)
    pallas_call x5, Pallas kernels, call(): pl.pallas_call(kernel, out_shape=jax.ShapeDtypeStruct((halves, 136, width...  55.8 us
    all_to_all x2, blocking collectives, over_chips(): return lax.all_to_all(v, 'branch', 0, 0, axis_index_groups=chips)  40.8 us
    ppermute x4, starting transfers between devices, from_partner(): return lax.ppermute(v, 'blk', [(PARTNERS[n][b], b) for b in range(BLOCKS)])  10.4 us
    ppermute x4, starting transfers between devices, to_partner(): return lax.ppermute(v, 'blk', [(b, PARTNERS[n][b]) for b in range(BLOCKS)])  8.9 us
    all_to_all x1, starting transfers between devices, over_chips(): return lax.all_to_all(v, 'branch', 0, 0, axis_index_groups=chips)  8.42 us
    ppermute x4, starting transfers between devices, other_core(): return lax.ppermute(v, 'branch', [(i, i ^ 1) for i in range(32)])  7.99 us
    all_to_all x1, waiting for transfers between devices, over_chips(): return lax.all_to_all(v, 'branch', 0, 0, axis_index_groups=chips)  4.78 us
  transfers between devices with their start and end apart: 13, of which 3 were waited for; matrix products, arithmetic and copies ran while one was open for 0% of the time, Pallas kernels for 38%

profile of v4, /device:TPU:1, one launch (start us, length us, event | category | flops | bytes accessed | tf_op | source)
XLA Modules:
  0.0 147.7 jit_solution(4625477371818524038)
XLA Ops:
  0.0 1.0 copy-done
  2.4 1.3 weigh.1
  3.7 3.4 %collective-permute-start.1 = (f32[512,256]{1,0:T(8,128)S(1)}, f32[512,256]{1,0:T(8,128)S(1)}, u32[]{:S(2)}, u32[]{:S(2)}) collective-permute-start(f32[512,256]{1,0:T(8,128)S(1)} %get-tuple-element.15.refs_0_), channel_id=1, source_target_pairs={{32,0},{64,32},{96,64},{0,96},{160,128},{192,160},{224,192},{128,2... | collective-permute-start | bytes 1572872 | tf_op jit(solution)/shard_map/ppermute | solution.py:334
  7.1 1.6 %collective-permute-start.2 = (f32[512,256]{1,0:T(8,128)S(1)}, f32[512,256]{1,0:T(8,128)S(1)}, u32[]{:S(2)}, u32[]{:S(2)}) collective-permute-start(f32[512,256]{1,0:T(8,128)S(1)} %get-tuple-element.15.refs_0_), channel_id=1, source_target_pairs={{224,0},{128,32},{160,64},{192,96},{96,128},{0,160},{32,192},{64,2... | collective-permute-start | bytes 1572872 | tf_op jit(solution)/shard_map/ppermute | solution.py:334
  8.7 13.4 %diagonal.1.refs_0_ = f32[2,136,256]{2,1,0:T(8,128)S(1)} custom-call(bf16[8,512,128]{2,1,0:T(8,128)(2,1)S(1)} %get-tuple-element.12.split_ref, f32[256,128]{1,0:T(8,128)S(1)} %get-tuple-element.13.col_ref, f32[512,256]{1,0:T(8,128)S(1)} %get-tuple-element.15.refs_0_), custom_call_target="tpu_custom_call" | custom-call | flops 8388608000 | bytes 4194304 | tf_op jit(solution)/shard_map/diagonal/pallas_call | solution.py:199
  22.1 1.3 collective-permute-start
  23.4 1.8 %collective-permute-start.4 = (f32[512,256]{1,0:T(8,128)S(1)}, f32[512,256]{1,0:T(8,128)S(1)}, u32[]{:S(2)}, u32[]{:S(2)}) collective-permute-start(f32[512,256]{1,0:T(8,128)S(1)} %get-tuple-element.15.refs_0_), channel_id=1, source_target_pairs={{64,0},{96,32},{192,64},{224,96},{0,128},{32,160},{128,192},{160,2... | collective-permute-start | bytes 1572872 | tf_op jit(solution)/shard_map/ppermute | solution.py:334
  25.3 3.6 %collective-permute-start.5 = (f32[512,256]{1,0:T(8,128)S(1)}, f32[512,256]{1,0:T(8,128)S(1)}, u32[]{:S(2)}, u32[]{:S(2)}) collective-permute-start(f32[512,256]{1,0:T(8,128)S(1)} %get-tuple-element.15.refs_0_), channel_id=1, source_target_pairs={{192,0},{224,32},{128,64},{160,96},{64,128},{96,160},{0,192},{32,2... | collective-permute-start | bytes 1572872 | tf_op jit(solution)/shard_map/ppermute | solution.py:334
  28.9 11.4 %first1.1 = f32[1,136,512]{2,1,0:T(8,128)S(1)} custom-call(bf16[8,512,128]{2,1,0:T(8,128)(2,1)S(1)} %get-tuple-element.12.split_ref, f32[256,128]{1,0:T(8,128)S(1)} %get-tuple-element.13.col_ref, f32[512,256]{1,0:T(8,128)S(1)} %collective-permute-done.1.refs_0_, f32[512,256]{1,0:T(8,128)S(1)} %collective-permute-done.2.refs_1_), custom_call_target="tpu_custom_call" | custom-call | flops 8388608000 | bytes 4194304 | tf_op jit(solution)/shard_map/first1/pallas_call | solution.py:199
  41.0 11.3 %first0.1.refs_2_ = f32[1,136,512]{2,1,0:T(8,128)S(1)} custom-call(bf16[8,512,128]{2,1,0:T(8,128)(2,1)S(1)} %get-tuple-element.12.split_ref, f32[256,128]{1,0:T(8,128)S(1)} %get-tuple-element.13.col_ref, f32[512,256]{1,0:T(8,128)S(1)} %collective-permute-done.1.refs_0_, f32[512,256]{1,0:T(8,128)S(1)} %collective-permute-done.2.refs_1_), custom_call_target="tpu_custom_call" | custom-call | flops 8388608000 | bytes 4194304 | tf_op jit(solution)/shard_map/first0/pallas_call | solution.py:199
  52.3 0.8 pack.2
  53.2 8.4 %all-to-all-start = ((f32[16,8,896]{2,1,0:T(8,128)}), f32[16,8,896]{2,1,0:T(8,128)S(1)}, u32[]{:S(2)}, u32[]{:S(2)}) async-start(f32[16,8,896]{2,1,0:T(8,128)} %pack.2), calls=%async_computation | async-start | bytes 917504 | tf_op jit(solution)/shard_map/all_to_all | solution.py:345
  61.6 9.8 %second1.1 = f32[1,136,384]{2,1,0:T(8,128)S(1)} custom-call(bf16[8,512,128]{2,1,0:T(8,128)(2,1)S(1)} %get-tuple-element.12.split_ref, f32[256,128]{1,0:T(8,128)S(1)} %get-tuple-element.13.col_ref, f32[512,256]{1,0:T(8,128)S(1)} %collective-permute-done.4.refs_0_, f32[512,256]{1,0:T(8,128)S(1)} %collective-permute-done.5.refs_1_), custom_call_target="tpu_custom_call" | custom-call | flops 6291456000 | bytes 4194304 | tf_op jit(solution)/shard_map/second1/pallas_call | solution.py:199
  71.9 4.8 %all-to-all-done = f32[16,8,896]{2,1,0:T(8,128)S(1)} async-done(((f32[16,8,896]{2,1,0:T(8,128)}), f32[16,8,896]{2,1,0:T(8,128)S(1)}, u32[]{:S(2)}, u32[]{:S(2)}) %all-to-all-start) | async-done | bytes 458784 | tf_op jit(solution)/shard_map/all_to_all | solution.py:345
  76.9 1.6 %collective-permute-start.7 = (f32[8,256]{1,0:T(8,128)S(1)}, f32[8,256]{1,0:T(8,128)S(1)}, u32[]{:S(2)}, u32[]{:S(2)}) collective-permute-start(f32[8,256]{1,0:T(8,128)S(1)} %get-tuple-element.24), channel_id=1, source_target_pairs={{0,32},{32,64},{64,96},{96,0},{128,160},{160,192},{192,224},{224,1... | collective-permute-start | bytes 24584 | tf_op jit(solution)/shard_map/ppermute | solution.py:337
  78.5 1.7 %collective-permute-start.8 = (f32[8,256]{1,0:T(8,128)S(1)}, f32[8,256]{1,0:T(8,128)S(1)}, u32[]{:S(2)}, u32[]{:S(2)}) collective-permute-start(f32[8,256]{1,0:T(8,128)S(1)} %get-tuple-element.23), channel_id=1, source_target_pairs={{0,224},{32,128},{64,160},{96,192},{128,96},{160,0},{192,32},{224,... | collective-permute-start | bytes 24584 | tf_op jit(solution)/shard_map/ppermute | solution.py:337
  80.2 9.9 %second0.1.refs_0_ = f32[1,136,384]{2,1,0:T(8,128)S(1)} custom-call(bf16[8,512,128]{2,1,0:T(8,128)(2,1)S(1)} %get-tuple-element.12.split_ref, f32[256,128]{1,0:T(8,128)S(1)} %get-tuple-element.13.col_ref, f32[512,256]{1,0:T(8,128)S(1)} %collective-permute-done.4.refs_0_, f32[512,256]{1,0:T(8,128)S(1)} %collective-permute-done.5.refs_1_), custom_call_target="tpu_custom_call" | custom-call | flops 6291456000 | bytes 4194304 | tf_op jit(solution)/shard_map/second0/pallas_call | solution.py:199
  90.2 13.4 %all_to_all.15 = f32[16,8,512]{2,1,0:T(8,128)S(1)} all-to-all(f32[16,8,512]{2,1,0:T(8,128)S(1)} %pack.3), channel_id=1, replica_groups={{0,2,4,6,8,10,12,14,16,18,20,22,24,26,28,30},{1,3,5,7,9,11,13,15,17,19,..., dimensions={0} | all-to-all | bytes 524288 | tf_op jit(solution)/shard_map/all_to_all | solution.py:345
  104.4 4.9 %collective-permute-start.10 = (f32[8,128]{1,0:T(8,128)S(1)}, f32[8,128]{1,0:T(8,128)S(1)}, u32[]{:S(2)}, u32[]{:S(2)}) collective-permute-start(f32[8,128]{1,0:T(8,128)S(1)} %slice.53), channel_id=1, source_target_pairs={{0,192},{32,224},{64,128},{96,160},{128,64},{160,96},{192,0},{224,... | collective-permute-start | bytes 12296 | tf_op jit(solution)/shard_map/ppermute | solution.py:337
  109.3 1.5 collective-permute-done.10
  110.9 27.4 %all_to_all.16 = f32[16,8,2048]{2,1,0:T(8,128)S(1)} all-to-all(f32[16,8,2048]{2,1,0:T(8,128)S(1)} %broadcast_in_dim.2), channel_id=1, replica_groups={{0,2,4,6,8,10,12,14,16,18,20,22,24,26,28,30},{1,3,5,7,9,11,13,15,17,19,..., dimensions={0} | all-to-all | bytes 2097152 | tf_op jit(solution)/shard_map/all_to_all | solution.py:345
  138.3 5.5 %collective-permute-start.11 = (f32[16,8,2048]{2,1,0:T(8,128)S(1)}, f32[16,8,2048]{2,1,0:T(8,128)S(1)}, u32[]{:S(2)}, u32[]{:S(2)}) collective-permute-start(f32[16,8,2048]{2,1,0:T(8,128)S(1)} %all_to_all.16), channel_id=1, source_target_pairs={{0,1},{1,0},{2,3},{3,2},{4,5},{5,4},{6,7},{7,6},{8,9},{9,8},{10,11... | collective-permute-start | bytes 3145736 | tf_op jit(solution)/shard_map/ppermute | solution.py:340
  143.8 2.3 %collective-permute-done.11 = f32[16,8,2048]{2,1,0:T(8,128)S(1)} collective-permute-done((f32[16,8,2048]{2,1,0:T(8,128)S(1)}, f32[16,8,2048]{2,1,0:T(8,128)S(1)}, u32[]{:S(2)}, u32[]{:S(2)}) %collective-permute-start.11) | collective-permute-done | bytes 1048608 | tf_op jit(solution)/shard_map/ppermute | solution.py:340
  146.0 1.5 assemble.1
  (35 shorter events, 3.7 us)
Async XLA Ops:
  0.0 1.0 copy-start
  1.0 0.7 copy-start.1
  1.7 0.7 copy-start.2
  3.7 25.2 %collective-permute-start.1 = (f32[512,256]{1,0:T(8,128)S(1)}, f32[512,256]{1,0:T(8,128)S(1)}, u32[]{:S(2)}, u32[]{:S(2)}) collective-permute-start(f32[512,256]{1,0:T(8,128)S(1)} %get-tuple-element.15.refs_0_), channel_id=1, source_target_pairs={{32,0},{64,32},{96,64},{0,96},{160,128},{192,160},{224,192},{128,2... | collective-permute-start | bytes 1572872 | tf_op jit(solution)/shard_map/ppermute | solution.py:334
  7.1 21.8 %collective-permute-start.2 = (f32[512,256]{1,0:T(8,128)S(1)}, f32[512,256]{1,0:T(8,128)S(1)}, u32[]{:S(2)}, u32[]{:S(2)}) collective-permute-start(f32[512,256]{1,0:T(8,128)S(1)} %get-tuple-element.15.refs_0_), channel_id=1, source_target_pairs={{224,0},{128,32},{160,64},{192,96},{96,128},{0,160},{32,192},{64,2... | collective-permute-start | bytes 1572872 | tf_op jit(solution)/shard_map/ppermute | solution.py:334
  22.1 30.2 %collective-permute-start = (f32[2,136,256]{2,1,0:T(8,128)S(1)}, f32[2,136,256]{2,1,0:T(8,128)S(1)}, u32[]{:S(2)}, u32[]{:S(2)}) collective-permute-start(f32[2,136,256]{2,1,0:T(8,128)S(1)} %diagonal.1.refs_0_), channel_id=1, source_target_pairs={{0,1},{1,0},{2,3},{3,2},{4,5},{5,4},{6,7},{7,6},{8,9},{9,8},{10,11... | collective-permute-start | bytes 835592 | tf_op jit(solution)/shard_map/ppermute | solution.py:340
  23.4 38.2 %collective-permute-start.4 = (f32[512,256]{1,0:T(8,128)S(1)}, f32[512,256]{1,0:T(8,128)S(1)}, u32[]{:S(2)}, u32[]{:S(2)}) collective-permute-start(f32[512,256]{1,0:T(8,128)S(1)} %get-tuple-element.15.refs_0_), channel_id=1, source_target_pairs={{64,0},{96,32},{192,64},{224,96},{0,128},{32,160},{128,192},{160,2... | collective-permute-start | bytes 1572872 | tf_op jit(solution)/shard_map/ppermute | solution.py:334
  25.3 36.4 %collective-permute-start.5 = (f32[512,256]{1,0:T(8,128)S(1)}, f32[512,256]{1,0:T(8,128)S(1)}, u32[]{:S(2)}, u32[]{:S(2)}) collective-permute-start(f32[512,256]{1,0:T(8,128)S(1)} %get-tuple-element.15.refs_0_), channel_id=1, source_target_pairs={{192,0},{224,32},{128,64},{160,96},{64,128},{96,160},{0,192},{32,2... | collective-permute-start | bytes 1572872 | tf_op jit(solution)/shard_map/ppermute | solution.py:334
  40.3 12.1 %collective-permute-start.3 = (f32[1,136,512]{2,1,0:T(8,128)S(1)}, f32[1,136,512]{2,1,0:T(8,128)S(1)}, u32[]{:S(2)}, u32[]{:S(2)}) collective-permute-start(f32[1,136,512]{2,1,0:T(8,128)S(1)} %first1.1), channel_id=1, source_target_pairs={{0,1},{1,0},{2,3},{3,2},{4,5},{5,4},{6,7},{7,6},{8,9},{9,8},{10,11... | collective-permute-start | bytes 835592 | tf_op jit(solution)/shard_map/ppermute | solution.py:340
  53.2 23.5 %all-to-all-start = ((f32[16,8,896]{2,1,0:T(8,128)}), f32[16,8,896]{2,1,0:T(8,128)S(1)}, u32[]{:S(2)}, u32[]{:S(2)}) async-start(f32[16,8,896]{2,1,0:T(8,128)} %pack.2), calls=%async_computation | async-start | bytes 917504 | tf_op jit(solution)/shard_map/all_to_all | solution.py:345
  71.4 5.5 %collective-permute-start.6 = (f32[1,136,384]{2,1,0:T(8,128)S(1)}, f32[1,136,384]{2,1,0:T(8,128)S(1)}, u32[]{:S(2)}, u32[]{:S(2)}) collective-permute-start(f32[1,136,384]{2,1,0:T(8,128)S(1)} %second1.1), channel_id=1, source_target_pairs={{0,1},{1,0},{2,3},{3,2},{4,5},{5,4},{6,7},{7,6},{8,9},{9,8},{10,11... | collective-permute-start | bytes 626696 | tf_op jit(solution)/shard_map/ppermute | solution.py:340
  76.9 13.2 %collective-permute-start.7 = (f32[8,256]{1,0:T(8,128)S(1)}, f32[8,256]{1,0:T(8,128)S(1)}, u32[]{:S(2)}, u32[]{:S(2)}) collective-permute-start(f32[8,256]{1,0:T(8,128)S(1)} %get-tuple-element.24), channel_id=1, source_target_pairs={{0,32},{32,64},{64,96},{96,0},{128,160},{160,192},{192,224},{224,1... | collective-permute-start | bytes 24584 | tf_op jit(solution)/shard_map/ppermute | solution.py:337
  78.5 11.6 %collective-permute-start.8 = (f32[8,256]{1,0:T(8,128)S(1)}, f32[8,256]{1,0:T(8,128)S(1)}, u32[]{:S(2)}, u32[]{:S(2)}) collective-permute-start(f32[8,256]{1,0:T(8,128)S(1)} %get-tuple-element.23), channel_id=1, source_target_pairs={{0,224},{32,128},{64,160},{96,192},{128,96},{160,0},{192,32},{224,... | collective-permute-start | bytes 24584 | tf_op jit(solution)/shard_map/ppermute | solution.py:337
  103.7 5.6 %collective-permute-start.9 = (f32[8,256]{1,0:T(8,128)S(1)}, f32[8,256]{1,0:T(8,128)S(1)}, u32[]{:S(2)}, u32[]{:S(2)}) collective-permute-start(f32[8,256]{1,0:T(8,128)S(1)} %slice.52), channel_id=1, source_target_pairs={{0,64},{32,96},{64,192},{96,224},{128,0},{160,32},{192,128},{224,1... | collective-permute-start | bytes 24584 | tf_op jit(solution)/shard_map/ppermute | solution.py:337
  104.4 6.4 %collective-permute-start.10 = (f32[8,128]{1,0:T(8,128)S(1)}, f32[8,128]{1,0:T(8,128)S(1)}, u32[]{:S(2)}, u32[]{:S(2)}) collective-permute-start(f32[8,128]{1,0:T(8,128)S(1)} %slice.53), channel_id=1, source_target_pairs={{0,192},{32,224},{64,128},{96,160},{128,64},{160,96},{192,0},{224,... | collective-permute-start | bytes 12296 | tf_op jit(solution)/shard_map/ppermute | solution.py:337
  138.3 7.8 %collective-permute-start.11 = (f32[16,8,2048]{2,1,0:T(8,128)S(1)}, f32[16,8,2048]{2,1,0:T(8,128)S(1)}, u32[]{:S(2)}, u32[]{:S(2)}) collective-permute-start(f32[16,8,2048]{2,1,0:T(8,128)S(1)} %all_to_all.16), channel_id=1, source_target_pairs={{0,1},{1,0},{2,3},{3,2},{4,5},{5,4},{6,7},{7,6},{8,9},{9,8},{10,11... | collective-permute-start | bytes 3145736 | tf_op jit(solution)/shard_map/ppermute | solution.py:340

commit v5 on v4

--- a/solution.py
+++ b/solution.py
@@ -33,7 +33,6 @@
 
 
 PARTNERS = partner_tables()
-OWNERS = [[table.index(b) for b in range(BLOCKS)] for table in PARTNERS]
 
 
 def params():
@@ -228,27 +227,30 @@
     return [(0, 0), (0, 128), (1, (half ^ y) * 128)]
 
 
-def pack_kernel(*refs):
-    out_ref = refs[-1]
+DIRECT = 1152
+
+
+def pack_kernel(own0, got0, own1, got1, own2, got2, out_ref):
     core = lax.axis_index("branch") % 2
     lane = 0
-    masses = jnp.zeros((8, 128), F32)
-    for own, got in zip(refs[:-1:2], refs[1:-1:2], strict=True):
+    masses = []
+    for own, got in ((own0, got0), (own1, got1), (own2, got2)):
         half = core if own.shape[0] == 2 else 0
         width = own.shape[2]
         both = own[half, 0:128, :] + got[half, 0:128, :]
         out_ref[:, :, lane : lane + width] = both.reshape(16, 8, width)
-        masses = masses + own[half, 128:136, 0:128] + got[half, 128:136, 0:128]
+        masses.append(own[half, 128:136, 0:128] + got[half, 128:136, 0:128])
         lane += width
-    out_ref[:, :, lane:] = jnp.broadcast_to(masses[None], (16, 8, 128))
+    for block in (masses[0] + masses[1], masses[2]):
+        out_ref[:, :, lane : lane + 128] = jnp.broadcast_to(block[None], (16, 8, 128))
+        lane += 128
 
 
 def pack(*parts):
-    width = sum(p.shape[2] for p in parts[::2]) + 128
     return pl.pallas_call(
         pack_kernel,
-        out_shape=jax.ShapeDtypeStruct((16, 8, width), F32),
-        in_specs=in_vmem(len(parts)),
+        out_shape=jax.ShapeDtypeStruct((16, 8, DIRECT + 256), F32),
+        in_specs=in_vmem(6),
         out_specs=in_vmem(1)[0],
         compiler_params=params(),
         name="pack",
@@ -274,6 +276,60 @@
     return jnp.where(keep_y, y * 4 + (x + 2) % 4, (1 - y) * 4 + x)
 
 
+def normalise_kernel(shards_ref, dist_ref, swap_ref):
+    branch = lax.axis_index("branch")
+    b = lax.axis_index("blk")
+    core, place = branch % 2, branch // 2
+    total = jnp.sum(shards_ref[...], axis=0)
+    rows = [total[r : r + 1, DIRECT : DIRECT + 128] for r in range(6)]
+    rows += [total[r : r + 1, DIRECT + 128 : DIRECT + 256] for r in range(3)]
+    mine = jnp.broadcast_to(jnp.where(core == 0, rows[0], rows[1]), (8, 128))
+    lane = lax.broadcasted_iota(jnp.int32, (8, 128), 1)
+    row = lax.broadcasted_iota(jnp.int32, (8, 128), 0)
+    own = jnp.sum(jnp.where(lane == place * 8 + row, mine, 0.0), axis=1, keepdims=True)
+    for j in range(DIRECT // 128):
+        at = slice(128 * j, 128 * j + 128)
+        dist_ref[:, at] = total[:, at] / (own + rows[j])
+    swap_ref[...] = jnp.zeros_like(swap_ref)
+    for slot in range(1, 4):
+        swap_ref[block_partner(b, slot)] = dist_ref[:, slot * ROWS : (slot + 1) * ROWS]
+    swap_ref[block_partner(b, 4), :, 0:128] = dist_ref[:, 4 * ROWS : DIRECT]
+
+
+def normalise(shards):
+    return pl.pallas_call(
+        normalise_kernel,
+        out_shape=(
+            jax.ShapeDtypeStruct((8, DIRECT), F32),
+            jax.ShapeDtypeStruct((BLOCKS, 8, ROWS), F32),
+        ),
+        in_specs=in_vmem(1),
+        out_specs=tuple(in_vmem(2)),
+        compiler_params=params(),
+        name="normalise",
+    )(shards)
+
+
+def spread_out_kernel(dist_ref, swapped_ref, out_ref):
+    b = lax.axis_index("blk")
+    pieces = [dist_ref[...]]
+    pieces += [swapped_ref[block_partner(b, slot)] for slot in (5, 6, 7)]
+    pieces.append(swapped_ref[block_partner(b, 4), :, 0:128])
+    whole = jnp.concatenate(pieces, axis=1)
+    out_ref[...] = jnp.broadcast_to(whole[None], out_ref.shape)
+
+
+def spread_out(dist, swapped):
+    return pl.pallas_call(
+        spread_out_kernel,
+        out_shape=jax.ShapeDtypeStruct((16, 8, BLOCKS * ROWS), F32),
+        in_specs=in_vmem(2),
+        out_specs=in_vmem(1)[0],
+        compiler_params=params(),
+        name="spread_out",
+    )(dist, swapped)
+
+
 def assemble_kernel(own, other, out_ref, turned_ref, sems):
     core = lax.axis_index("branch") % 2
     b = lax.axis_index("blk")
@@ -327,15 +383,9 @@
 
 
 def on_device(counts, totals, lengths):
-    branch = lax.axis_index("branch")
-    place = branch // 2
-
     def from_partner(v, n):
         return lax.ppermute(v, "blk", [(PARTNERS[n][b], b) for b in range(BLOCKS)])
 
-    def to_partner(v, n):
-        return lax.ppermute(v, "blk", [(b, PARTNERS[n][b]) for b in range(BLOCKS)])
-
     def other_core(v):
         return lax.ppermute(v, "branch", [(i, i ^ 1) for i in range(32)])
 
@@ -343,47 +393,29 @@
 
     def over_chips(v):
         return lax.all_to_all(v, "branch", 0, 0, axis_index_groups=chips)
-
-    def gather(pieces):
-        mine = jnp.concatenate(pieces, axis=1)
-        whole = over_chips(jnp.broadcast_to(mine[None], (16, *mine.shape)))
-        return whole, other_core(whole)
-
-    def tied(v, *others):
-        return lax.optimization_barrier((v, *others))[0]
 
     wt, split, mass_col = weigh(counts, totals, lengths)
     got = [from_partner(wt, n) for n in range(2)]
     diagonal = spread_call("diagonal", 1, diagonal_columns, 256, 16, 0)
-    first = [spread_call(f"first{s}", 2, first_columns, 512, 8, 2, s) for s in range(2)]
+    first = spread_call("first", 2, first_columns, 512, 8, 2)
     second = [spread_call(f"second{s}", 2, second_columns, 384, 8, 0, s) for s in range(2)]
 
     part0 = diagonal(split, mass_col, wt)
-    later = tied(wt, part0)
+    later = lax.optimization_barrier((wt, part0))[0]
     got += [from_partner(later, n) for n in (2, 3)]
     received0 = other_core(part0)
-    received1 = other_core(first[1](split, mass_col, got[0], got[1]))
-    kept1 = first[0](split, mass_col, got[0], got[1])
-    payload1 = pack(part0, received0, kept1, received1)
-    shard = jnp.sum(over_chips(payload1), axis=0)
-
-    third = tied(got[2], payload1)
-    received2 = other_core(second[1](split, mass_col, third, got[3]))
-
-    mass = shard[:, 768:]
-    own_half = jnp.where(branch % 2 == 0, mass[0], mass[1])
-    own_mass = lax.dynamic_slice_in_dim(own_half, place * 8, 8)[:, None]
-    dist1 = shard[:, :768] / (own_mass + mass[0:6].reshape(768)[None, :])
-    swapped1 = [to_partner(dist1[:, 256 * (n + 1) : 256 * (n + 2)], n) for n in range(2)]
-
-    third = tied(third, dist1, received2)
-    kept2 = second[0](split, mass_col, third, got[3])
-    payload2 = pack(tied(kept2, *swapped1), received2)
-    shard = jnp.sum(over_chips(payload2), axis=0)
-    dist2 = shard[:, :384] / (own_mass + shard[0:3, 384:].reshape(384)[None, :])
-    swapped2 = [to_partner(dist2[:, 0:256], 2), to_partner(dist2[:, 256:384], 3)]
-
-    return assemble(*gather([dist1, dist2, *swapped1, *swapped2]))
+    part1 = first(split, mass_col, got[0], got[1])
+    received1 = other_core(part1)
+    third = lax.optimization_barrier((got[2], part1))[0]
+    sent2 = second[1](split, mass_col, third, got[3])
+    received2 = other_core(sent2)
+    third = lax.optimization_barrier((third, sent2))[0]
+    part2 = second[0](split, mass_col, third, got[3])
+
+    shards = over_chips(pack(part0, received0, part1, received1, part2, received2))
+    dist, swap = normalise(shards)
+    whole = over_chips(spread_out(dist, lax.all_to_all(swap, "blk", 0, 0)))
+    return assemble(whole, other_core(whole))
 
 
 def solution(mesh):

time: 148 us -> 147 us (level)
  blocking collectives: 40.8 us -> 67.8 us
  starting transfers between devices: 35.8 us -> 17.7 us
  waiting for transfers between devices: 8.55 us -> 2.31 us
  Pallas kernels: 59.4 us -> 56.7 us
    all_to_all x2, blocking collectives: 40.8 us -> 57.6 us  [over_chips(): return lax.all_to_all(v, 'branch', 0, 0, axis_index_groups=chips)]
    all_to_all x0 -> x1, blocking collectives: none -> 10.1 us  [on_device(): whole = over_chips(spread_out(dist, lax.all_to_all(swap, 'blk', 0, 0)))]
    ppermute x4 -> x0, starting transfers between devices: 8.9 us -> none  [to_partner(): return lax.ppermute(v, 'blk', [(b, PARTNERS[n][b]) for b in range(BLOCKS)])]
    all_to_all x1 -> x0, starting transfers between devices: 8.42 us -> none  [over_chips(): return lax.all_to_all(v, 'branch', 0, 0, axis_index_groups=chips)]
    all_to_all x1 -> x0, waiting for transfers between devices: 4.78 us -> none  [over_chips(): return lax.all_to_all(v, 'branch', 0, 0, axis_index_groups=chips)]
    pallas_call x5 -> x4, Pallas kernels: 55.8 us -> 53.7 us  [call(): pl.pallas_call(kernel, out_shape=jax.ShapeDtypeStruct((halves, 136, width...]
  transfers between devices with their start and end apart: 13 -> 8, of which waited for: 3 -> 1; matrix products, arithmetic and copies ran while one was open for 0% -> 0% of each run, Pallas kernels for 38% -> 36%
where the time goes in v5:
time: 147 us
  blocking collectives  67.8 us (46%)
  Pallas kernels  56.7 us (39%)
  starting transfers between devices  17.7 us (12%)
  local copies, waits for them, and re-layouts  2.4 us (2%)
  waiting for transfers between devices  2.31 us (2%)
    all_to_all x2, blocking collectives, over_chips(): return lax.all_to_all(v, 'branch', 0, 0, axis_index_groups=chips)  57.6 us
    pallas_call x4, Pallas kernels, call(): pl.pallas_call(kernel, out_shape=jax.ShapeDtypeStruct((halves, 136, width...  53.7 us
    ppermute x4, starting transfers between devices, from_partner(): return lax.ppermute(v, 'blk', [(PARTNERS[n][b], b) for b in range(BLOCKS)])  10.5 us
    all_to_all x1, blocking collectives, on_device(): whole = over_chips(spread_out(dist, lax.all_to_all(swap, 'blk', 0, 0)))  10.1 us
    ppermute x4, starting transfers between devices, other_core(): return lax.ppermute(v, 'branch', [(i, i ^ 1) for i in range(32)])  7.22 us
  transfers between devices with their start and end apart: 8, of which 1 were waited for; matrix products, arithmetic and copies ran while one was open for 0% of the time, Pallas kernels for 36%

profile of v5, /device:TPU:1, one launch (start us, length us, event | category | flops | bytes accessed | tf_op | source)
XLA Modules:
  0.0 147.2 jit_solution(7930445748305631855)
XLA Ops:
  0.0 1.0 copy-done
  1.0 0.7 copy-done.1
  1.7 0.7 copy-done.2
  2.4 1.3 weigh.1
  3.7 3.4 %collective-permute-start.1 = (f32[512,256]{1,0:T(8,128)S(1)}, f32[512,256]{1,0:T(8,128)S(1)}, u32[]{:S(2)}, u32[]{:S(2)}) collective-permute-start(f32[512,256]{1,0:T(8,128)S(1)} %get-tuple-element.16.refs_0_), channel_id=1, source_target_pairs={{32,0},{64,32},{96,64},{0,96},{160,128},{192,160},{224,192},{128,2... | collective-permute-start | bytes 1572872 | tf_op jit(solution)/shard_map/ppermute | solution.py:387
  7.1 1.6 %collective-permute-start.2 = (f32[512,256]{1,0:T(8,128)S(1)}, f32[512,256]{1,0:T(8,128)S(1)}, u32[]{:S(2)}, u32[]{:S(2)}) collective-permute-start(f32[512,256]{1,0:T(8,128)S(1)} %get-tuple-element.16.refs_0_), channel_id=1, source_target_pairs={{224,0},{128,32},{160,64},{192,96},{96,128},{0,160},{32,192},{64,2... | collective-permute-start | bytes 1572872 | tf_op jit(solution)/shard_map/ppermute | solution.py:387
  8.7 13.3 %diagonal.1.own0 = f32[2,136,256]{2,1,0:T(8,128)S(1)} custom-call(bf16[8,512,128]{2,1,0:T(8,128)(2,1)S(1)} %get-tuple-element.13.split_ref, f32[256,128]{1,0:T(8,128)S(1)} %get-tuple-element.14.col_ref, f32[512,256]{1,0:T(8,128)S(1)} %get-tuple-element.16.refs_0_), custom_call_target="tpu_custom_call" | custom-call | flops 8388608000 | bytes 4194304 | tf_op jit(solution)/shard_map/diagonal/pallas_call | solution.py:198
  22.1 1.4 collective-permute-start.4
  23.4 4.1 %collective-permute-start.5 = (f32[512,256]{1,0:T(8,128)S(1)}, f32[512,256]{1,0:T(8,128)S(1)}, u32[]{:S(2)}, u32[]{:S(2)}) collective-permute-start(f32[512,256]{1,0:T(8,128)S(1)} %get-tuple-element.16.refs_0_), channel_id=1, source_target_pairs={{192,0},{224,32},{128,64},{160,96},{64,128},{96,160},{0,192},{32,2... | collective-permute-start | bytes 1572872 | tf_op jit(solution)/shard_map/ppermute | solution.py:387
  27.6 1.8 %collective-permute-start = (f32[2,136,256]{2,1,0:T(8,128)S(1)}, f32[2,136,256]{2,1,0:T(8,128)S(1)}, u32[]{:S(2)}, u32[]{:S(2)}) collective-permute-start(f32[2,136,256]{2,1,0:T(8,128)S(1)} %diagonal.1.own0), channel_id=1, source_target_pairs={{0,1},{1,0},{2,3},{3,2},{4,5},{5,4},{6,7},{7,6},{8,9},{9,8},{10,11... | collective-permute-start | bytes 835592 | tf_op jit(solution)/shard_map/ppermute | solution.py:390
  29.4 21.8 %first.1.own1 = f32[2,136,512]{2,1,0:T(8,128)S(1)} custom-call(bf16[8,512,128]{2,1,0:T(8,128)(2,1)S(1)} %get-tuple-element.13.split_ref, f32[256,128]{1,0:T(8,128)S(1)} %get-tuple-element.14.col_ref, f32[512,256]{1,0:T(8,128)S(1)} %collective-permute-done.1.refs_0_, f32[512,256]{1,0:T(8,128)S(1)} %collective-permute-done.2.refs_1_), custom_call_target="tpu_custom_call" | custom-call | flops 16777216000 | bytes 4194304 | tf_op jit(solution)/shard_map/first/pallas_call | solution.py:198
  51.2 9.0 %second1.1 = f32[1,136,384]{2,1,0:T(8,128)S(1)} custom-call(bf16[8,512,128]{2,1,0:T(8,128)(2,1)S(1)} %get-tuple-element.13.split_ref, f32[256,128]{1,0:T(8,128)S(1)} %get-tuple-element.14.col_ref, f32[512,256]{1,0:T(8,128)S(1)} %collective-permute-done.4.refs_0_, f32[512,256]{1,0:T(8,128)S(1)} %collective-permute-done.5.refs_1_), custom_call_target="tpu_custom_call" | custom-call | flops 6291456000 | bytes 4194304 | tf_op jit(solution)/shard_map/second1/pallas_call | solution.py:198
  60.2 0.6 collective-permute-start.6
  60.8 0.3 collective-permute-start.3
  61.1 9.5 %second0.1.own2 = f32[1,136,384]{2,1,0:T(8,128)S(1)} custom-call(bf16[8,512,128]{2,1,0:T(8,128)(2,1)S(1)} %get-tuple-element.13.split_ref, f32[256,128]{1,0:T(8,128)S(1)} %get-tuple-element.14.col_ref, f32[512,256]{1,0:T(8,128)S(1)} %collective-permute-done.4.refs_0_, f32[512,256]{1,0:T(8,128)S(1)} %collective-permute-done.5.refs_1_), custom_call_target="tpu_custom_call" | custom-call | flops 6291456000 | bytes 4194304 | tf_op jit(solution)/shard_map/second0/pallas_call | solution.py:198
  70.6 0.1 pack.1
  70.7 29.9 %all_to_all.15.shards_ref = f32[16,8,1408]{2,1,0:T(8,128)S(1)} all-to-all(f32[16,8,1408]{2,1,0:T(8,128)S(1)} %pack.1), channel_id=1, replica_groups={{0,2,4,6,8,10,12,14,16,18,20,22,24,26,28,30},{1,3,5,7,9,11,13,15,17,19,..., dimensions={0} | all-to-all | bytes 1441792 | tf_op jit(solution)/shard_map/all_to_all | solution.py:395
  100.6 0.1 normalise.1
  100.7 10.1 %all_to_all.16.swapped_ref = f32[8,8,256]{2,1,0:T(8,128)S(1)} all-to-all(f32[8,8,256]{2,1,0:T(8,128)S(1)} %get-tuple-element.20), channel_id=1, replica_groups=mesh['blk'=8,'branch'=32] {'blk'}, dimensions={0} | all-to-all | bytes 131072 | tf_op jit(solution)/shard_map/all_to_all | solution.py:417
  110.8 0.1 spread_out.1
  110.9 27.8 %all_to_all.17 = f32[16,8,2048]{2,1,0:T(8,128)S(1)} all-to-all(f32[16,8,2048]{2,1,0:T(8,128)S(1)} %spread_out.1), channel_id=1, replica_groups={{0,2,4,6,8,10,12,14,16,18,20,22,24,26,28,30},{1,3,5,7,9,11,13,15,17,19,..., dimensions={0} | all-to-all | bytes 2097152 | tf_op jit(solution)/shard_map/all_to_all | solution.py:395
  138.7 4.5 %collective-permute-start.7 = (f32[16,8,2048]{2,1,0:T(8,128)S(1)}, f32[16,8,2048]{2,1,0:T(8,128)S(1)}, u32[]{:S(2)}, u32[]{:S(2)}) collective-permute-start(f32[16,8,2048]{2,1,0:T(8,128)S(1)} %all_to_all.17), channel_id=1, source_target_pairs={{0,1},{1,0},{2,3},{3,2},{4,5},{5,4},{6,7},{7,6},{8,9},{9,8},{10,11... | collective-permute-start | bytes 3145736 | tf_op jit(solution)/shard_map/ppermute | solution.py:390
  143.3 2.3 %collective-permute-done.7 = f32[16,8,2048]{2,1,0:T(8,128)S(1)} collective-permute-done((f32[16,8,2048]{2,1,0:T(8,128)S(1)}, f32[16,8,2048]{2,1,0:T(8,128)S(1)}, u32[]{:S(2)}, u32[]{:S(2)}) %collective-permute-start.7) | collective-permute-done | bytes 1048608 | tf_op jit(solution)/shard_map/ppermute | solution.py:390
  145.5 1.5 assemble.1
  (10 shorter events, 0.0 us)
Async XLA Ops:
  0.0 1.0 copy-start
  1.0 0.7 copy-start.1
  1.7 0.7 copy-start.2
  3.7 25.7 %collective-permute-start.1 = (f32[512,256]{1,0:T(8,128)S(1)}, f32[512,256]{1,0:T(8,128)S(1)}, u32[]{:S(2)}, u32[]{:S(2)}) collective-permute-start(f32[512,256]{1,0:T(8,128)S(1)} %get-tuple-element.16.refs_0_), channel_id=1, source_target_pairs={{32,0},{64,32},{96,64},{0,96},{160,128},{192,160},{224,192},{128,2... | collective-permute-start | bytes 1572872 | tf_op jit(solution)/shard_map/ppermute | solution.py:387
  7.1 22.3 %collective-permute-start.2 = (f32[512,256]{1,0:T(8,128)S(1)}, f32[512,256]{1,0:T(8,128)S(1)}, u32[]{:S(2)}, u32[]{:S(2)}) collective-permute-start(f32[512,256]{1,0:T(8,128)S(1)} %get-tuple-element.16.refs_0_), channel_id=1, source_target_pairs={{224,0},{128,32},{160,64},{192,96},{96,128},{0,160},{32,192},{64,2... | collective-permute-start | bytes 1572872 | tf_op jit(solution)/shard_map/ppermute | solution.py:387
  22.1 29.1 %collective-permute-start.4 = (f32[512,256]{1,0:T(8,128)S(1)}, f32[512,256]{1,0:T(8,128)S(1)}, u32[]{:S(2)}, u32[]{:S(2)}) collective-permute-start(f32[512,256]{1,0:T(8,128)S(1)} %get-tuple-element.16.refs_0_), channel_id=1, source_target_pairs={{64,0},{96,32},{192,64},{224,96},{0,128},{32,160},{128,192},{160,2... | collective-permute-start | bytes 1572872 | tf_op jit(solution)/shard_map/ppermute | solution.py:387
  23.4 27.7 %collective-permute-start.5 = (f32[512,256]{1,0:T(8,128)S(1)}, f32[512,256]{1,0:T(8,128)S(1)}, u32[]{:S(2)}, u32[]{:S(2)}) collective-permute-start(f32[512,256]{1,0:T(8,128)S(1)} %get-tuple-element.16.refs_0_), channel_id=1, source_target_pairs={{192,0},{224,32},{128,64},{160,96},{64,128},{96,160},{0,192},{32,2... | collective-permute-start | bytes 1572872 | tf_op jit(solution)/shard_map/ppermute | solution.py:387
  27.6 43.0 %collective-permute-start = (f32[2,136,256]{2,1,0:T(8,128)S(1)}, f32[2,136,256]{2,1,0:T(8,128)S(1)}, u32[]{:S(2)}, u32[]{:S(2)}) collective-permute-start(f32[2,136,256]{2,1,0:T(8,128)S(1)} %diagonal.1.own0), channel_id=1, source_target_pairs={{0,1},{1,0},{2,3},{3,2},{4,5},{5,4},{6,7},{7,6},{8,9},{9,8},{10,11... | collective-permute-start | bytes 835592 | tf_op jit(solution)/shard_map/ppermute | solution.py:390
  60.2 10.4 %collective-permute-start.6 = (f32[1,136,384]{2,1,0:T(8,128)S(1)}, f32[1,136,384]{2,1,0:T(8,128)S(1)}, u32[]{:S(2)}, u32[]{:S(2)}) collective-permute-start(f32[1,136,384]{2,1,0:T(8,128)S(1)} %second1.1), channel_id=1, source_target_pairs={{0,1},{1,0},{2,3},{3,2},{4,5},{5,4},{6,7},{7,6},{8,9},{9,8},{10,11... | collective-permute-start | bytes 626696 | tf_op jit(solution)/shard_map/ppermute | solution.py:390
  60.8 9.8 %collective-permute-start.3 = (f32[2,136,512]{2,1,0:T(8,128)S(1)}, f32[2,136,512]{2,1,0:T(8,128)S(1)}, u32[]{:S(2)}, u32[]{:S(2)}) collective-permute-start(f32[2,136,512]{2,1,0:T(8,128)S(1)} %first.1.own1), channel_id=1, source_target_pairs={{0,1},{1,0},{2,3},{3,2},{4,5},{5,4},{6,7},{7,6},{8,9},{9,8},{10,11... | collective-permute-start | bytes 1671176 | tf_op jit(solution)/shard_map/ppermute | solution.py:390
  138.7 6.8 %collective-permute-start.7 = (f32[16,8,2048]{2,1,0:T(8,128)S(1)}, f32[16,8,2048]{2,1,0:T(8,128)S(1)}, u32[]{:S(2)}, u32[]{:S(2)}) collective-permute-start(f32[16,8,2048]{2,1,0:T(8,128)S(1)} %all_to_all.17), channel_id=1, source_target_pairs={{0,1},{1,0},{2,3},{3,2},{4,5},{5,4},{6,7},{7,6},{8,9},{9,8},{10,11... | collective-permute-start | bytes 3145736 | tf_op jit(solution)/shard_map/ppermute | solution.py:390

commit v6 on v5

--- a/solution.py
+++ b/solution.py
@@ -230,27 +230,32 @@
 DIRECT = 1152
 
 
-def pack_kernel(own0, got0, own1, got1, own2, got2, out_ref):
+FIRST = 768
+SECOND = 384
+DIRECT = FIRST + SECOND
+
+
+def pack_kernel(*refs):
+    out_ref = refs[-1]
     core = lax.axis_index("branch") % 2
     lane = 0
-    masses = []
-    for own, got in ((own0, got0), (own1, got1), (own2, got2)):
+    masses = jnp.zeros((8, 128), F32)
+    for own, got in zip(refs[:-1:2], refs[1:-1:2], strict=True):
         half = core if own.shape[0] == 2 else 0
         width = own.shape[2]
         both = own[half, 0:128, :] + got[half, 0:128, :]
         out_ref[:, :, lane : lane + width] = both.reshape(16, 8, width)
-        masses.append(own[half, 128:136, 0:128] + got[half, 128:136, 0:128])
+        masses = masses + own[half, 128:136, 0:128] + got[half, 128:136, 0:128]
         lane += width
-    for block in (masses[0] + masses[1], masses[2]):
-        out_ref[:, :, lane : lane + 128] = jnp.broadcast_to(block[None], (16, 8, 128))
-        lane += 128
+    out_ref[:, :, lane:] = jnp.broadcast_to(masses[None], (16, 8, 128))
 
 
 def pack(*parts):
+    width = sum(p.shape[2] for p in parts[::2]) + 128
     return pl.pallas_call(
         pack_kernel,
-        out_shape=jax.ShapeDtypeStruct((16, 8, DIRECT + 256), F32),
-        in_specs=in_vmem(6),
+        out_shape=jax.ShapeDtypeStruct((16, 8, width), F32),
+        in_specs=in_vmem(len(parts)),
         out_specs=in_vmem(1)[0],
         compiler_params=params(),
         name="pack",
@@ -276,13 +281,15 @@
     return jnp.where(keep_y, y * 4 + (x + 2) % 4, (1 - y) * 4 + x)
 
 
-def normalise_kernel(shards_ref, dist_ref, swap_ref):
+def normalise_kernel(first_ref, second_ref, dist_ref, swap_ref):
     branch = lax.axis_index("branch")
     b = lax.axis_index("blk")
     core, place = branch % 2, branch // 2
-    total = jnp.sum(shards_ref[...], axis=0)
-    rows = [total[r : r + 1, DIRECT : DIRECT + 128] for r in range(6)]
-    rows += [total[r : r + 1, DIRECT + 128 : DIRECT + 256] for r in range(3)]
+    first = jnp.sum(first_ref[...], axis=0)
+    second = jnp.sum(second_ref[...], axis=0)
+    rows = [first[r : r + 1, FIRST:] for r in range(6)]
+    rows += [second[r : r + 1, SECOND:] for r in range(3)]
+    total = jnp.concatenate([first[:, :FIRST], second[:, :SECOND]], axis=1)
     mine = jnp.broadcast_to(jnp.where(core == 0, rows[0], rows[1]), (8, 128))
     lane = lax.broadcasted_iota(jnp.int32, (8, 128), 1)
     row = lax.broadcasted_iota(jnp.int32, (8, 128), 0)
@@ -296,18 +303,18 @@
     swap_ref[block_partner(b, 4), :, 0:128] = dist_ref[:, 4 * ROWS : DIRECT]
 
 
-def normalise(shards):
+def normalise(first, second):
     return pl.pallas_call(
         normalise_kernel,
         out_shape=(
             jax.ShapeDtypeStruct((8, DIRECT), F32),
             jax.ShapeDtypeStruct((BLOCKS, 8, ROWS), F32),
         ),
-        in_specs=in_vmem(1),
+        in_specs=in_vmem(2),
         out_specs=tuple(in_vmem(2)),
         compiler_params=params(),
         name="normalise",
-    )(shards)
+    )(first, second)
 
 
 def spread_out_kernel(dist_ref, swapped_ref, out_ref):
@@ -397,23 +404,29 @@
     wt, split, mass_col = weigh(counts, totals, lengths)
     got = [from_partner(wt, n) for n in range(2)]
     diagonal = spread_call("diagonal", 1, diagonal_columns, 256, 16, 0)
-    first = spread_call("first", 2, first_columns, 512, 8, 2)
+    first = [spread_call(f"first{s}", 2, first_columns, 512, 8, 2, s) for s in range(2)]
     second = [spread_call(f"second{s}", 2, second_columns, 384, 8, 0, s) for s in range(2)]
 
+    def after(v, *others):
+        return lax.optimization_barrier((v, *others))[0]
+
     part0 = diagonal(split, mass_col, wt)
-    later = lax.optimization_barrier((wt, part0))[0]
+    later = after(wt, part0)
     got += [from_partner(later, n) for n in (2, 3)]
     received0 = other_core(part0)
-    part1 = first(split, mass_col, got[0], got[1])
-    received1 = other_core(part1)
-    third = lax.optimization_barrier((got[2], part1))[0]
+    sent1 = first[1](split, mass_col, *got[:2])
+    received1 = other_core(sent1)
+    part1 = first[0](split, mass_col, after(got[0], sent1), got[1])
+    payload1 = pack(part0, received0, part1, received1)
+    shards1 = over_chips(payload1)
+
+    third = after(got[2], payload1)
     sent2 = second[1](split, mass_col, third, got[3])
     received2 = other_core(sent2)
-    third = lax.optimization_barrier((third, sent2))[0]
-    part2 = second[0](split, mass_col, third, got[3])
-
-    shards = over_chips(pack(part0, received0, part1, received1, part2, received2))
-    dist, swap = normalise(shards)
+    part2 = second[0](split, mass_col, after(third, sent2), got[3])
+    shards2 = over_chips(pack(part2, received2))
+
+    dist, swap = normalise(shards1, shards2)
     whole = over_chips(spread_out(dist, lax.all_to_all(swap, "blk", 0, 0)))
     return assemble(whole, other_core(whole))
 

time: 147 us -> 158 us (1.075)
  blocking collectives: 67.8 us -> 75.4 us
  Pallas kernels: 56.7 us -> 59.2 us
    all_to_all x2 -> x3, blocking collectives: 57.6 us -> 65.7 us  [over_chips(): return lax.all_to_all(v, 'branch', 0, 0, axis_index_groups=chips)]
    pallas_call x4 -> x5, Pallas kernels: 53.7 us -> 56.1 us  [call(): pl.pallas_call(kernel, out_shape=jax.ShapeDtypeStruct((halves, 136, width...]
  transfers between devices with their start and end apart: 8 -> 8, of which waited for: 1 -> 1; matrix products, arithmetic and copies ran while one was open for 0% -> 0% of each run, Pallas kernels for 36% -> 30%
where the time goes in v6:
time: 158 us
  blocking collectives  75.4 us (48%)
  Pallas kernels  59.2 us (37%)
  starting transfers between devices  18 us (11%)
  local copies, waits for them, and re-layouts  2.4 us (2%)
  waiting for transfers between devices  2.31 us (1%)
    all_to_all x3, blocking collectives, over_chips(): return lax.all_to_all(v, 'branch', 0, 0, axis_index_groups=chips)  65.7 us
    pallas_call x5, Pallas kernels, call(): pl.pallas_call(kernel, out_shape=jax.ShapeDtypeStruct((halves, 136, width...  56.1 us
    ppermute x4, starting transfers between devices, from_partner(): return lax.ppermute(v, 'blk', [(PARTNERS[n][b], b) for b in range(BLOCKS)])  10.4 us
    all_to_all x1, blocking collectives, on_device(): whole = over_chips(spread_out(dist, lax.all_to_all(swap, 'blk', 0, 0)))  9.67 us
    ppermute x4, starting transfers between devices, other_core(): return lax.ppermute(v, 'branch', [(i, i ^ 1) for i in range(32)])  7.51 us
  transfers between devices with their start and end apart: 8, of which 1 were waited for; matrix products, arithmetic and copies ran while one was open for 0% of the time, Pallas kernels for 30%

profile of v6, /device:TPU:1, one launch (start us, length us, event | category | flops | bytes accessed | tf_op | source)
XLA Modules:
  0.0 157.5 jit_solution(11081355394962624897)
XLA Ops:
  0.0 1.0 copy-done
  1.0 0.7 copy-done.1
  1.7 0.7 copy-done.2
  2.4 1.3 weigh.1
  3.7 3.4 %collective-permute-start.1 = (f32[512,256]{1,0:T(8,128)S(1)}, f32[512,256]{1,0:T(8,128)S(1)}, u32[]{:S(2)}, u32[]{:S(2)}) collective-permute-start(f32[512,256]{1,0:T(8,128)S(1)} %get-tuple-element.18.refs_0_), channel_id=1, source_target_pairs={{32,0},{64,32},{96,64},{0,96},{160,128},{192,160},{224,192},{128,2... | collective-permute-start | bytes 1572872 | tf_op jit(solution)/shard_map/ppermute | solution.py:394
  7.1 1.6 %collective-permute-start.2 = (f32[512,256]{1,0:T(8,128)S(1)}, f32[512,256]{1,0:T(8,128)S(1)}, u32[]{:S(2)}, u32[]{:S(2)}) collective-permute-start(f32[512,256]{1,0:T(8,128)S(1)} %get-tuple-element.18.refs_0_), channel_id=1, source_target_pairs={{224,0},{128,32},{160,64},{192,96},{96,128},{0,160},{32,192},{64,2... | collective-permute-start | bytes 1572872 | tf_op jit(solution)/shard_map/ppermute | solution.py:394
  8.7 13.4 %diagonal.1.refs_0_ = f32[2,136,256]{2,1,0:T(8,128)S(1)} custom-call(bf16[8,512,128]{2,1,0:T(8,128)(2,1)S(1)} %get-tuple-element.14.split_ref, f32[256,128]{1,0:T(8,128)S(1)} %get-tuple-element.15.col_ref, f32[512,256]{1,0:T(8,128)S(1)} %get-tuple-element.18.refs_0_), custom_call_target="tpu_custom_call" | custom-call | flops 8388608000 | bytes 4194304 | tf_op jit(solution)/shard_map/diagonal/pallas_call | solution.py:198
  22.1 1.3 collective-permute-start
  23.4 1.8 %collective-permute-start.4 = (f32[512,256]{1,0:T(8,128)S(1)}, f32[512,256]{1,0:T(8,128)S(1)}, u32[]{:S(2)}, u32[]{:S(2)}) collective-permute-start(f32[512,256]{1,0:T(8,128)S(1)} %get-tuple-element.18.refs_0_), channel_id=1, source_target_pairs={{64,0},{96,32},{192,64},{224,96},{0,128},{32,160},{128,192},{160,2... | collective-permute-start | bytes 1572872 | tf_op jit(solution)/shard_map/ppermute | solution.py:394
  25.3 3.6 %collective-permute-start.5 = (f32[512,256]{1,0:T(8,128)S(1)}, f32[512,256]{1,0:T(8,128)S(1)}, u32[]{:S(2)}, u32[]{:S(2)}) collective-permute-start(f32[512,256]{1,0:T(8,128)S(1)} %get-tuple-element.18.refs_0_), channel_id=1, source_target_pairs={{192,0},{224,32},{128,64},{160,96},{64,128},{96,160},{0,192},{32,2... | collective-permute-start | bytes 1572872 | tf_op jit(solution)/shard_map/ppermute | solution.py:394
  28.9 11.9 %first1.1 = f32[1,136,512]{2,1,0:T(8,128)S(1)} custom-call(bf16[8,512,128]{2,1,0:T(8,128)(2,1)S(1)} %get-tuple-element.14.split_ref, f32[256,128]{1,0:T(8,128)S(1)} %get-tuple-element.15.col_ref, f32[512,256]{1,0:T(8,128)S(1)} %collective-permute-done.1.refs_0_, f32[512,256]{1,0:T(8,128)S(1)} %collective-permute-done.2.refs_1_), custom_call_target="tpu_custom_call" | custom-call | flops 8388608000 | bytes 4194304 | tf_op jit(solution)/shard_map/first1/pallas_call | solution.py:198
  40.8 0.9 collective-permute-start.3
  41.7 11.9 %first0.1.refs_2_ = f32[1,136,512]{2,1,0:T(8,128)S(1)} custom-call(bf16[8,512,128]{2,1,0:T(8,128)(2,1)S(1)} %get-tuple-element.14.split_ref, f32[256,128]{1,0:T(8,128)S(1)} %get-tuple-element.15.col_ref, f32[512,256]{1,0:T(8,128)S(1)} %collective-permute-done.1.refs_0_, f32[512,256]{1,0:T(8,128)S(1)} %collective-permute-done.2.refs_1_), custom_call_target="tpu_custom_call" | custom-call | flops 8388608000 | bytes 4194304 | tf_op jit(solution)/shard_map/first0/pallas_call | solution.py:198
  53.7 9.3 %second1.1 = f32[1,136,384]{2,1,0:T(8,128)S(1)} custom-call(bf16[8,512,128]{2,1,0:T(8,128)(2,1)S(1)} %get-tuple-element.14.split_ref, f32[256,128]{1,0:T(8,128)S(1)} %get-tuple-element.15.col_ref, f32[512,256]{1,0:T(8,128)S(1)} %collective-permute-done.4.refs_0_, f32[512,256]{1,0:T(8,128)S(1)} %collective-permute-done.5.refs_1_), custom_call_target="tpu_custom_call" | custom-call | flops 6291456000 | bytes 4194304 | tf_op jit(solution)/shard_map/second1/pallas_call | solution.py:198
  62.9 0.6 collective-permute-start.6
  63.5 9.7 %second0.1.refs_0_ = f32[1,136,384]{2,1,0:T(8,128)S(1)} custom-call(bf16[8,512,128]{2,1,0:T(8,128)(2,1)S(1)} %get-tuple-element.14.split_ref, f32[256,128]{1,0:T(8,128)S(1)} %get-tuple-element.15.col_ref, f32[512,256]{1,0:T(8,128)S(1)} %collective-permute-done.4.refs_0_, f32[512,256]{1,0:T(8,128)S(1)} %collective-permute-done.5.refs_1_), custom_call_target="tpu_custom_call" | custom-call | flops 6291456000 | bytes 4194304 | tf_op jit(solution)/shard_map/second0/pallas_call | solution.py:198
  73.3 19.9 %all_to_all.20.second_ref = f32[16,8,512]{2,1,0:T(8,128)S(1)} all-to-all(f32[16,8,512]{2,1,0:T(8,128)S(1)} %pack.3), channel_id=1, replica_groups={{0,2,4,6,8,10,12,14,16,18,20,22,24,26,28,30},{1,3,5,7,9,11,13,15,17,19,..., dimensions={0} | all-to-all | bytes 524288 | tf_op jit(solution)/shard_map/all_to_all | solution.py:402
  93.2 17.2 %all_to_all.21.first_ref = f32[16,8,896]{2,1,0:T(8,128)S(1)} all-to-all(f32[16,8,896]{2,1,0:T(8,128)S(1)} %pack.2), channel_id=1, replica_groups={{0,2,4,6,8,10,12,14,16,18,20,22,24,26,28,30},{1,3,5,7,9,11,13,15,17,19,..., dimensions={0} | all-to-all | bytes 917504 | tf_op jit(solution)/shard_map/all_to_all | solution.py:402
  110.3 0.1 normalise.1
  110.4 9.7 %all_to_all.22.swapped_ref = f32[8,8,256]{2,1,0:T(8,128)S(1)} all-to-all(f32[8,8,256]{2,1,0:T(8,128)S(1)} %get-tuple-element.22), channel_id=1, replica_groups=mesh['blk'=8,'branch'=32] {'blk'}, dimensions={0} | all-to-all | bytes 131072 | tf_op jit(solution)/shard_map/all_to_all | solution.py:430
  120.2 28.7 %all_to_all.23 = f32[16,8,2048]{2,1,0:T(8,128)S(1)} all-to-all(f32[16,8,2048]{2,1,0:T(8,128)S(1)} %spread_out.1), channel_id=1, replica_groups={{0,2,4,6,8,10,12,14,16,18,20,22,24,26,28,30},{1,3,5,7,9,11,13,15,17,19,..., dimensions={0} | all-to-all | bytes 2097152 | tf_op jit(solution)/shard_map/all_to_all | solution.py:402
  148.9 4.7 %collective-permute-start.7 = (f32[16,8,2048]{2,1,0:T(8,128)S(1)}, f32[16,8,2048]{2,1,0:T(8,128)S(1)}, u32[]{:S(2)}, u32[]{:S(2)}) collective-permute-start(f32[16,8,2048]{2,1,0:T(8,128)S(1)} %all_to_all.23), channel_id=1, source_target_pairs={{0,1},{1,0},{2,3},{3,2},{4,5},{5,4},{6,7},{7,6},{8,9},{9,8},{10,11... | collective-permute-start | bytes 3145736 | tf_op jit(solution)/shard_map/ppermute | solution.py:397
  153.6 2.3 %collective-permute-done.7 = f32[16,8,2048]{2,1,0:T(8,128)S(1)} collective-permute-done((f32[16,8,2048]{2,1,0:T(8,128)S(1)}, f32[16,8,2048]{2,1,0:T(8,128)S(1)}, u32[]{:S(2)}, u32[]{:S(2)}) %collective-permute-start.7) | collective-permute-done | bytes 1048608 | tf_op jit(solution)/shard_map/ppermute | solution.py:397
  155.9 1.5 assemble.1
  (13 shorter events, 0.2 us)
Async XLA Ops:
  0.0 1.0 copy-start
  1.0 0.7 copy-start.1
  1.7 0.7 copy-start.2
  3.7 25.2 %collective-permute-start.1 = (f32[512,256]{1,0:T(8,128)S(1)}, f32[512,256]{1,0:T(8,128)S(1)}, u32[]{:S(2)}, u32[]{:S(2)}) collective-permute-start(f32[512,256]{1,0:T(8,128)S(1)} %get-tuple-element.18.refs_0_), channel_id=1, source_target_pairs={{32,0},{64,32},{96,64},{0,96},{160,128},{192,160},{224,192},{128,2... | collective-permute-start | bytes 1572872 | tf_op jit(solution)/shard_map/ppermute | solution.py:394
  7.1 21.8 %collective-permute-start.2 = (f32[512,256]{1,0:T(8,128)S(1)}, f32[512,256]{1,0:T(8,128)S(1)}, u32[]{:S(2)}, u32[]{:S(2)}) collective-permute-start(f32[512,256]{1,0:T(8,128)S(1)} %get-tuple-element.18.refs_0_), channel_id=1, source_target_pairs={{224,0},{128,32},{160,64},{192,96},{96,128},{0,160},{32,192},{64,2... | collective-permute-start | bytes 1572872 | tf_op jit(solution)/shard_map/ppermute | solution.py:394
  22.1 31.4 %collective-permute-start = (f32[2,136,256]{2,1,0:T(8,128)S(1)}, f32[2,136,256]{2,1,0:T(8,128)S(1)}, u32[]{:S(2)}, u32[]{:S(2)}) collective-permute-start(f32[2,136,256]{2,1,0:T(8,128)S(1)} %diagonal.1.refs_0_), channel_id=1, source_target_pairs={{0,1},{1,0},{2,3},{3,2},{4,5},{5,4},{6,7},{7,6},{8,9},{9,8},{10,11... | collective-permute-start | bytes 835592 | tf_op jit(solution)/shard_map/ppermute | solution.py:397
  23.4 30.2 %collective-permute-start.4 = (f32[512,256]{1,0:T(8,128)S(1)}, f32[512,256]{1,0:T(8,128)S(1)}, u32[]{:S(2)}, u32[]{:S(2)}) collective-permute-start(f32[512,256]{1,0:T(8,128)S(1)} %get-tuple-element.18.refs_0_), channel_id=1, source_target_pairs={{64,0},{96,32},{192,64},{224,96},{0,128},{32,160},{128,192},{160,2... | collective-permute-start | bytes 1572872 | tf_op jit(solution)/shard_map/ppermute | solution.py:394
  25.3 28.4 %collective-permute-start.5 = (f32[512,256]{1,0:T(8,128)S(1)}, f32[512,256]{1,0:T(8,128)S(1)}, u32[]{:S(2)}, u32[]{:S(2)}) collective-permute-start(f32[512,256]{1,0:T(8,128)S(1)} %get-tuple-element.18.refs_0_), channel_id=1, source_target_pairs={{192,0},{224,32},{128,64},{160,96},{64,128},{96,160},{0,192},{32,2... | collective-permute-start | bytes 1572872 | tf_op jit(solution)/shard_map/ppermute | solution.py:394
  40.8 12.8 %collective-permute-start.3 = (f32[1,136,512]{2,1,0:T(8,128)S(1)}, f32[1,136,512]{2,1,0:T(8,128)S(1)}, u32[]{:S(2)}, u32[]{:S(2)}) collective-permute-start(f32[1,136,512]{2,1,0:T(8,128)S(1)} %first1.1), channel_id=1, source_target_pairs={{0,1},{1,0},{2,3},{3,2},{4,5},{5,4},{6,7},{7,6},{8,9},{9,8},{10,11... | collective-permute-start | bytes 835592 | tf_op jit(solution)/shard_map/ppermute | solution.py:397
  62.9 10.3 %collective-permute-start.6 = (f32[1,136,384]{2,1,0:T(8,128)S(1)}, f32[1,136,384]{2,1,0:T(8,128)S(1)}, u32[]{:S(2)}, u32[]{:S(2)}) collective-permute-start(f32[1,136,384]{2,1,0:T(8,128)S(1)} %second1.1), channel_id=1, source_target_pairs={{0,1},{1,0},{2,3},{3,2},{4,5},{5,4},{6,7},{7,6},{8,9},{9,8},{10,11... | collective-permute-start | bytes 626696 | tf_op jit(solution)/shard_map/ppermute | solution.py:397
  148.9 7.0 %collective-permute-start.7 = (f32[16,8,2048]{2,1,0:T(8,128)S(1)}, f32[16,8,2048]{2,1,0:T(8,128)S(1)}, u32[]{:S(2)}, u32[]{:S(2)}) collective-permute-start(f32[16,8,2048]{2,1,0:T(8,128)S(1)} %all_to_all.23), channel_id=1, source_target_pairs={{0,1},{1,0},{2,3},{3,2},{4,5},{5,4},{6,7},{7,6},{8,9},{9,8},{10,11... | collective-permute-start | bytes 3145736 | tf_op jit(solution)/shard_map/ppermute | solution.py:397

commit v7 on v5

--- a/solution.py
+++ b/solution.py
@@ -276,9 +276,8 @@
     return jnp.where(keep_y, y * 4 + (x + 2) % 4, (1 - y) * 4 + x)
 
 
-def normalise_kernel(shards_ref, dist_ref, swap_ref):
+def normalise_kernel(shards_ref, out_ref):
     branch = lax.axis_index("branch")
-    b = lax.axis_index("blk")
     core, place = branch % 2, branch // 2
     total = jnp.sum(shards_ref[...], axis=0)
     rows = [total[r : r + 1, DIRECT : DIRECT + 128] for r in range(6)]
@@ -289,48 +288,22 @@
     own = jnp.sum(jnp.where(lane == place * 8 + row, mine, 0.0), axis=1, keepdims=True)
     for j in range(DIRECT // 128):
         at = slice(128 * j, 128 * j + 128)
-        dist_ref[:, at] = total[:, at] / (own + rows[j])
-    swap_ref[...] = jnp.zeros_like(swap_ref)
-    for slot in range(1, 4):
-        swap_ref[block_partner(b, slot)] = dist_ref[:, slot * ROWS : (slot + 1) * ROWS]
-    swap_ref[block_partner(b, 4), :, 0:128] = dist_ref[:, 4 * ROWS : DIRECT]
+        dist = total[:, at] / (own + rows[j])
+        out_ref[:, :, at] = jnp.broadcast_to(dist[None], (16, 8, 128))
 
 
 def normalise(shards):
     return pl.pallas_call(
         normalise_kernel,
-        out_shape=(
-            jax.ShapeDtypeStruct((8, DIRECT), F32),
-            jax.ShapeDtypeStruct((BLOCKS, 8, ROWS), F32),
-        ),
+        out_shape=jax.ShapeDtypeStruct((16, 8, DIRECT), F32),
         in_specs=in_vmem(1),
-        out_specs=tuple(in_vmem(2)),
+        out_specs=in_vmem(1)[0],
         compiler_params=params(),
         name="normalise",
     )(shards)
 
 
-def spread_out_kernel(dist_ref, swapped_ref, out_ref):
-    b = lax.axis_index("blk")
-    pieces = [dist_ref[...]]
-    pieces += [swapped_ref[block_partner(b, slot)] for slot in (5, 6, 7)]
-    pieces.append(swapped_ref[block_partner(b, 4), :, 0:128])
-    whole = jnp.concatenate(pieces, axis=1)
-    out_ref[...] = jnp.broadcast_to(whole[None], out_ref.shape)
-
-
-def spread_out(dist, swapped):
-    return pl.pallas_call(
-        spread_out_kernel,
-        out_shape=jax.ShapeDtypeStruct((16, 8, BLOCKS * ROWS), F32),
-        in_specs=in_vmem(2),
-        out_specs=in_vmem(1)[0],
-        compiler_params=params(),
-        name="spread_out",
-    )(dist, swapped)
-
-
-def assemble_kernel(own, other, out_ref, turned_ref, sems):
+def assemble_kernel(own, other, own_swapped, other_swapped, out_ref, turned_ref, sems):
     core = lax.axis_index("branch") % 2
     b = lax.axis_index("blk")
     y = b // 4
@@ -350,18 +323,16 @@
             return pl.ds(pl.multiple_of(first, ROWS), ROWS)
         return pl.ds(pl.multiple_of(first + half * 128, 128), 128)
 
-    both = ((0, core, own), (1, 1 - core, other))
-    for _, half, ref in both:
+    for half, ref in ((core, own), (1 - core, other)):
         rows = rows_of(half)
-        for slot, lane in ((0, 0), (1, 256), (2, 512), (3, 768)):
-            store(ref.at[:, lane : lane + ROWS], rows, columns(slot))
-        store(ref.at[:, 1024:1152], rows, columns(4, half ^ y))
-    for side, half, ref in both:
+        for slot in range(4):
+            store(ref.at[:, slot * ROWS : (slot + 1) * ROWS], rows, columns(slot))
+        store(ref.at[:, 4 * ROWS : DIRECT], rows, columns(4, half ^ y))
+    for side, half, ref in ((0, core, own_swapped), (1, 1 - core, other_swapped)):
         for n, slot in enumerate((5, 6, 7)):
-            lane = 1152 + n * ROWS
-            turned_ref[side, n] = ref[:, lane : lane + ROWS].T
+            turned_ref[side, n] = ref[:, n * ROWS : (n + 1) * ROWS].T
             store(turned_ref.at[side, n], slice(0, ROWS), columns(slot, half))
-        turned_ref[side, 3, 0:128] = ref[:, 1920:2048].T
+        turned_ref[side, 3, 0:128] = ref[:, 3 * ROWS :].T
         store(turned_ref.at[side, 3, 0:128], rows_of(half ^ (1 - y)), columns(4, half))
     for copy in stores:
         copy.wait()
@@ -371,7 +342,7 @@
     return pl.pallas_call(
         assemble_kernel,
         out_shape=jax.ShapeDtypeStruct((ROWS, BLOCKS * ROWS), F32),
-        in_specs=in_vmem(2),
+        in_specs=in_vmem(4),
         out_specs=pl.BlockSpec(memory_space=pl.ANY),
         scratch_shapes=[
             pltpu.VMEM((2, 4, ROWS, 128), F32),
@@ -379,7 +350,7 @@
         ],
         compiler_params=params(),
         name="assemble",
-    )(*[p.reshape(128, p.shape[2]) for p in pieces])
+    )(*pieces)
 
 
 def on_device(counts, totals, lengths):
@@ -413,9 +384,14 @@
     part2 = second[0](split, mass_col, third, got[3])
 
     shards = over_chips(pack(part0, received0, part1, received1, part2, received2))
-    dist, swap = normalise(shards)
-    whole = over_chips(spread_out(dist, lax.all_to_all(swap, "blk", 0, 0)))
-    return assemble(whole, other_core(whole))
+    own = over_chips(normalise(shards)).reshape(128, DIRECT)
+    swapped = []
+    for n in range(4):
+        tile = own[:, (n + 1) * ROWS : min((n + 2) * ROWS, DIRECT)]
+        swapped.append(lax.ppermute(tile, "blk", [(b, PARTNERS[n][b]) for b in range(BLOCKS)]))
+    other = other_core(own)
+    swapped = jnp.concatenate(swapped, axis=1)
+    return assemble(own, other, swapped, other_core(swapped))
 
 
 def solution(mesh):

time: 147 us -> 142 us (0.966)
  blocking collectives: 67.8 us -> 51.1 us
  starting transfers between devices: 17.7 us -> 24.9 us
  waiting for transfers between devices: 2.31 us -> 6.39 us
    all_to_all x1 -> x0, blocking collectives: 10.1 us -> none  [on_device(): whole = over_chips(spread_out(dist, lax.all_to_all(swap, 'blk', 0, 0)))]
    ppermute x0 -> x4, starting transfers between devices: none -> 8.14 us  [on_device(): lax.ppermute(tile, 'blk', [(b, PARTNERS[n][b]) for b in range(BLOCKS)])]
    all_to_all x2, blocking collectives: 57.6 us -> 51.1 us  [over_chips(): return lax.all_to_all(v, 'branch', 0, 0, axis_index_groups=chips)]
    ppermute x0 -> x4, waiting for transfers between devices: none -> 4.93 us  [on_device(): lax.ppermute(tile, 'blk', [(b, PARTNERS[n][b]) for b in range(BLOCKS)])]
    ppermute x4 -> x5, starting transfers between devices: 7.22 us -> 6.23 us  [other_core(): return lax.ppermute(v, 'branch', [(i, i ^ 1) for i in range(32)])]
  transfers between devices with their start and end apart: 8 -> 13, of which waited for: 1 -> 3; matrix products, arithmetic and copies ran while one was open for 0% -> 0% of each run, Pallas kernels for 36% -> 38%
where the time goes in v7:
time: 142 us
  Pallas kernels  56.7 us (40%)
  blocking collectives  51.1 us (36%)
  starting transfers between devices  24.9 us (18%)
  waiting for transfers between devices  6.39 us (4%)
  local copies, waits for them, and re-layouts  2.47 us (2%)
    pallas_call x4, Pallas kernels, call(): pl.pallas_call(kernel, out_shape=jax.ShapeDtypeStruct((halves, 136, width...  53.7 us
    all_to_all x2, blocking collectives, over_chips(): return lax.all_to_all(v, 'branch', 0, 0, axis_index_groups=chips)  51.1 us
    ppermute x4, starting transfers between devices, from_partner(): return lax.ppermute(v, 'blk', [(PARTNERS[n][b], b) for b in range(BLOCKS)])  10.5 us
    ppermute x4, starting transfers between devices, on_device(): lax.ppermute(tile, 'blk', [(b, PARTNERS[n][b]) for b in range(BLOCKS)])  8.14 us
    ppermute x5, starting transfers between devices, other_core(): return lax.ppermute(v, 'branch', [(i, i ^ 1) for i in range(32)])  6.23 us
    ppermute x4, waiting for transfers between devices, on_device(): lax.ppermute(tile, 'blk', [(b, PARTNERS[n][b]) for b in range(BLOCKS)])  4.93 us
  transfers between devices with their start and end apart: 13, of which 3 were waited for; matrix products, arithmetic and copies ran while one was open for 0% of the time, Pallas kernels for 38%

profile of v7, /device:TPU:1, one launch (start us, length us, event | category | flops | bytes accessed | tf_op | source)
XLA Modules:
  0.0 141.8 jit_solution(1117976080578428285)
XLA Ops:
  0.0 1.0 copy-done
  1.0 0.7 copy-done.1
  1.7 0.7 copy-done.2
  2.4 1.3 weigh.1
  3.7 3.4 %collective-permute-start.1 = (f32[512,256]{1,0:T(8,128)S(1)}, f32[512,256]{1,0:T(8,128)S(1)}, u32[]{:S(2)}, u32[]{:S(2)}) collective-permute-start(f32[512,256]{1,0:T(8,128)S(1)} %get-tuple-element.14.refs_0_), channel_id=1, source_target_pairs={{32,0},{64,32},{96,64},{0,96},{160,128},{192,160},{224,192},{128,2... | collective-permute-start | bytes 1572872 | tf_op jit(solution)/shard_map/ppermute | solution.py:358
  7.1 1.6 %collective-permute-start.2 = (f32[512,256]{1,0:T(8,128)S(1)}, f32[512,256]{1,0:T(8,128)S(1)}, u32[]{:S(2)}, u32[]{:S(2)}) collective-permute-start(f32[512,256]{1,0:T(8,128)S(1)} %get-tuple-element.14.refs_0_), channel_id=1, source_target_pairs={{224,0},{128,32},{160,64},{192,96},{96,128},{0,160},{32,192},{64,2... | collective-permute-start | bytes 1572872 | tf_op jit(solution)/shard_map/ppermute | solution.py:358
  8.7 13.3 %diagonal.1.own0 = f32[2,136,256]{2,1,0:T(8,128)S(1)} custom-call(bf16[8,512,128]{2,1,0:T(8,128)(2,1)S(1)} %get-tuple-element.11.split_ref, f32[256,128]{1,0:T(8,128)S(1)} %get-tuple-element.12.col_ref, f32[512,256]{1,0:T(8,128)S(1)} %get-tuple-element.14.refs_0_), custom_call_target="tpu_custom_call" | custom-call | flops 8388608000 | bytes 4194304 | tf_op jit(solution)/shard_map/diagonal/pallas_call | solution.py:198
  22.1 1.4 collective-permute-start.4
  23.4 4.1 %collective-permute-start.5 = (f32[512,256]{1,0:T(8,128)S(1)}, f32[512,256]{1,0:T(8,128)S(1)}, u32[]{:S(2)}, u32[]{:S(2)}) collective-permute-start(f32[512,256]{1,0:T(8,128)S(1)} %get-tuple-element.14.refs_0_), channel_id=1, source_target_pairs={{192,0},{224,32},{128,64},{160,96},{64,128},{96,160},{0,192},{32,2... | collective-permute-start | bytes 1572872 | tf_op jit(solution)/shard_map/ppermute | solution.py:358
  27.6 1.8 %collective-permute-start = (f32[2,136,256]{2,1,0:T(8,128)S(1)}, f32[2,136,256]{2,1,0:T(8,128)S(1)}, u32[]{:S(2)}, u32[]{:S(2)}) collective-permute-start(f32[2,136,256]{2,1,0:T(8,128)S(1)} %diagonal.1.own0), channel_id=1, source_target_pairs={{0,1},{1,0},{2,3},{3,2},{4,5},{5,4},{6,7},{7,6},{8,9},{9,8},{10,11... | collective-permute-start | bytes 835592 | tf_op jit(solution)/shard_map/ppermute | solution.py:361
  29.4 21.8 %first.1.own1 = f32[2,136,512]{2,1,0:T(8,128)S(1)} custom-call(bf16[8,512,128]{2,1,0:T(8,128)(2,1)S(1)} %get-tuple-element.11.split_ref, f32[256,128]{1,0:T(8,128)S(1)} %get-tuple-element.12.col_ref, f32[512,256]{1,0:T(8,128)S(1)} %collective-permute-done.1.refs_0_, f32[512,256]{1,0:T(8,128)S(1)} %collective-permute-done.2.refs_1_), custom_call_target="tpu_custom_call" | custom-call | flops 16777216000 | bytes 4194304 | tf_op jit(solution)/shard_map/first/pallas_call | solution.py:198
  51.2 9.0 %second1.1 = f32[1,136,384]{2,1,0:T(8,128)S(1)} custom-call(bf16[8,512,128]{2,1,0:T(8,128)(2,1)S(1)} %get-tuple-element.11.split_ref, f32[256,128]{1,0:T(8,128)S(1)} %get-tuple-element.12.col_ref, f32[512,256]{1,0:T(8,128)S(1)} %collective-permute-done.4.refs_0_, f32[512,256]{1,0:T(8,128)S(1)} %collective-permute-done.5.refs_1_), custom_call_target="tpu_custom_call" | custom-call | flops 6291456000 | bytes 4194304 | tf_op jit(solution)/shard_map/second1/pallas_call | solution.py:198
  61.1 9.5 %second0.1.own2 = f32[1,136,384]{2,1,0:T(8,128)S(1)} custom-call(bf16[8,512,128]{2,1,0:T(8,128)(2,1)S(1)} %get-tuple-element.11.split_ref, f32[256,128]{1,0:T(8,128)S(1)} %get-tuple-element.12.col_ref, f32[512,256]{1,0:T(8,128)S(1)} %collective-permute-done.4.refs_0_, f32[512,256]{1,0:T(8,128)S(1)} %collective-permute-done.5.refs_1_), custom_call_target="tpu_custom_call" | custom-call | flops 6291456000 | bytes 4194304 | tf_op jit(solution)/shard_map/second0/pallas_call | solution.py:198
  70.7 29.9 %all_to_all.10.shards_ref = f32[16,8,1408]{2,1,0:T(8,128)S(1)} all-to-all(f32[16,8,1408]{2,1,0:T(8,128)S(1)} %pack.1), channel_id=1, replica_groups={{0,2,4,6,8,10,12,14,16,18,20,22,24,26,28,30},{1,3,5,7,9,11,13,15,17,19,..., dimensions={0} | all-to-all | bytes 1441792 | tf_op jit(solution)/shard_map/all_to_all | solution.py:366
  100.7 21.3 %all_to_all.11 = f32[16,8,1152]{2,1,0:T(8,128)S(1)} all-to-all(f32[16,8,1152]{2,1,0:T(8,128)S(1)} %normalise.1), channel_id=1, replica_groups={{0,2,4,6,8,10,12,14,16,18,20,22,24,26,28,30},{1,3,5,7,9,11,13,15,17,19,..., dimensions={0} | all-to-all | bytes 1179648 | tf_op jit(solution)/shard_map/all_to_all | solution.py:366
  122.0 1.6 %collective-permute-start.8 = (f32[128,256]{1,0:T(8,128)S(1)}, f32[128,256]{1,0:T(8,128)S(1)}, u32[]{:S(2)}, u32[]{:S(2)}) collective-permute-start(f32[128,256]{1,0:T(8,128)S(1)} %get-tuple-element.19), channel_id=1, source_target_pairs={{0,32},{32,64},{64,96},{96,0},{128,160},{160,192},{192,224},{224,1... | collective-permute-start | bytes 393224 | tf_op jit(solution)/shard_map/ppermute | solution.py:391
  123.6 1.3 collective-permute-start.9
  125.0 2.7 %collective-permute-start.7 = (f32[128,1152]{1,0:T(8,128)S(1)}, f32[128,1152]{1,0:T(8,128)S(1)}, u32[]{:S(2)}, u32[]{:S(2)}) collective-permute-start(f32[128,1152]{1,0:T(8,128)S(1)} %bitcast.5), channel_id=1, source_target_pairs={{0,1},{1,0},{2,3},{3,2},{4,5},{5,4},{6,7},{7,6},{8,9},{9,8},{10,11... | collective-permute-start | bytes 1769480 | tf_op jit(solution)/shard_map/ppermute | solution.py:361
  128.2 4.7 %collective-permute-start.11 = (f32[128,128]{1,0:T(8,128)S(1)}, f32[128,128]{1,0:T(8,128)S(1)}, u32[]{:S(2)}, u32[]{:S(2)}) collective-permute-start(f32[128,128]{1,0:T(8,128)S(1)} %slice.19), channel_id=1, source_target_pairs={{0,192},{32,224},{64,128},{96,160},{128,64},{160,96},{192,0},{224,... | collective-permute-start | bytes 196616 | tf_op jit(solution)/shard_map/ppermute | solution.py:391
  132.9 2.9 %collective-permute-done.10 = f32[128,256]{1,0:T(8,128)S(1)} collective-permute-done((f32[128,256]{1,0:T(8,128)S(1)}, f32[128,256]{1,0:T(8,128)S(1)}, u32[]{:S(2)}, u32[]{:S(2)}) %collective-permute-start.10) | collective-permute-done | bytes 131104 | tf_op jit(solution)/shard_map/ppermute | solution.py:391
  135.8 2.1 %collective-permute-done.11 = f32[128,128]{1,0:T(8,128)S(1)} collective-permute-done((f32[128,128]{1,0:T(8,128)S(1)}, f32[128,128]{1,0:T(8,128)S(1)}, u32[]{:S(2)}, u32[]{:S(2)}) %collective-permute-start.11) | collective-permute-done | bytes 65568 | tf_op jit(solution)/shard_map/ppermute | solution.py:391
  137.9 0.9 collective-permute-start.12
  138.7 1.4 %collective-permute-done.12.other_swapped = f32[128,896]{1,0:T(8,128)S(1)} collective-permute-done((f32[128,896]{1,0:T(8,128)S(1)}, f32[128,896]{1,0:T(8,128)S(1)}, u32[]{:S(2)}, u32[]{:S(2)}) %collective-permute-start.12) | collective-permute-done | bytes 458784 | tf_op jit(solution)/shard_map/ppermute | solution.py:361
  140.2 1.5 %assemble.1 = f32[256,2048]{1,0:T(8,128)} custom-call(f32[128,1152]{1,0:T(8,128)S(1)} %bitcast.6, f32[128,1152]{1,0:T(8,128)S(1)} %collective-permute-done.7.other, f32[128,896]{1,0:T(8,128)S(1)} %constant_dynamic-update-slice_fusion.own_swapped, f32[128,896]{1,0:T(8,128)S(1)} %collective-permute-done.12.other_swapped), custom_call_target="tpu_custom_call" | custom-call | tf_op jit(solution)/shard_map/assemble/pallas_call | solution.py:342
  (24 shorter events, 1.7 us)
Async XLA Ops:
  0.0 1.0 copy-start
  1.0 0.7 copy-start.1
  1.7 0.7 copy-start.2
  3.7 25.7 %collective-permute-start.1 = (f32[512,256]{1,0:T(8,128)S(1)}, f32[512,256]{1,0:T(8,128)S(1)}, u32[]{:S(2)}, u32[]{:S(2)}) collective-permute-start(f32[512,256]{1,0:T(8,128)S(1)} %get-tuple-element.14.refs_0_), channel_id=1, source_target_pairs={{32,0},{64,32},{96,64},{0,96},{160,128},{192,160},{224,192},{128,2... | collective-permute-start | bytes 1572872 | tf_op jit(solution)/shard_map/ppermute | solution.py:358
  7.1 22.3 %collective-permute-start.2 = (f32[512,256]{1,0:T(8,128)S(1)}, f32[512,256]{1,0:T(8,128)S(1)}, u32[]{:S(2)}, u32[]{:S(2)}) collective-permute-start(f32[512,256]{1,0:T(8,128)S(1)} %get-tuple-element.14.refs_0_), channel_id=1, source_target_pairs={{224,0},{128,32},{160,64},{192,96},{96,128},{0,160},{32,192},{64,2... | collective-permute-start | bytes 1572872 | tf_op jit(solution)/shard_map/ppermute | solution.py:358
  22.1 29.1 %collective-permute-start.4 = (f32[512,256]{1,0:T(8,128)S(1)}, f32[512,256]{1,0:T(8,128)S(1)}, u32[]{:S(2)}, u32[]{:S(2)}) collective-permute-start(f32[512,256]{1,0:T(8,128)S(1)} %get-tuple-element.14.refs_0_), channel_id=1, source_target_pairs={{64,0},{96,32},{192,64},{224,96},{0,128},{32,160},{128,192},{160,2... | collective-permute-start | bytes 1572872 | tf_op jit(solution)/shard_map/ppermute | solution.py:358
  23.4 27.7 %collective-permute-start.5 = (f32[512,256]{1,0:T(8,128)S(1)}, f32[512,256]{1,0:T(8,128)S(1)}, u32[]{:S(2)}, u32[]{:S(2)}) collective-permute-start(f32[512,256]{1,0:T(8,128)S(1)} %get-tuple-element.14.refs_0_), channel_id=1, source_target_pairs={{192,0},{224,32},{128,64},{160,96},{64,128},{96,160},{0,192},{32,2... | collective-permute-start | bytes 1572872 | tf_op jit(solution)/shard_map/ppermute | solution.py:358
  27.6 43.0 %collective-permute-start = (f32[2,136,256]{2,1,0:T(8,128)S(1)}, f32[2,136,256]{2,1,0:T(8,128)S(1)}, u32[]{:S(2)}, u32[]{:S(2)}) collective-permute-start(f32[2,136,256]{2,1,0:T(8,128)S(1)} %diagonal.1.own0), channel_id=1, source_target_pairs={{0,1},{1,0},{2,3},{3,2},{4,5},{5,4},{6,7},{7,6},{8,9},{9,8},{10,11... | collective-permute-start | bytes 835592 | tf_op jit(solution)/shard_map/ppermute | solution.py:361
  60.2 10.4 %collective-permute-start.6 = (f32[1,136,384]{2,1,0:T(8,128)S(1)}, f32[1,136,384]{2,1,0:T(8,128)S(1)}, u32[]{:S(2)}, u32[]{:S(2)}) collective-permute-start(f32[1,136,384]{2,1,0:T(8,128)S(1)} %second1.1), channel_id=1, source_target_pairs={{0,1},{1,0},{2,3},{3,2},{4,5},{5,4},{6,7},{7,6},{8,9},{9,8},{10,11... | collective-permute-start | bytes 626696 | tf_op jit(solution)/shard_map/ppermute | solution.py:361
  60.8 9.8 %collective-permute-start.3 = (f32[2,136,512]{2,1,0:T(8,128)S(1)}, f32[2,136,512]{2,1,0:T(8,128)S(1)}, u32[]{:S(2)}, u32[]{:S(2)}) collective-permute-start(f32[2,136,512]{2,1,0:T(8,128)S(1)} %first.1.own1), channel_id=1, source_target_pairs={{0,1},{1,0},{2,3},{3,2},{4,5},{5,4},{6,7},{7,6},{8,9},{9,8},{10,11... | collective-permute-start | bytes 1671176 | tf_op jit(solution)/shard_map/ppermute | solution.py:361
  122.0 10.8 %collective-permute-start.8 = (f32[128,256]{1,0:T(8,128)S(1)}, f32[128,256]{1,0:T(8,128)S(1)}, u32[]{:S(2)}, u32[]{:S(2)}) collective-permute-start(f32[128,256]{1,0:T(8,128)S(1)} %get-tuple-element.19), channel_id=1, source_target_pairs={{0,32},{32,64},{64,96},{96,0},{128,160},{160,192},{192,224},{224,1... | collective-permute-start | bytes 393224 | tf_op jit(solution)/shard_map/ppermute | solution.py:391
  123.6 9.3 %collective-permute-start.9 = (f32[128,256]{1,0:T(8,128)S(1)}, f32[128,256]{1,0:T(8,128)S(1)}, u32[]{:S(2)}, u32[]{:S(2)}) collective-permute-start(f32[128,256]{1,0:T(8,128)S(1)} %get-tuple-element.18), channel_id=1, source_target_pairs={{0,224},{32,128},{64,160},{96,192},{128,96},{160,0},{192,32},{224,... | collective-permute-start | bytes 393224 | tf_op jit(solution)/shard_map/ppermute | solution.py:391
  125.0 13.8 %collective-permute-start.7 = (f32[128,1152]{1,0:T(8,128)S(1)}, f32[128,1152]{1,0:T(8,128)S(1)}, u32[]{:S(2)}, u32[]{:S(2)}) collective-permute-start(f32[128,1152]{1,0:T(8,128)S(1)} %bitcast.5), channel_id=1, source_target_pairs={{0,1},{1,0},{2,3},{3,2},{4,5},{5,4},{6,7},{7,6},{8,9},{9,8},{10,11... | collective-permute-start | bytes 1769480 | tf_op jit(solution)/shard_map/ppermute | solution.py:361
  127.6 8.1 %collective-permute-start.10 = (f32[128,256]{1,0:T(8,128)S(1)}, f32[128,256]{1,0:T(8,128)S(1)}, u32[]{:S(2)}, u32[]{:S(2)}) collective-permute-start(f32[128,256]{1,0:T(8,128)S(1)} %get-tuple-element.17), channel_id=1, source_target_pairs={{0,64},{32,96},{64,192},{96,224},{128,0},{160,32},{192,128},{224,1... | collective-permute-start | bytes 393224 | tf_op jit(solution)/shard_map/ppermute | solution.py:391
  128.2 9.7 %collective-permute-start.11 = (f32[128,128]{1,0:T(8,128)S(1)}, f32[128,128]{1,0:T(8,128)S(1)}, u32[]{:S(2)}, u32[]{:S(2)}) collective-permute-start(f32[128,128]{1,0:T(8,128)S(1)} %slice.19), channel_id=1, source_target_pairs={{0,192},{32,224},{64,128},{96,160},{128,64},{160,96},{192,0},{224,... | collective-permute-start | bytes 196616 | tf_op jit(solution)/shard_map/ppermute | solution.py:391
  137.9 2.3 %collective-permute-start.12 = (f32[128,896]{1,0:T(8,128)S(1)}, f32[128,896]{1,0:T(8,128)S(1)}, u32[]{:S(2)}, u32[]{:S(2)}) collective-permute-start(f32[128,896]{1,0:T(8,128)S(1)} %constant_dynamic-update-slice_fusion.own_swapped), channel_id=1, source_target_pairs={{0,1},{1,0},{2,3},{3,2},{4,5},{5,4},{6,7},{7,6},{8,9},{9,8},{10,11... | collective-permute-start | bytes 1376264 | tf_op jit(solution)/shard_map/ppermute | solution.py:361

commit v8 on v7

--- a/solution.py
+++ b/solution.py
@@ -43,13 +43,29 @@
     return [pl.BlockSpec(memory_space=pltpu.VMEM)] * n
 
 
-def branch_sums(ref, lane):
-    def add(k8, total):
-        at = pl.ds(pl.multiple_of(k8 * 8, 8), 8)
-        return total + ref[at, lane : lane + 128]
-
-    total = lax.fori_loop(0, KS // 8, add, jnp.zeros((8, 128), F32), unroll=8)
-    return jnp.sum(total, axis=0, keepdims=True)
+def row_sums(parts):
+    parts = parts + [jnp.zeros((8, 128), F32)] * (8 - len(parts))
+    sub = lax.broadcasted_iota(jnp.int32, (8, 128), 0)
+    for bit in (4, 2, 1):
+        first = (sub & bit) == 0
+        merged = []
+        for r in range(bit):
+            kept = jnp.where(first, parts[r], parts[r + bit])
+            other = jnp.where(first, parts[r + bit], parts[r])
+            if bit == 4:
+                moved = pltpu.roll(other, 4, 0)
+            else:
+                moved = jnp.where(first, pltpu.roll(other, 8 - bit, 0), pltpu.roll(other, bit, 0))
+            merged.append(kept + moved)
+        parts = merged
+    return parts[0]
+
+
+def branch_sums(read):
+    total = jnp.zeros((8, 128), F32)
+    for k8 in range(KS // 8):
+        total = total + read(slice(k8 * 8, k8 * 8 + 8))
+    return total
 
 
 def weigh_kernel(counts_hbm, totals_hbm, lengths_hbm, wt_ref, split_ref, col_ref, *scratch):
@@ -74,9 +90,11 @@
         middle = rest.astype(BF16)
         low = (rest - middle.astype(F32)).astype(BF16)
         split_ref[n] = jnp.concatenate([high, middle, low, jnp.zeros_like(low)], axis=1)
+    sums = row_sums(
+        [branch_sums(lambda at, h=h: wt_ref[at, h * 128 : h * 128 + 128]) for h in range(2)]
+    )
     for h in range(2):
-        sums = branch_sums(wt_ref, h * 128)
-        col_ref[h * 128 : (h + 1) * 128, :] = jnp.broadcast_to(sums, (128, 128)).T
+        col_ref[h * 128 : (h + 1) * 128, :] = jnp.broadcast_to(sums[h : h + 1], (128, 128)).T
 
 
 def weigh(counts, totals, lengths):
@@ -100,10 +118,9 @@
     )(counts, totals.reshape(1, ROWS), lengths.reshape(1, KS))
 
 
-def spread_call(name, n_blocks, columns, width, group, mass_row, side=None):
+def spread_call(name, n_blocks, columns, width, group, mass_row, half=None, side=None):
     pairs = group // 2
-    halves = 2 if side is None else 1
-    groups = halves * ROWS // 2 // group
+    groups = ROWS // 2 // group
 
     def kernel(split_ref, col_ref, *refs):
         blocks = refs[:n_blocks]
@@ -111,9 +128,12 @@
         core = lax.axis_index("branch") % 2
         y = lax.axis_index("blk") // 4
         if side is None:
-            base = 0
+            rows_half = half
         else:
-            base = (core if side == 0 else 1 - core) * groups
+            rows_half = core if side == 0 else 1 - core
+        base = rows_half * groups
+        cols = columns(rows_half, y)
+        n_cols = len(cols)
 
         part = lax.broadcasted_iota(jnp.int32, (128, 256), 0)
         lane = lax.broadcasted_iota(jnp.int32, (128, 256), 1)
@@ -132,26 +152,16 @@
                 return blocks[n][at, lane : lane + 128]
             return blocks[n][at, pl.ds(pl.multiple_of(lane, 128), 128)]
 
-        def columns_at(h):
-            return columns(h if side is None else base // groups, y)
-
-        for h in range(halves):
-            below = [jnp.zeros((1, 128), F32)] * mass_row
-            for n, lane in columns_at(h):
-                total = jnp.zeros((8, 128), F32)
-                for k8 in range(KS // 8):
-                    total = total + span(n, lane, slice(k8 * 8, k8 * 8 + 8))
-                below.append(jnp.sum(total, axis=0, keepdims=True))
-            below += [jnp.zeros((1, 128), F32)] * (8 - len(below))
-            out_ref[h, 128:136, 0:128] = jnp.concatenate(below, axis=0)
+        totals = [
+            branch_sums(lambda at, n=n, lane=lane: span(n, lane, at)) for n, lane in cols
+        ]
+        masses = row_sums([jnp.zeros((8, 128), F32)] * mass_row + totals)
+        out_ref[128:136, 0:128] = masses
 
         for q in range(pairs):
             broadcast_pair(even_ref, base, q)
 
         def one_group(g, now, later):
-            h = g * group // 128
-            cols = columns_at(h)
-            n_cols = len(cols)
             following = base + jnp.minimum(g + 1, groups - 1)
             steps = []
             if group == 8:
@@ -171,19 +181,13 @@
                     for j in range(n_cols):
                         acc[r * n_cols + j] += jnp.minimum(own, spans[j])
             for r0 in range(0, group, 8):
-                row = pl.multiple_of(g * group + r0 - h * 128, 8)
+                row = pl.multiple_of(g * group + r0, 8)
                 first = pl.multiple_of((base + g) * group + r0, 8)
                 own_mass = col_ref[pl.ds(first, 8), :]
                 for j in range(n_cols):
-                    mass = out_ref[h, 128 + mass_row + j : 129 + mass_row + j, 0:128]
-                    least = jnp.concatenate(
-                        [
-                            jnp.sum(acc[(r0 + r) * n_cols + j], axis=0, keepdims=True)
-                            for r in range(8)
-                        ],
-                        axis=0,
-                    )
-                    out_ref[h, pl.ds(row, 8), 128 * j : 128 * j + 128] = (
+                    mass = out_ref[128 + mass_row + j : 129 + mass_row + j, 0:128]
+                    least = row_sums([acc[(r0 + r) * n_cols + j] for r in range(8)])
+                    out_ref[pl.ds(row, 8), 128 * j : 128 * j + 128] = (
                         own_mass + mass - 2.0 * least
                     )
 
@@ -197,7 +201,7 @@
     def call(split, col, *blocks):
         return pl.pallas_call(
             kernel,
-            out_shape=jax.ShapeDtypeStruct((halves, 136, width), F32),
+            out_shape=jax.ShapeDtypeStruct((136, width), F32),
             in_specs=in_vmem(2 + n_blocks),
             out_specs=in_vmem(1)[0],
             scratch_shapes=[
@@ -207,7 +211,7 @@
             ],
             compiler_params=params(),
             cost_estimate=pl.CostEstimate(
-                flops=halves * width * 128 * KS * 250, bytes_accessed=4 << 20, transcendentals=0
+                flops=width * 128 * KS * 250, bytes_accessed=4 << 20, transcendentals=0
             ),
             name=name,
         )(split, col, *blocks)
@@ -223,6 +227,10 @@
     return [(0, 0), (0, 128), (1, 0), (1, 128)]
 
 
+def lower_columns(half, y):
+    return first_columns(half, y) + [(2, 128)]
+
+
 def second_columns(half, y):
     return [(0, 0), (0, 128), (1, (half ^ y) * 128)]
 
@@ -230,27 +238,48 @@
 DIRECT = 1152
 
 
-def pack_kernel(own0, got0, own1, got1, own2, got2, out_ref):
+def pack_kernel(*refs):
+    diagonal, upper, lower, second = [
+        (own, got) for own, got in zip(refs[:8:2], refs[1:8:2], strict=True)
+    ]
+    out_ref = refs[8]
     core = lax.axis_index("branch") % 2
-    lane = 0
-    masses = []
-    for own, got in ((own0, got0), (own1, got1), (own2, got2)):
-        half = core if own.shape[0] == 2 else 0
-        width = own.shape[2]
-        both = own[half, 0:128, :] + got[half, 0:128, :]
-        out_ref[:, :, lane : lane + width] = both.reshape(16, 8, width)
-        masses.append(own[half, 128:136, 0:128] + got[half, 128:136, 0:128])
-        lane += width
-    for block in (masses[0] + masses[1], masses[2]):
+
+    def both(parts, rows=slice(0, 128), lanes=slice(None)):
+        return parts[0][rows, lanes] + parts[1][rows, lanes]
+
+    def put(lane, value):
+        out_ref[:, :, lane : lane + value.shape[1]] = value.reshape(16, 8, -1)
+
+    def put_masses(lane, block):
         out_ref[:, :, lane : lane + 128] = jnp.broadcast_to(block[None], (16, 8, 128))
-        lane += 128
+
+    below, masses = slice(128, 136), slice(0, 128)
+
+    @pl.when(core == 0)
+    def _():
+        put(0, both(diagonal))
+        put(256, both(upper))
+        put_masses(DIRECT, both(diagonal, below, masses) + both(upper, below, masses))
+
+    @pl.when(core == 1)
+    def _():
+        put(0, jnp.zeros((128, 128), F32))
+        put(128, both(lower, lanes=slice(512, 640)))
+        put(256, both(lower, lanes=slice(0, 512)))
+        block = both(lower, below, masses)
+        none = jnp.zeros((1, 128), F32)
+        put_masses(DIRECT, jnp.concatenate([none, block[6:7], block[2:6], none, none]))
+
+    put(768, both(second))
+    put_masses(DIRECT + 128, both(second, below, masses))
 
 
 def pack(*parts):
     return pl.pallas_call(
         pack_kernel,
         out_shape=jax.ShapeDtypeStruct((16, 8, DIRECT + 256), F32),
-        in_specs=in_vmem(6),
+        in_specs=in_vmem(8),
         out_specs=in_vmem(1)[0],
         compiler_params=params(),
         name="pack",
@@ -325,9 +354,15 @@
 
     for half, ref in ((core, own), (1 - core, other)):
         rows = rows_of(half)
-        for slot in range(4):
+        store(ref.at[:, 128:256], rows, columns(0, 1))
+        for slot in range(1, 4):
             store(ref.at[:, slot * ROWS : (slot + 1) * ROWS], rows, columns(slot))
         store(ref.at[:, 4 * ROWS : DIRECT], rows, columns(4, half ^ y))
+    upper = jnp.where(core == 0, own[:, 0:256], other[:, 0:256])
+    turned_ref[0, 3, 128:256] = upper[:, 0:128]
+    turned_ref[1, 3, 128:256] = upper[:, 128:256].T
+    for half in range(2):
+        store(turned_ref.at[half, 3, 128:256], rows_of(half), columns(0, 0))
     for side, half, ref in ((0, core, own_swapped), (1, 1 - core, other_swapped)):
         for n, slot in enumerate((5, 6, 7)):
             turned_ref[side, n] = ref[:, n * ROWS : (n + 1) * ROWS].T
@@ -346,7 +381,7 @@
         out_specs=pl.BlockSpec(memory_space=pl.ANY),
         scratch_shapes=[
             pltpu.VMEM((2, 4, ROWS, 128), F32),
-            pltpu.SemaphoreType.DMA((18,)),
+            pltpu.SemaphoreType.DMA((20,)),
         ],
         compiler_params=params(),
         name="assemble",
@@ -367,23 +402,27 @@
 
     wt, split, mass_col = weigh(counts, totals, lengths)
     got = [from_partner(wt, n) for n in range(2)]
-    diagonal = spread_call("diagonal", 1, diagonal_columns, 256, 16, 0)
-    first = spread_call("first", 2, first_columns, 512, 8, 2)
-    second = [spread_call(f"second{s}", 2, second_columns, 384, 8, 0, s) for s in range(2)]
+    diagonal = spread_call("diagonal", 1, diagonal_columns, 256, 16, 0, half=0)
+    upper = spread_call("upper", 2, first_columns, 512, 8, 2, half=0)
+    lower = spread_call("lower", 3, lower_columns, 640, 8, 2, half=1)
+    second = [spread_call(f"second{s}", 2, second_columns, 384, 8, 0, side=s) for s in range(2)]
+
+    def after(v, *others):
+        return lax.optimization_barrier((v, *others))[0]
 
     part0 = diagonal(split, mass_col, wt)
-    later = lax.optimization_barrier((wt, part0))[0]
+    later = after(wt, part0)
     got += [from_partner(later, n) for n in (2, 3)]
-    received0 = other_core(part0)
-    part1 = first(split, mass_col, got[0], got[1])
-    received1 = other_core(part1)
-    third = lax.optimization_barrier((got[2], part1))[0]
-    sent2 = second[1](split, mass_col, third, got[3])
-    received2 = other_core(sent2)
-    third = lax.optimization_barrier((third, sent2))[0]
-    part2 = second[0](split, mass_col, third, got[3])
-
-    shards = over_chips(pack(part0, received0, part1, received1, part2, received2))
+    part1 = upper(split, mass_col, *got[:2])
+    part2 = lower(split, mass_col, after(got[0], part1), got[1], wt)
+    third = after(got[2], part2)
+    sent3 = second[1](split, mass_col, third, got[3])
+    part3 = second[0](split, mass_col, after(third, sent3), got[3])
+
+    parts = []
+    for own, sent in ((part0, part0), (part1, part1), (part2, part2), (part3, sent3)):
+        parts += [own, other_core(sent)]
+    shards = over_chips(pack(*parts))
     own = over_chips(normalise(shards)).reshape(128, DIRECT)
     swapped = []
     for n in range(4):

time: 142 us -> 162 us (1.14)
  starting transfers between devices: 24.9 us -> 46.2 us
  Pallas kernels: 56.7 us -> 52 us
  waiting for transfers between devices: 6.39 us -> 9.15 us
    ppermute x5 -> x6, starting transfers between devices: 6.23 us -> 20.4 us  [other_core(): return lax.ppermute(v, 'branch', [(i, i ^ 1) for i in range(32)])]
    ppermute x4, starting transfers between devices: 8.14 us -> 15.2 us  [on_device(): lax.ppermute(tile, 'blk', [(b, PARTNERS[n][b]) for b in range(BLOCKS)])]
    pallas_call x4 -> x5, Pallas kernels: 53.7 us -> 49.3 us  [call(): pl.pallas_call(kernel, out_shape=jax.ShapeDtypeStruct((136, width), F32),...]
    ppermute x4, waiting for transfers between devices: 4.93 us -> 7.36 us  [on_device(): lax.ppermute(tile, 'blk', [(b, PARTNERS[n][b]) for b in range(BLOCKS)])]
  transfers between devices with their start and end apart: 13 -> 14, of which waited for: 3 -> 4; matrix products, arithmetic and copies ran while one was open for 0% -> 0% of each run, Pallas kernels for 38% -> 30%
where the time goes in v8:
time: 162 us
  Pallas kernels  52 us (32%)
  blocking collectives  52 us (32%)
  starting transfers between devices  46.2 us (29%)
  waiting for transfers between devices  9.15 us (6%)
  local copies, waits for them, and re-layouts  2.47 us (2%)
    all_to_all x2, blocking collectives, over_chips(): return lax.all_to_all(v, 'branch', 0, 0, axis_index_groups=chips)  52 us
    pallas_call x5, Pallas kernels, call(): pl.pallas_call(kernel, out_shape=jax.ShapeDtypeStruct((136, width), F32),...  49.3 us
    ppermute x6, starting transfers between devices, other_core(): return lax.ppermute(v, 'branch', [(i, i ^ 1) for i in range(32)])  20.4 us
    ppermute x4, starting transfers between devices, on_device(): lax.ppermute(tile, 'blk', [(b, PARTNERS[n][b]) for b in range(BLOCKS)])  15.2 us
    ppermute x4, starting transfers between devices, from_partner(): return lax.ppermute(v, 'blk', [(PARTNERS[n][b], b) for b in range(BLOCKS)])  10.5 us
    ppermute x4, waiting for transfers between devices, on_device(): lax.ppermute(tile, 'blk', [(b, PARTNERS[n][b]) for b in range(BLOCKS)])  7.36 us
  transfers between devices with their start and end apart: 14, of which 4 were waited for; matrix products, arithmetic and copies ran while one was open for 0% of the time, Pallas kernels for 30%

profile of v8, /device:TPU:1, one launch (start us, length us, event | category | flops | bytes accessed | tf_op | source)
XLA Modules:
  0.0 162.0 jit_solution(4355086213979221156)
XLA Ops:
  0.0 1.0 copy-done
  1.0 0.7 copy-done.1
  1.7 0.7 copy-done.2
  2.4 0.9 weigh.1
  3.4 3.4 %collective-permute-start.1 = (f32[512,256]{1,0:T(8,128)S(1)}, f32[512,256]{1,0:T(8,128)S(1)}, u32[]{:S(2)}, u32[]{:S(2)}) collective-permute-start(f32[512,256]{1,0:T(8,128)S(1)} %get-tuple-element.16.refs_0_.refs_2_), channel_id=1, source_target_pairs={{32,0},{64,32},{96,64},{0,96},{160,128},{192,160},{224,192},{128,2... | collective-permute-start | bytes 1572872 | tf_op jit(solution)/shard_map/ppermute | solution.py:393
  6.7 1.6 collective-permute-start.2
  8.4 6.8 %diagonal.1.refs_0_ = f32[136,256]{1,0:T(8,128)S(1)} custom-call(bf16[8,512,128]{2,1,0:T(8,128)(2,1)S(1)} %get-tuple-element.12.split_ref, f32[256,128]{1,0:T(8,128)S(1)} %get-tuple-element.13.col_ref, f32[512,256]{1,0:T(8,128)S(1)} %get-tuple-element.16.refs_0_.refs_2_), custom_call_target="tpu_custom_call" | custom-call | flops 4194304000 | bytes 4194304 | tf_op jit(solution)/shard_map/diagonal/pallas_call | solution.py:202
  15.2 1.4 collective-permute-start.5
  16.6 4.1 %collective-permute-start.6 = (f32[512,256]{1,0:T(8,128)S(1)}, f32[512,256]{1,0:T(8,128)S(1)}, u32[]{:S(2)}, u32[]{:S(2)}) collective-permute-start(f32[512,256]{1,0:T(8,128)S(1)} %get-tuple-element.16.refs_0_.refs_2_), channel_id=1, source_target_pairs={{192,0},{224,32},{128,64},{160,96},{64,128},{96,160},{0,192},{32,2... | collective-permute-start | bytes 1572872 | tf_op jit(solution)/shard_map/ppermute | solution.py:393
  20.7 1.8 %collective-permute-start = (f32[136,256]{1,0:T(8,128)S(1)}, f32[136,256]{1,0:T(8,128)S(1)}, u32[]{:S(2)}, u32[]{:S(2)}) collective-permute-start(f32[136,256]{1,0:T(8,128)S(1)} %diagonal.1.refs_0_), channel_id=1, source_target_pairs={{0,1},{1,0},{2,3},{3,2},{4,5},{5,4},{6,7},{7,6},{8,9},{9,8},{10,11... | collective-permute-start | bytes 417800 | tf_op jit(solution)/shard_map/ppermute | solution.py:396
  22.8 10.9 %upper.1.refs_2_ = f32[136,512]{1,0:T(8,128)S(1)} custom-call(bf16[8,512,128]{2,1,0:T(8,128)(2,1)S(1)} %get-tuple-element.12.split_ref, f32[256,128]{1,0:T(8,128)S(1)} %get-tuple-element.13.col_ref, f32[512,256]{1,0:T(8,128)S(1)} %collective-permute-done.1.refs_0_, f32[512,256]{1,0:T(8,128)S(1)} %collective-permute-done.2.refs_1_), custom_call_target="tpu_custom_call" | custom-call | flops 8388608000 | bytes 4194304 | tf_op jit(solution)/shard_map/upper/pallas_call | solution.py:202
  33.7 13.4 %lower.1.refs_4_ = f32[136,640]{1,0:T(8,128)S(1)} custom-call(bf16[8,512,128]{2,1,0:T(8,128)(2,1)S(1)} %get-tuple-element.12.split_ref, f32[256,128]{1,0:T(8,128)S(1)} %get-tuple-element.13.col_ref, f32[512,256]{1,0:T(8,128)S(1)} %collective-permute-done.1.refs_0_, f32[512,256]{1,0:T(8,128)S(1)} %collective-permute-done.2.refs_1_, ...), custom_call_target="tpu_custom_call" | custom-call | flops 10485760000 | bytes 4194304 | tf_op jit(solution)/shard_map/lower/pallas_call | solution.py:202
  47.1 8.8 %second1.1 = f32[136,384]{1,0:T(8,128)S(1)} custom-call(bf16[8,512,128]{2,1,0:T(8,128)(2,1)S(1)} %get-tuple-element.12.split_ref, f32[256,128]{1,0:T(8,128)S(1)} %get-tuple-element.13.col_ref, f32[512,256]{1,0:T(8,128)S(1)} %collective-permute-done.5.refs_0_, f32[512,256]{1,0:T(8,128)S(1)} %collective-permute-done.6.refs_1_), custom_call_target="tpu_custom_call" | custom-call | flops 6291456000 | bytes 4194304 | tf_op jit(solution)/shard_map/second1/pallas_call | solution.py:202
  55.9 13.9 %collective-permute-start.7 = (f32[136,384]{1,0:T(8,128)S(1)}, f32[136,384]{1,0:T(8,128)S(1)}, u32[]{:S(2)}, u32[]{:S(2)}) collective-permute-start(f32[136,384]{1,0:T(8,128)S(1)} %second1.1), channel_id=1, source_target_pairs={{0,1},{1,0},{2,3},{3,2},{4,5},{5,4},{6,7},{7,6},{8,9},{9,8},{10,11... | collective-permute-start | bytes 626696 | tf_op jit(solution)/shard_map/ppermute | solution.py:396
  70.4 9.4 %second0.1.refs_6_ = f32[136,384]{1,0:T(8,128)S(1)} custom-call(bf16[8,512,128]{2,1,0:T(8,128)(2,1)S(1)} %get-tuple-element.12.split_ref, f32[256,128]{1,0:T(8,128)S(1)} %get-tuple-element.13.col_ref, f32[512,256]{1,0:T(8,128)S(1)} %collective-permute-done.5.refs_0_, f32[512,256]{1,0:T(8,128)S(1)} %collective-permute-done.6.refs_1_), custom_call_target="tpu_custom_call" | custom-call | flops 6291456000 | bytes 4194304 | tf_op jit(solution)/shard_map/second0/pallas_call | solution.py:202
  79.9 30.8 %all_to_all.10.shards_ref = f32[16,8,1408]{2,1,0:T(8,128)S(1)} all-to-all(f32[16,8,1408]{2,1,0:T(8,128)S(1)} %pack.1), channel_id=1, replica_groups={{0,2,4,6,8,10,12,14,16,18,20,22,24,26,28,30},{1,3,5,7,9,11,13,15,17,19,..., dimensions={0} | all-to-all | bytes 1441792 | tf_op jit(solution)/shard_map/all_to_all | solution.py:401
  110.8 21.2 %all_to_all.11 = f32[16,8,1152]{2,1,0:T(8,128)S(1)} all-to-all(f32[16,8,1152]{2,1,0:T(8,128)S(1)} %normalise.1), channel_id=1, replica_groups={{0,2,4,6,8,10,12,14,16,18,20,22,24,26,28,30},{1,3,5,7,9,11,13,15,17,19,..., dimensions={0} | all-to-all | bytes 1179648 | tf_op jit(solution)/shard_map/all_to_all | solution.py:401
  132.1 15.1 %collective-permute-start.10 = (f32[128,256]{1,0:T(8,128)S(1)}, f32[128,256]{1,0:T(8,128)S(1)}, u32[]{:S(2)}, u32[]{:S(2)}) collective-permute-start(f32[128,256]{1,0:T(8,128)S(1)} %get-tuple-element.20), channel_id=1, source_target_pairs={{0,224},{32,128},{64,160},{96,192},{128,96},{160,0},{192,32},{224,... | collective-permute-start | bytes 393224 | tf_op jit(solution)/shard_map/ppermute | solution.py:430
  147.3 2.7 %collective-permute-start.8 = (f32[128,1152]{1,0:T(8,128)S(1)}, f32[128,1152]{1,0:T(8,128)S(1)}, u32[]{:S(2)}, u32[]{:S(2)}) collective-permute-start(f32[128,1152]{1,0:T(8,128)S(1)} %bitcast.5), channel_id=1, source_target_pairs={{0,1},{1,0},{2,3},{3,2},{4,5},{5,4},{6,7},{7,6},{8,9},{9,8},{10,11... | collective-permute-start | bytes 1769480 | tf_op jit(solution)/shard_map/ppermute | solution.py:396
  150.0 6.5 %collective-permute-done.11 = f32[128,256]{1,0:T(8,128)S(1)} collective-permute-done((f32[128,256]{1,0:T(8,128)S(1)}, f32[128,256]{1,0:T(8,128)S(1)}, u32[]{:S(2)}, u32[]{:S(2)}) %collective-permute-start.11) | collective-permute-done | bytes 131104 | tf_op jit(solution)/shard_map/ppermute | solution.py:430
  156.5 0.9 collective-permute-done.12
  157.4 1.5 collective-permute-start.13
  158.9 1.4 collective-permute-done.13.other_swapped
  160.4 1.5 assemble.1
  (27 shorter events, 1.3 us)
Async XLA Ops:
  0.0 1.0 copy-start
  1.0 0.7 copy-start.1
  1.7 0.7 copy-start.2
  3.4 19.1 %collective-permute-start.1 = (f32[512,256]{1,0:T(8,128)S(1)}, f32[512,256]{1,0:T(8,128)S(1)}, u32[]{:S(2)}, u32[]{:S(2)}) collective-permute-start(f32[512,256]{1,0:T(8,128)S(1)} %get-tuple-element.16.refs_0_.refs_2_), channel_id=1, source_target_pairs={{32,0},{64,32},{96,64},{0,96},{160,128},{192,160},{224,192},{128,2... | collective-permute-start | bytes 1572872 | tf_op jit(solution)/shard_map/ppermute | solution.py:393
  6.7 16.1 %collective-permute-start.2 = (f32[512,256]{1,0:T(8,128)S(1)}, f32[512,256]{1,0:T(8,128)S(1)}, u32[]{:S(2)}, u32[]{:S(2)}) collective-permute-start(f32[512,256]{1,0:T(8,128)S(1)} %get-tuple-element.16.refs_0_.refs_2_), channel_id=1, source_target_pairs={{224,0},{128,32},{160,64},{192,96},{96,128},{0,160},{32,192},{64,2... | collective-permute-start | bytes 1572872 | tf_op jit(solution)/shard_map/ppermute | solution.py:393
  15.2 31.9 %collective-permute-start.5 = (f32[512,256]{1,0:T(8,128)S(1)}, f32[512,256]{1,0:T(8,128)S(1)}, u32[]{:S(2)}, u32[]{:S(2)}) collective-permute-start(f32[512,256]{1,0:T(8,128)S(1)} %get-tuple-element.16.refs_0_.refs_2_), channel_id=1, source_target_pairs={{64,0},{96,32},{192,64},{224,96},{0,128},{32,160},{128,192},{160,2... | collective-permute-start | bytes 1572872 | tf_op jit(solution)/shard_map/ppermute | solution.py:393
  16.6 30.5 %collective-permute-start.6 = (f32[512,256]{1,0:T(8,128)S(1)}, f32[512,256]{1,0:T(8,128)S(1)}, u32[]{:S(2)}, u32[]{:S(2)}) collective-permute-start(f32[512,256]{1,0:T(8,128)S(1)} %get-tuple-element.16.refs_0_.refs_2_), channel_id=1, source_target_pairs={{192,0},{224,32},{128,64},{160,96},{64,128},{96,160},{0,192},{32,2... | collective-permute-start | bytes 1572872 | tf_op jit(solution)/shard_map/ppermute | solution.py:393
  20.7 59.0 %collective-permute-start = (f32[136,256]{1,0:T(8,128)S(1)}, f32[136,256]{1,0:T(8,128)S(1)}, u32[]{:S(2)}, u32[]{:S(2)}) collective-permute-start(f32[136,256]{1,0:T(8,128)S(1)} %diagonal.1.refs_0_), channel_id=1, source_target_pairs={{0,1},{1,0},{2,3},{3,2},{4,5},{5,4},{6,7},{7,6},{8,9},{9,8},{10,11... | collective-permute-start | bytes 417800 | tf_op jit(solution)/shard_map/ppermute | solution.py:396
  55.9 23.8 %collective-permute-start.7 = (f32[136,384]{1,0:T(8,128)S(1)}, f32[136,384]{1,0:T(8,128)S(1)}, u32[]{:S(2)}, u32[]{:S(2)}) collective-permute-start(f32[136,384]{1,0:T(8,128)S(1)} %second1.1), channel_id=1, source_target_pairs={{0,1},{1,0},{2,3},{3,2},{4,5},{5,4},{6,7},{7,6},{8,9},{9,8},{10,11... | collective-permute-start | bytes 626696 | tf_op jit(solution)/shard_map/ppermute | solution.py:396
  69.8 9.9 %collective-permute-start.4 = (f32[136,640]{1,0:T(8,128)S(1)}, f32[136,640]{1,0:T(8,128)S(1)}, u32[]{:S(2)}, u32[]{:S(2)}) collective-permute-start(f32[136,640]{1,0:T(8,128)S(1)} %lower.1.refs_4_), channel_id=1, source_target_pairs={{0,1},{1,0},{2,3},{3,2},{4,5},{5,4},{6,7},{7,6},{8,9},{9,8},{10,11... | collective-permute-start | bytes 1044488 | tf_op jit(solution)/shard_map/ppermute | solution.py:396
  70.0 9.8 %collective-permute-start.3 = (f32[136,512]{1,0:T(8,128)S(1)}, f32[136,512]{1,0:T(8,128)S(1)}, u32[]{:S(2)}, u32[]{:S(2)}) collective-permute-start(f32[136,512]{1,0:T(8,128)S(1)} %upper.1.refs_2_), channel_id=1, source_target_pairs={{0,1},{1,0},{2,3},{3,2},{4,5},{5,4},{6,7},{7,6},{8,9},{9,8},{10,11... | collective-permute-start | bytes 835592 | tf_op jit(solution)/shard_map/ppermute | solution.py:396
  132.0 17.9 %collective-permute-start.9 = (f32[128,256]{1,0:T(8,128)S(1)}, f32[128,256]{1,0:T(8,128)S(1)}, u32[]{:S(2)}, u32[]{:S(2)}) collective-permute-start(f32[128,256]{1,0:T(8,128)S(1)} %get-tuple-element.21), channel_id=1, source_target_pairs={{0,32},{32,64},{64,96},{96,0},{128,160},{160,192},{192,224},{224,1... | collective-permute-start | bytes 393224 | tf_op jit(solution)/shard_map/ppermute | solution.py:430
  132.1 17.9 %collective-permute-start.10 = (f32[128,256]{1,0:T(8,128)S(1)}, f32[128,256]{1,0:T(8,128)S(1)}, u32[]{:S(2)}, u32[]{:S(2)}) collective-permute-start(f32[128,256]{1,0:T(8,128)S(1)} %get-tuple-element.20), channel_id=1, source_target_pairs={{0,224},{32,128},{64,160},{96,192},{128,96},{160,0},{192,32},{224,... | collective-permute-start | bytes 393224 | tf_op jit(solution)/shard_map/ppermute | solution.py:430
  147.3 11.7 %collective-permute-start.8 = (f32[128,1152]{1,0:T(8,128)S(1)}, f32[128,1152]{1,0:T(8,128)S(1)}, u32[]{:S(2)}, u32[]{:S(2)}) collective-permute-start(f32[128,1152]{1,0:T(8,128)S(1)} %bitcast.5), channel_id=1, source_target_pairs={{0,1},{1,0},{2,3},{3,2},{4,5},{5,4},{6,7},{7,6},{8,9},{9,8},{10,11... | collective-permute-start | bytes 1769480 | tf_op jit(solution)/shard_map/ppermute | solution.py:396
  150.0 6.6 %collective-permute-start.11 = (f32[128,256]{1,0:T(8,128)S(1)}, f32[128,256]{1,0:T(8,128)S(1)}, u32[]{:S(2)}, u32[]{:S(2)}) collective-permute-start(f32[128,256]{1,0:T(8,128)S(1)} %get-tuple-element.19), channel_id=1, source_target_pairs={{0,64},{32,96},{64,192},{96,224},{128,0},{160,32},{192,128},{224,1... | collective-permute-start | bytes 393224 | tf_op jit(solution)/shard_map/ppermute | solution.py:430
  150.0 7.4 %collective-permute-start.12 = (f32[128,128]{1,0:T(8,128)S(1)}, f32[128,128]{1,0:T(8,128)S(1)}, u32[]{:S(2)}, u32[]{:S(2)}) collective-permute-start(f32[128,128]{1,0:T(8,128)S(1)} %slice.19), channel_id=1, source_target_pairs={{0,192},{32,224},{64,128},{96,160},{128,64},{160,96},{192,0},{224,... | collective-permute-start | bytes 196616 | tf_op jit(solution)/shard_map/ppermute | solution.py:430
  157.4 3.0 %collective-permute-start.13 = (f32[128,896]{1,0:T(8,128)S(1)}, f32[128,896]{1,0:T(8,128)S(1)}, u32[]{:S(2)}, u32[]{:S(2)}) collective-permute-start(f32[128,896]{1,0:T(8,128)S(1)} %constant_dynamic-update-slice_fusion.own_swapped), channel_id=1, source_target_pairs={{0,1},{1,0},{2,3},{3,2},{4,5},{5,4},{6,7},{7,6},{8,9},{9,8},{10,11... | collective-permute-start | bytes 1376264 | tf_op jit(solution)/shard_map/ppermute | solution.py:396

commit v9 on v7

--- a/solution.py
+++ b/solution.py
@@ -43,13 +43,29 @@
     return [pl.BlockSpec(memory_space=pltpu.VMEM)] * n
 
 
-def branch_sums(ref, lane):
-    def add(k8, total):
-        at = pl.ds(pl.multiple_of(k8 * 8, 8), 8)
-        return total + ref[at, lane : lane + 128]
-
-    total = lax.fori_loop(0, KS // 8, add, jnp.zeros((8, 128), F32), unroll=8)
-    return jnp.sum(total, axis=0, keepdims=True)
+def row_sums(parts):
+    parts = parts + [jnp.zeros((8, 128), F32)] * (8 - len(parts))
+    sub = lax.broadcasted_iota(jnp.int32, (8, 128), 0)
+    for bit in (4, 2, 1):
+        first = (sub & bit) == 0
+        merged = []
+        for r in range(bit):
+            kept = jnp.where(first, parts[r], parts[r + bit])
+            other = jnp.where(first, parts[r + bit], parts[r])
+            if bit == 4:
+                moved = pltpu.roll(other, 4, 0)
+            else:
+                moved = jnp.where(first, pltpu.roll(other, 8 - bit, 0), pltpu.roll(other, bit, 0))
+            merged.append(kept + moved)
+        parts = merged
+    return parts[0]
+
+
+def branch_sums(read):
+    total = jnp.zeros((8, 128), F32)
+    for k8 in range(KS // 8):
+        total = total + read(slice(k8 * 8, k8 * 8 + 8))
+    return total
 
 
 def weigh_kernel(counts_hbm, totals_hbm, lengths_hbm, wt_ref, split_ref, col_ref, *scratch):
@@ -74,9 +90,11 @@
         middle = rest.astype(BF16)
         low = (rest - middle.astype(F32)).astype(BF16)
         split_ref[n] = jnp.concatenate([high, middle, low, jnp.zeros_like(low)], axis=1)
+    sums = row_sums(
+        [branch_sums(lambda at, h=h: wt_ref[at, h * 128 : h * 128 + 128]) for h in range(2)]
+    )
     for h in range(2):
-        sums = branch_sums(wt_ref, h * 128)
-        col_ref[h * 128 : (h + 1) * 128, :] = jnp.broadcast_to(sums, (128, 128)).T
+        col_ref[h * 128 : (h + 1) * 128, :] = jnp.broadcast_to(sums[h : h + 1], (128, 128)).T
 
 
 def weigh(counts, totals, lengths):
@@ -136,14 +154,12 @@
             return columns(h if side is None else base // groups, y)
 
         for h in range(halves):
-            below = [jnp.zeros((1, 128), F32)] * mass_row
-            for n, lane in columns_at(h):
-                total = jnp.zeros((8, 128), F32)
-                for k8 in range(KS // 8):
-                    total = total + span(n, lane, slice(k8 * 8, k8 * 8 + 8))
-                below.append(jnp.sum(total, axis=0, keepdims=True))
-            below += [jnp.zeros((1, 128), F32)] * (8 - len(below))
-            out_ref[h, 128:136, 0:128] = jnp.concatenate(below, axis=0)
+            totals = [
+                branch_sums(lambda at, n=n, lane=lane: span(n, lane, at))
+                for n, lane in columns_at(h)
+            ]
+            masses = row_sums([jnp.zeros((8, 128), F32)] * mass_row + totals)
+            out_ref[h, 128:136, 0:128] = masses
 
         for q in range(pairs):
             broadcast_pair(even_ref, base, q)
@@ -176,13 +192,7 @@
                 own_mass = col_ref[pl.ds(first, 8), :]
                 for j in range(n_cols):
                     mass = out_ref[h, 128 + mass_row + j : 129 + mass_row + j, 0:128]
-                    least = jnp.concatenate(
-                        [
-                            jnp.sum(acc[(r0 + r) * n_cols + j], axis=0, keepdims=True)
-                            for r in range(8)
-                        ],
-                        axis=0,
-                    )
+                    least = row_sums([acc[(r0 + r) * n_cols + j] for r in range(8)])
                     out_ref[h, pl.ds(row, 8), 128 * j : 128 * j + 128] = (
                         own_mass + mass - 2.0 * least
                     )

time: 142 us -> 140 us (0.986)
  Pallas kernels: 56.7 us -> 55 us
  transfers between devices with their start and end apart: 13 -> 13, of which waited for: 3 -> 3; matrix products, arithmetic and copies ran while one was open for 0% -> 0% of each run, Pallas kernels for 38% -> 37%
where the time goes in v9:
time: 140 us
  Pallas kernels  55 us (39%)
  blocking collectives  51 us (36%)
  starting transfers between devices  25 us (18%)
  waiting for transfers between devices  6.39 us (5%)
  local copies, waits for them, and re-layouts  2.47 us (2%)
    pallas_call x4, Pallas kernels, call(): pl.pallas_call(kernel, out_shape=jax.ShapeDtypeStruct((halves, 136, width...  52.4 us
    all_to_all x2, blocking collectives, over_chips(): return lax.all_to_all(v, 'branch', 0, 0, axis_index_groups=chips)  51 us
    ppermute x4, starting transfers between devices, from_partner(): return lax.ppermute(v, 'blk', [(PARTNERS[n][b], b) for b in range(BLOCKS)])  10.5 us
    ppermute x4, starting transfers between devices, on_device(): lax.ppermute(tile, 'blk', [(b, PARTNERS[n][b]) for b in range(BLOCKS)])  8.23 us
    ppermute x5, starting transfers between devices, other_core(): return lax.ppermute(v, 'branch', [(i, i ^ 1) for i in range(32)])  6.29 us
    ppermute x4, waiting for transfers between devices, on_device(): lax.ppermute(tile, 'blk', [(b, PARTNERS[n][b]) for b in range(BLOCKS)])  4.93 us
  transfers between devices with their start and end apart: 13, of which 3 were waited for; matrix products, arithmetic and copies ran while one was open for 0% of the time, Pallas kernels for 37%

profile of v9, /device:TPU:1, one launch (start us, length us, event | category | flops | bytes accessed | tf_op | source)
XLA Modules:
  0.0 140.2 jit_solution(3416376658696391747)
XLA Ops:
  0.0 1.0 copy-done
  1.0 0.7 copy-done.1
  2.4 0.9 weigh.1
  3.4 3.4 %collective-permute-start.1 = (f32[512,256]{1,0:T(8,128)S(1)}, f32[512,256]{1,0:T(8,128)S(1)}, u32[]{:S(2)}, u32[]{:S(2)}) collective-permute-start(f32[512,256]{1,0:T(8,128)S(1)} %get-tuple-element.14.refs_0_), channel_id=1, source_target_pairs={{32,0},{64,32},{96,64},{0,96},{160,128},{192,160},{224,192},{128,2... | collective-permute-start | bytes 1572872 | tf_op jit(solution)/shard_map/ppermute | solution.py:368
  6.7 1.6 %collective-permute-start.2 = (f32[512,256]{1,0:T(8,128)S(1)}, f32[512,256]{1,0:T(8,128)S(1)}, u32[]{:S(2)}, u32[]{:S(2)}) collective-permute-start(f32[512,256]{1,0:T(8,128)S(1)} %get-tuple-element.14.refs_0_), channel_id=1, source_target_pairs={{224,0},{128,32},{160,64},{192,96},{96,128},{0,160},{32,192},{64,2... | collective-permute-start | bytes 1572872 | tf_op jit(solution)/shard_map/ppermute | solution.py:368
  8.4 12.9 %diagonal.1.own0 = f32[2,136,256]{2,1,0:T(8,128)S(1)} custom-call(bf16[8,512,128]{2,1,0:T(8,128)(2,1)S(1)} %get-tuple-element.11.split_ref, f32[256,128]{1,0:T(8,128)S(1)} %get-tuple-element.12.col_ref, f32[512,256]{1,0:T(8,128)S(1)} %get-tuple-element.14.refs_0_), custom_call_target="tpu_custom_call" | custom-call | flops 8388608000 | bytes 4194304 | tf_op jit(solution)/shard_map/diagonal/pallas_call | solution.py:208
  21.3 1.4 collective-permute-start.4
  22.7 4.1 %collective-permute-start.5 = (f32[512,256]{1,0:T(8,128)S(1)}, f32[512,256]{1,0:T(8,128)S(1)}, u32[]{:S(2)}, u32[]{:S(2)}) collective-permute-start(f32[512,256]{1,0:T(8,128)S(1)} %get-tuple-element.14.refs_0_), channel_id=1, source_target_pairs={{192,0},{224,32},{128,64},{160,96},{64,128},{96,160},{0,192},{32,2... | collective-permute-start | bytes 1572872 | tf_op jit(solution)/shard_map/ppermute | solution.py:368
  26.8 1.8 %collective-permute-start = (f32[2,136,256]{2,1,0:T(8,128)S(1)}, f32[2,136,256]{2,1,0:T(8,128)S(1)}, u32[]{:S(2)}, u32[]{:S(2)}) collective-permute-start(f32[2,136,256]{2,1,0:T(8,128)S(1)} %diagonal.1.own0), channel_id=1, source_target_pairs={{0,1},{1,0},{2,3},{3,2},{4,5},{5,4},{6,7},{7,6},{8,9},{9,8},{10,11... | collective-permute-start | bytes 835592 | tf_op jit(solution)/shard_map/ppermute | solution.py:371
  28.6 21.3 %first.1.own1 = f32[2,136,512]{2,1,0:T(8,128)S(1)} custom-call(bf16[8,512,128]{2,1,0:T(8,128)(2,1)S(1)} %get-tuple-element.11.split_ref, f32[256,128]{1,0:T(8,128)S(1)} %get-tuple-element.12.col_ref, f32[512,256]{1,0:T(8,128)S(1)} %collective-permute-done.1.refs_0_, f32[512,256]{1,0:T(8,128)S(1)} %collective-permute-done.2.refs_1_), custom_call_target="tpu_custom_call" | custom-call | flops 16777216000 | bytes 4194304 | tf_op jit(solution)/shard_map/first/pallas_call | solution.py:208
  49.9 8.8 %second1.1 = f32[1,136,384]{2,1,0:T(8,128)S(1)} custom-call(bf16[8,512,128]{2,1,0:T(8,128)(2,1)S(1)} %get-tuple-element.11.split_ref, f32[256,128]{1,0:T(8,128)S(1)} %get-tuple-element.12.col_ref, f32[512,256]{1,0:T(8,128)S(1)} %collective-permute-done.4.refs_0_, f32[512,256]{1,0:T(8,128)S(1)} %collective-permute-done.5.refs_1_), custom_call_target="tpu_custom_call" | custom-call | flops 6291456000 | bytes 4194304 | tf_op jit(solution)/shard_map/second1/pallas_call | solution.py:208
  59.7 9.4 %second0.1.own2 = f32[1,136,384]{2,1,0:T(8,128)S(1)} custom-call(bf16[8,512,128]{2,1,0:T(8,128)(2,1)S(1)} %get-tuple-element.11.split_ref, f32[256,128]{1,0:T(8,128)S(1)} %get-tuple-element.12.col_ref, f32[512,256]{1,0:T(8,128)S(1)} %collective-permute-done.4.refs_0_, f32[512,256]{1,0:T(8,128)S(1)} %collective-permute-done.5.refs_1_), custom_call_target="tpu_custom_call" | custom-call | flops 6291456000 | bytes 4194304 | tf_op jit(solution)/shard_map/second0/pallas_call | solution.py:208
  69.2 29.9 %all_to_all.10.shards_ref = f32[16,8,1408]{2,1,0:T(8,128)S(1)} all-to-all(f32[16,8,1408]{2,1,0:T(8,128)S(1)} %pack.1), channel_id=1, replica_groups={{0,2,4,6,8,10,12,14,16,18,20,22,24,26,28,30},{1,3,5,7,9,11,13,15,17,19,..., dimensions={0} | all-to-all | bytes 1441792 | tf_op jit(solution)/shard_map/all_to_all | solution.py:376
  99.2 21.1 %all_to_all.11 = f32[16,8,1152]{2,1,0:T(8,128)S(1)} all-to-all(f32[16,8,1152]{2,1,0:T(8,128)S(1)} %normalise.1), channel_id=1, replica_groups={{0,2,4,6,8,10,12,14,16,18,20,22,24,26,28,30},{1,3,5,7,9,11,13,15,17,19,..., dimensions={0} | all-to-all | bytes 1179648 | tf_op jit(solution)/shard_map/all_to_all | solution.py:376
  120.3 1.6 %collective-permute-start.8 = (f32[128,256]{1,0:T(8,128)S(1)}, f32[128,256]{1,0:T(8,128)S(1)}, u32[]{:S(2)}, u32[]{:S(2)}) collective-permute-start(f32[128,256]{1,0:T(8,128)S(1)} %get-tuple-element.19), channel_id=1, source_target_pairs={{0,32},{32,64},{64,96},{96,0},{128,160},{160,192},{192,224},{224,1... | collective-permute-start | bytes 393224 | tf_op jit(solution)/shard_map/ppermute | solution.py:401
  121.9 1.6 %collective-permute-start.9 = (f32[128,256]{1,0:T(8,128)S(1)}, f32[128,256]{1,0:T(8,128)S(1)}, u32[]{:S(2)}, u32[]{:S(2)}) collective-permute-start(f32[128,256]{1,0:T(8,128)S(1)} %get-tuple-element.18), channel_id=1, source_target_pairs={{0,224},{32,128},{64,160},{96,192},{128,96},{160,0},{192,32},{224,... | collective-permute-start | bytes 393224 | tf_op jit(solution)/shard_map/ppermute | solution.py:401
  123.5 2.7 %collective-permute-start.7 = (f32[128,1152]{1,0:T(8,128)S(1)}, f32[128,1152]{1,0:T(8,128)S(1)}, u32[]{:S(2)}, u32[]{:S(2)}) collective-permute-start(f32[128,1152]{1,0:T(8,128)S(1)} %bitcast.5), channel_id=1, source_target_pairs={{0,1},{1,0},{2,3},{3,2},{4,5},{5,4},{6,7},{7,6},{8,9},{9,8},{10,11... | collective-permute-start | bytes 1769480 | tf_op jit(solution)/shard_map/ppermute | solution.py:371
  126.2 0.9 collective-permute-start.10
  127.1 4.2 %collective-permute-start.11 = (f32[128,128]{1,0:T(8,128)S(1)}, f32[128,128]{1,0:T(8,128)S(1)}, u32[]{:S(2)}, u32[]{:S(2)}) collective-permute-start(f32[128,128]{1,0:T(8,128)S(1)} %slice.19), channel_id=1, source_target_pairs={{0,192},{32,224},{64,128},{96,160},{128,64},{160,96},{192,0},{224,... | collective-permute-start | bytes 196616 | tf_op jit(solution)/shard_map/ppermute | solution.py:401
  131.3 2.8 %collective-permute-done.10 = f32[128,256]{1,0:T(8,128)S(1)} collective-permute-done((f32[128,256]{1,0:T(8,128)S(1)}, f32[128,256]{1,0:T(8,128)S(1)}, u32[]{:S(2)}, u32[]{:S(2)}) %collective-permute-start.10) | collective-permute-done | bytes 131104 | tf_op jit(solution)/shard_map/ppermute | solution.py:401
  134.2 2.1 %collective-permute-done.11 = f32[128,128]{1,0:T(8,128)S(1)} collective-permute-done((f32[128,128]{1,0:T(8,128)S(1)}, f32[128,128]{1,0:T(8,128)S(1)}, u32[]{:S(2)}, u32[]{:S(2)}) %collective-permute-start.11) | collective-permute-done | bytes 65568 | tf_op jit(solution)/shard_map/ppermute | solution.py:401
  136.3 0.9 collective-permute-start.12
  137.1 1.4 %collective-permute-done.12.other_swapped = f32[128,896]{1,0:T(8,128)S(1)} collective-permute-done((f32[128,896]{1,0:T(8,128)S(1)}, f32[128,896]{1,0:T(8,128)S(1)}, u32[]{:S(2)}, u32[]{:S(2)}) %collective-permute-start.12) | collective-permute-done | bytes 458784 | tf_op jit(solution)/shard_map/ppermute | solution.py:371
  138.6 1.5 %assemble.1 = f32[256,2048]{1,0:T(8,128)} custom-call(f32[128,1152]{1,0:T(8,128)S(1)} %bitcast.6, f32[128,1152]{1,0:T(8,128)S(1)} %collective-permute-done.7.other, f32[128,896]{1,0:T(8,128)S(1)} %constant_dynamic-update-slice_fusion.own_swapped, f32[128,896]{1,0:T(8,128)S(1)} %collective-permute-done.12.other_swapped), custom_call_target="tpu_custom_call" | custom-call | tf_op jit(solution)/shard_map/assemble/pallas_call | solution.py:352
  (24 shorter events, 1.9 us)
Async XLA Ops:
  0.0 1.0 copy-start
  1.0 0.7 copy-start.1
  1.7 0.7 copy-start.2
  3.4 25.2 %collective-permute-start.1 = (f32[512,256]{1,0:T(8,128)S(1)}, f32[512,256]{1,0:T(8,128)S(1)}, u32[]{:S(2)}, u32[]{:S(2)}) collective-permute-start(f32[512,256]{1,0:T(8,128)S(1)} %get-tuple-element.14.refs_0_), channel_id=1, source_target_pairs={{32,0},{64,32},{96,64},{0,96},{160,128},{192,160},{224,192},{128,2... | collective-permute-start | bytes 1572872 | tf_op jit(solution)/shard_map/ppermute | solution.py:368
  6.7 21.8 %collective-permute-start.2 = (f32[512,256]{1,0:T(8,128)S(1)}, f32[512,256]{1,0:T(8,128)S(1)}, u32[]{:S(2)}, u32[]{:S(2)}) collective-permute-start(f32[512,256]{1,0:T(8,128)S(1)} %get-tuple-element.14.refs_0_), channel_id=1, source_target_pairs={{224,0},{128,32},{160,64},{192,96},{96,128},{0,160},{32,192},{64,2... | collective-permute-start | bytes 1572872 | tf_op jit(solution)/shard_map/ppermute | solution.py:368
  21.3 28.6 %collective-permute-start.4 = (f32[512,256]{1,0:T(8,128)S(1)}, f32[512,256]{1,0:T(8,128)S(1)}, u32[]{:S(2)}, u32[]{:S(2)}) collective-permute-start(f32[512,256]{1,0:T(8,128)S(1)} %get-tuple-element.14.refs_0_), channel_id=1, source_target_pairs={{64,0},{96,32},{192,64},{224,96},{0,128},{32,160},{128,192},{160,2... | collective-permute-start | bytes 1572872 | tf_op jit(solution)/shard_map/ppermute | solution.py:368
  22.7 27.2 %collective-permute-start.5 = (f32[512,256]{1,0:T(8,128)S(1)}, f32[512,256]{1,0:T(8,128)S(1)}, u32[]{:S(2)}, u32[]{:S(2)}) collective-permute-start(f32[512,256]{1,0:T(8,128)S(1)} %get-tuple-element.14.refs_0_), channel_id=1, source_target_pairs={{192,0},{224,32},{128,64},{160,96},{64,128},{96,160},{0,192},{32,2... | collective-permute-start | bytes 1572872 | tf_op jit(solution)/shard_map/ppermute | solution.py:368
  26.8 42.3 %collective-permute-start = (f32[2,136,256]{2,1,0:T(8,128)S(1)}, f32[2,136,256]{2,1,0:T(8,128)S(1)}, u32[]{:S(2)}, u32[]{:S(2)}) collective-permute-start(f32[2,136,256]{2,1,0:T(8,128)S(1)} %diagonal.1.own0), channel_id=1, source_target_pairs={{0,1},{1,0},{2,3},{3,2},{4,5},{5,4},{6,7},{7,6},{8,9},{9,8},{10,11... | collective-permute-start | bytes 835592 | tf_op jit(solution)/shard_map/ppermute | solution.py:371
  58.7 10.3 %collective-permute-start.6 = (f32[1,136,384]{2,1,0:T(8,128)S(1)}, f32[1,136,384]{2,1,0:T(8,128)S(1)}, u32[]{:S(2)}, u32[]{:S(2)}) collective-permute-start(f32[1,136,384]{2,1,0:T(8,128)S(1)} %second1.1), channel_id=1, source_target_pairs={{0,1},{1,0},{2,3},{3,2},{4,5},{5,4},{6,7},{7,6},{8,9},{9,8},{10,11... | collective-permute-start | bytes 626696 | tf_op jit(solution)/shard_map/ppermute | solution.py:371
  59.4 9.7 %collective-permute-start.3 = (f32[2,136,512]{2,1,0:T(8,128)S(1)}, f32[2,136,512]{2,1,0:T(8,128)S(1)}, u32[]{:S(2)}, u32[]{:S(2)}) collective-permute-start(f32[2,136,512]{2,1,0:T(8,128)S(1)} %first.1.own1), channel_id=1, source_target_pairs={{0,1},{1,0},{2,3},{3,2},{4,5},{5,4},{6,7},{7,6},{8,9},{9,8},{10,11... | collective-permute-start | bytes 1671176 | tf_op jit(solution)/shard_map/ppermute | solution.py:371
  120.3 10.9 %collective-permute-start.8 = (f32[128,256]{1,0:T(8,128)S(1)}, f32[128,256]{1,0:T(8,128)S(1)}, u32[]{:S(2)}, u32[]{:S(2)}) collective-permute-start(f32[128,256]{1,0:T(8,128)S(1)} %get-tuple-element.19), channel_id=1, source_target_pairs={{0,32},{32,64},{64,96},{96,0},{128,160},{160,192},{192,224},{224,1... | collective-permute-start | bytes 393224 | tf_op jit(solution)/shard_map/ppermute | solution.py:401
  121.9 9.4 %collective-permute-start.9 = (f32[128,256]{1,0:T(8,128)S(1)}, f32[128,256]{1,0:T(8,128)S(1)}, u32[]{:S(2)}, u32[]{:S(2)}) collective-permute-start(f32[128,256]{1,0:T(8,128)S(1)} %get-tuple-element.18), channel_id=1, source_target_pairs={{0,224},{32,128},{64,160},{96,192},{128,96},{160,0},{192,32},{224,... | collective-permute-start | bytes 393224 | tf_op jit(solution)/shard_map/ppermute | solution.py:401
  123.5 13.6 %collective-permute-start.7 = (f32[128,1152]{1,0:T(8,128)S(1)}, f32[128,1152]{1,0:T(8,128)S(1)}, u32[]{:S(2)}, u32[]{:S(2)}) collective-permute-start(f32[128,1152]{1,0:T(8,128)S(1)} %bitcast.5), channel_id=1, source_target_pairs={{0,1},{1,0},{2,3},{3,2},{4,5},{5,4},{6,7},{7,6},{8,9},{9,8},{10,11... | collective-permute-start | bytes 1769480 | tf_op jit(solution)/shard_map/ppermute | solution.py:371
  126.2 7.9 %collective-permute-start.10 = (f32[128,256]{1,0:T(8,128)S(1)}, f32[128,256]{1,0:T(8,128)S(1)}, u32[]{:S(2)}, u32[]{:S(2)}) collective-permute-start(f32[128,256]{1,0:T(8,128)S(1)} %get-tuple-element.17), channel_id=1, source_target_pairs={{0,64},{32,96},{64,192},{96,224},{128,0},{160,32},{192,128},{224,1... | collective-permute-start | bytes 393224 | tf_op jit(solution)/shard_map/ppermute | solution.py:401
  127.1 9.2 %collective-permute-start.11 = (f32[128,128]{1,0:T(8,128)S(1)}, f32[128,128]{1,0:T(8,128)S(1)}, u32[]{:S(2)}, u32[]{:S(2)}) collective-permute-start(f32[128,128]{1,0:T(8,128)S(1)} %slice.19), channel_id=1, source_target_pairs={{0,192},{32,224},{64,128},{96,160},{128,64},{160,96},{192,0},{224,... | collective-permute-start | bytes 196616 | tf_op jit(solution)/shard_map/ppermute | solution.py:401
  136.3 2.3 %collective-permute-start.12 = (f32[128,896]{1,0:T(8,128)S(1)}, f32[128,896]{1,0:T(8,128)S(1)}, u32[]{:S(2)}, u32[]{:S(2)}) collective-permute-start(f32[128,896]{1,0:T(8,128)S(1)} %constant_dynamic-update-slice_fusion.own_swapped), channel_id=1, source_target_pairs={{0,1},{1,0},{2,3},{3,2},{4,5},{5,4},{6,7},{7,6},{8,9},{9,8},{10,11... | collective-permute-start | bytes 1376264 | tf_op jit(solution)/shard_map/ppermute | solution.py:371

commit v10 on v9

--- a/solution.py
+++ b/solution.py
@@ -169,17 +169,10 @@
             cols = columns_at(h)
             n_cols = len(cols)
             following = base + jnp.minimum(g + 1, groups - 1)
-            steps = []
-            if group == 8:
-                for q in range(pairs):
-                    broadcast_pair(later, following, q)
-            else:
-                steps = [(q, slice(k, k + 128)) for k in range(0, KS, 128) for q in range(pairs)]
+            for q in range(pairs):
+                broadcast_pair(later, following, q)
             acc = [jnp.zeros((8, 128), F32)] * (group * n_cols)
             for k8 in range(KS // 8):
-                if steps and k8 % 2 == 0:
-                    q, at = steps[k8 // 2]
-                    broadcast_pair(later, following, q, at)
                 at = slice(k8 * 8, k8 * 8 + 8)
                 spans = [span(n, lane, at) for n, lane in cols]
                 for r in range(group):
@@ -378,14 +371,14 @@
     wt, split, mass_col = weigh(counts, totals, lengths)
     got = [from_partner(wt, n) for n in range(2)]
     diagonal = spread_call("diagonal", 1, diagonal_columns, 256, 16, 0)
-    first = spread_call("first", 2, first_columns, 512, 8, 2)
-    second = [spread_call(f"second{s}", 2, second_columns, 384, 8, 0, s) for s in range(2)]
+    first = spread_call("first", 2, first_columns, 512, 16, 2)
+    second = [spread_call(f"second{s}", 2, second_columns, 384, 16, 0, s) for s in range(2)]
 
     part0 = diagonal(split, mass_col, wt)
     later = lax.optimization_barrier((wt, part0))[0]
     got += [from_partner(later, n) for n in (2, 3)]
-    received0 = other_core(part0)
     part1 = first(split, mass_col, got[0], got[1])
+    received0 = other_core(lax.optimization_barrier((part0, part1))[0])
     received1 = other_core(part1)
     third = lax.optimization_barrier((got[2], part1))[0]
     sent2 = second[1](split, mass_col, third, got[3])

time: 140 us -> 141 us (level)
  waiting for transfers between devices: 6.39 us -> 8.62 us
  Pallas kernels: 55 us -> 53.1 us
    pallas_call x4, Pallas kernels: 52.4 us -> 50.4 us  [call(): pl.pallas_call(kernel, out_shape=jax.ShapeDtypeStruct((halves, 136, width...]
    ppermute x4, waiting for transfers between devices: 4.93 us -> 6.47 us  [on_device(): lax.ppermute(tile, 'blk', [(b, PARTNERS[n][b]) for b in range(BLOCKS)])]
    ppermute x4, starting transfers between devices: 8.23 us -> 6.78 us  [on_device(): lax.ppermute(tile, 'blk', [(b, PARTNERS[n][b]) for b in range(BLOCKS)])]
  transfers between devices with their start and end apart: 13 -> 13, of which waited for: 3 -> 3; matrix products, arithmetic and copies ran while one was open for 0% -> 0% of each run, Pallas kernels for 37% -> 30%
where the time goes in v10:
time: 141 us
  Pallas kernels  53.1 us (38%)
  blocking collectives  51.8 us (37%)
  starting transfers between devices  25 us (18%)
  waiting for transfers between devices  8.62 us (6%)
  local copies, waits for them, and re-layouts  2.47 us (2%)
    all_to_all x2, blocking collectives, over_chips(): return lax.all_to_all(v, 'branch', 0, 0, axis_index_groups=chips)  51.8 us
    pallas_call x4, Pallas kernels, call(): pl.pallas_call(kernel, out_shape=jax.ShapeDtypeStruct((halves, 136, width...  50.4 us
    ppermute x4, starting transfers between devices, from_partner(): return lax.ppermute(v, 'blk', [(PARTNERS[n][b], b) for b in range(BLOCKS)])  10.5 us
    ppermute x5, starting transfers between devices, other_core(): return lax.ppermute(v, 'branch', [(i, i ^ 1) for i in range(32)])  7.67 us
    ppermute x4, starting transfers between devices, on_device(): lax.ppermute(tile, 'blk', [(b, PARTNERS[n][b]) for b in range(BLOCKS)])  6.78 us
    ppermute x4, waiting for transfers between devices, on_device(): lax.ppermute(tile, 'blk', [(b, PARTNERS[n][b]) for b in range(BLOCKS)])  6.47 us
  transfers between devices with their start and end apart: 13, of which 3 were waited for; matrix products, arithmetic and copies ran while one was open for 0% of the time, Pallas kernels for 30%

profile of v10, /device:TPU:1, one launch (start us, length us, event | category | flops | bytes accessed | tf_op | source)
XLA Modules:
  0.0 141.2 jit_solution(1244539159515577141)
XLA Ops:
  0.0 1.0 copy-done
  1.0 0.7 copy-done.1
  1.7 0.7 copy-done.2
  2.4 0.9 weigh.1
  3.4 4.7 %collective-permute-start.1 = (f32[512,256]{1,0:T(8,128)S(1)}, f32[512,256]{1,0:T(8,128)S(1)}, u32[]{:S(2)}, u32[]{:S(2)}) collective-permute-start(f32[512,256]{1,0:T(8,128)S(1)} %get-tuple-element.16.refs_0_), channel_id=1, source_target_pairs={{224,0},{128,32},{160,64},{192,96},{96,128},{0,160},{32,192},{64,2... | collective-permute-start | bytes 1572872 | tf_op jit(solution)/shard_map/ppermute | solution.py:361
  8.1 1.5 %collective-permute-start = (f32[512,256]{1,0:T(8,128)S(1)}, f32[512,256]{1,0:T(8,128)S(1)}, u32[]{:S(2)}, u32[]{:S(2)}) collective-permute-start(f32[512,256]{1,0:T(8,128)S(1)} %get-tuple-element.16.refs_0_), channel_id=1, source_target_pairs={{32,0},{64,32},{96,64},{0,96},{160,128},{192,160},{224,192},{128,2... | collective-permute-start | bytes 1572872 | tf_op jit(solution)/shard_map/ppermute | solution.py:361
  9.6 12.2 %diagonal.1.own0 = f32[2,136,256]{2,1,0:T(8,128)S(1)} custom-call(bf16[8,512,128]{2,1,0:T(8,128)(2,1)S(1)} %get-tuple-element.12.split_ref, f32[256,128]{1,0:T(8,128)S(1)} %get-tuple-element.13.col_ref, f32[512,256]{1,0:T(8,128)S(1)} %get-tuple-element.16.refs_0_), custom_call_target="tpu_custom_call" | custom-call | flops 8388608000 | bytes 4194304 | tf_op jit(solution)/shard_map/diagonal/pallas_call | solution.py:201
  21.8 1.4 collective-permute-start.5
  23.2 2.9 %collective-permute-start.4 = (f32[512,256]{1,0:T(8,128)S(1)}, f32[512,256]{1,0:T(8,128)S(1)}, u32[]{:S(2)}, u32[]{:S(2)}) collective-permute-start(f32[512,256]{1,0:T(8,128)S(1)} %get-tuple-element.16.refs_0_), channel_id=1, source_target_pairs={{64,0},{96,32},{192,64},{224,96},{0,128},{32,160},{128,192},{160,2... | collective-permute-start | bytes 1572872 | tf_op jit(solution)/shard_map/ppermute | solution.py:361
  26.1 20.5 %first.1.own1 = f32[2,136,512]{2,1,0:T(8,128)S(1)} custom-call(bf16[8,512,128]{2,1,0:T(8,128)(2,1)S(1)} %get-tuple-element.12.split_ref, f32[256,128]{1,0:T(8,128)S(1)} %get-tuple-element.13.col_ref, f32[512,256]{1,0:T(8,128)S(1)} %collective-permute-done.refs_0_, f32[512,256]{1,0:T(8,128)S(1)} %collective-permute-done.1.refs_1_), custom_call_target="tpu_custom_call" | custom-call | flops 16777216000 | bytes 4194304 | tf_op jit(solution)/shard_map/first/pallas_call | solution.py:201
  46.7 0.7 collective-permute-done.4.refs_0_
  47.4 8.6 %second1.1 = f32[1,136,384]{2,1,0:T(8,128)S(1)} custom-call(bf16[8,512,128]{2,1,0:T(8,128)(2,1)S(1)} %get-tuple-element.12.split_ref, f32[256,128]{1,0:T(8,128)S(1)} %get-tuple-element.13.col_ref, f32[512,256]{1,0:T(8,128)S(1)} %collective-permute-done.4.refs_0_, f32[512,256]{1,0:T(8,128)S(1)} %collective-permute-done.5.refs_1_), custom_call_target="tpu_custom_call" | custom-call | flops 6291456000 | bytes 4194304 | tf_op jit(solution)/shard_map/second1/pallas_call | solution.py:201
  55.9 2.4 %collective-permute-start.6 = (f32[1,136,384]{2,1,0:T(8,128)S(1)}, f32[1,136,384]{2,1,0:T(8,128)S(1)}, u32[]{:S(2)}, u32[]{:S(2)}) collective-permute-start(f32[1,136,384]{2,1,0:T(8,128)S(1)} %second1.1), channel_id=1, source_target_pairs={{0,1},{1,0},{2,3},{3,2},{4,5},{5,4},{6,7},{7,6},{8,9},{9,8},{10,11... | collective-permute-start | bytes 626696 | tf_op jit(solution)/shard_map/ppermute | solution.py:364
  58.8 9.1 %second0.1.own2 = f32[1,136,384]{2,1,0:T(8,128)S(1)} custom-call(bf16[8,512,128]{2,1,0:T(8,128)(2,1)S(1)} %get-tuple-element.12.split_ref, f32[256,128]{1,0:T(8,128)S(1)} %get-tuple-element.13.col_ref, f32[512,256]{1,0:T(8,128)S(1)} %collective-permute-done.4.refs_0_, f32[512,256]{1,0:T(8,128)S(1)} %collective-permute-done.5.refs_1_), custom_call_target="tpu_custom_call" | custom-call | flops 6291456000 | bytes 4194304 | tf_op jit(solution)/shard_map/second0/pallas_call | solution.py:201
  68.0 30.7 %all_to_all.10.shards_ref = f32[16,8,1408]{2,1,0:T(8,128)S(1)} all-to-all(f32[16,8,1408]{2,1,0:T(8,128)S(1)} %pack.1), channel_id=1, replica_groups={{0,2,4,6,8,10,12,14,16,18,20,22,24,26,28,30},{1,3,5,7,9,11,13,15,17,19,..., dimensions={0} | all-to-all | bytes 1441792 | tf_op jit(solution)/shard_map/all_to_all | solution.py:369
  98.8 21.2 %all_to_all.11 = f32[16,8,1152]{2,1,0:T(8,128)S(1)} all-to-all(f32[16,8,1152]{2,1,0:T(8,128)S(1)} %normalise.1), channel_id=1, replica_groups={{0,2,4,6,8,10,12,14,16,18,20,22,24,26,28,30},{1,3,5,7,9,11,13,15,17,19,..., dimensions={0} | all-to-all | bytes 1179648 | tf_op jit(solution)/shard_map/all_to_all | solution.py:369
  120.1 2.6 %collective-permute-start.9 = (f32[128,256]{1,0:T(8,128)S(1)}, f32[128,256]{1,0:T(8,128)S(1)}, u32[]{:S(2)}, u32[]{:S(2)}) collective-permute-start(f32[128,256]{1,0:T(8,128)S(1)} %get-tuple-element.20), channel_id=1, source_target_pairs={{0,224},{32,128},{64,160},{96,192},{128,96},{160,0},{192,32},{224,... | collective-permute-start | bytes 393224 | tf_op jit(solution)/shard_map/ppermute | solution.py:394
  122.7 4.1 %collective-permute-start.7 = (f32[128,1152]{1,0:T(8,128)S(1)}, f32[128,1152]{1,0:T(8,128)S(1)}, u32[]{:S(2)}, u32[]{:S(2)}) collective-permute-start(f32[128,1152]{1,0:T(8,128)S(1)} %bitcast.5), channel_id=1, source_target_pairs={{0,1},{1,0},{2,3},{3,2},{4,5},{5,4},{6,7},{7,6},{8,9},{9,8},{10,11... | collective-permute-start | bytes 1769480 | tf_op jit(solution)/shard_map/ppermute | solution.py:364
  126.8 2.9 %collective-permute-start.11 = (f32[128,128]{1,0:T(8,128)S(1)}, f32[128,128]{1,0:T(8,128)S(1)}, u32[]{:S(2)}, u32[]{:S(2)}) collective-permute-start(f32[128,128]{1,0:T(8,128)S(1)} %slice.19), channel_id=1, source_target_pairs={{0,192},{32,224},{64,128},{96,160},{128,64},{160,96},{192,0},{224,... | collective-permute-start | bytes 196616 | tf_op jit(solution)/shard_map/ppermute | solution.py:394
  129.7 1.2 collective-permute-start.10
  131.0 6.5 %collective-permute-done.10 = f32[128,256]{1,0:T(8,128)S(1)} collective-permute-done((f32[128,256]{1,0:T(8,128)S(1)}, f32[128,256]{1,0:T(8,128)S(1)}, u32[]{:S(2)}, u32[]{:S(2)}) %collective-permute-start.10) | collective-permute-done | bytes 131104 | tf_op jit(solution)/shard_map/ppermute | solution.py:394
  137.5 0.7 collective-permute-start.12
  138.2 1.4 %collective-permute-done.12.other_swapped = f32[128,896]{1,0:T(8,128)S(1)} collective-permute-done((f32[128,896]{1,0:T(8,128)S(1)}, f32[128,896]{1,0:T(8,128)S(1)}, u32[]{:S(2)}, u32[]{:S(2)}) %collective-permute-start.12) | collective-permute-done | bytes 458784 | tf_op jit(solution)/shard_map/ppermute | solution.py:364
  139.6 1.5 %assemble.1 = f32[256,2048]{1,0:T(8,128)} custom-call(f32[128,1152]{1,0:T(8,128)S(1)} %bitcast.6, f32[128,1152]{1,0:T(8,128)S(1)} %collective-permute-done.7.other, f32[128,896]{1,0:T(8,128)S(1)} %constant_dynamic-update-slice_fusion.own_swapped, f32[128,896]{1,0:T(8,128)S(1)} %collective-permute-done.12.other_swapped), custom_call_target="tpu_custom_call" | custom-call | tf_op jit(solution)/shard_map/assemble/pallas_call | solution.py:345
  (24 shorter events, 0.9 us)
Async XLA Ops:
  0.0 1.0 copy-start
  1.0 0.7 copy-start.1
  1.7 0.7 copy-start.2
  3.4 22.8 %collective-permute-start.1 = (f32[512,256]{1,0:T(8,128)S(1)}, f32[512,256]{1,0:T(8,128)S(1)}, u32[]{:S(2)}, u32[]{:S(2)}) collective-permute-start(f32[512,256]{1,0:T(8,128)S(1)} %get-tuple-element.16.refs_0_), channel_id=1, source_target_pairs={{224,0},{128,32},{160,64},{192,96},{96,128},{0,160},{32,192},{64,2... | collective-permute-start | bytes 1572872 | tf_op jit(solution)/shard_map/ppermute | solution.py:361
  8.1 18.0 %collective-permute-start = (f32[512,256]{1,0:T(8,128)S(1)}, f32[512,256]{1,0:T(8,128)S(1)}, u32[]{:S(2)}, u32[]{:S(2)}) collective-permute-start(f32[512,256]{1,0:T(8,128)S(1)} %get-tuple-element.16.refs_0_), channel_id=1, source_target_pairs={{32,0},{64,32},{96,64},{0,96},{160,128},{192,160},{224,192},{128,2... | collective-permute-start | bytes 1572872 | tf_op jit(solution)/shard_map/ppermute | solution.py:361
  21.8 25.6 %collective-permute-start.5 = (f32[512,256]{1,0:T(8,128)S(1)}, f32[512,256]{1,0:T(8,128)S(1)}, u32[]{:S(2)}, u32[]{:S(2)}) collective-permute-start(f32[512,256]{1,0:T(8,128)S(1)} %get-tuple-element.16.refs_0_), channel_id=1, source_target_pairs={{192,0},{224,32},{128,64},{160,96},{64,128},{96,160},{0,192},{32,2... | collective-permute-start | bytes 1572872 | tf_op jit(solution)/shard_map/ppermute | solution.py:361
  23.2 24.2 %collective-permute-start.4 = (f32[512,256]{1,0:T(8,128)S(1)}, f32[512,256]{1,0:T(8,128)S(1)}, u32[]{:S(2)}, u32[]{:S(2)}) collective-permute-start(f32[512,256]{1,0:T(8,128)S(1)} %get-tuple-element.16.refs_0_), channel_id=1, source_target_pairs={{64,0},{96,32},{192,64},{224,96},{0,128},{32,160},{128,192},{160,2... | collective-permute-start | bytes 1572872 | tf_op jit(solution)/shard_map/ppermute | solution.py:361
  55.9 12.0 %collective-permute-start.6 = (f32[1,136,384]{2,1,0:T(8,128)S(1)}, f32[1,136,384]{2,1,0:T(8,128)S(1)}, u32[]{:S(2)}, u32[]{:S(2)}) collective-permute-start(f32[1,136,384]{2,1,0:T(8,128)S(1)} %second1.1), channel_id=1, source_target_pairs={{0,1},{1,0},{2,3},{3,2},{4,5},{5,4},{6,7},{7,6},{8,9},{9,8},{10,11... | collective-permute-start | bytes 626696 | tf_op jit(solution)/shard_map/ppermute | solution.py:364
  58.3 9.7 %collective-permute-start.3 = (f32[2,136,512]{2,1,0:T(8,128)S(1)}, f32[2,136,512]{2,1,0:T(8,128)S(1)}, u32[]{:S(2)}, u32[]{:S(2)}) collective-permute-start(f32[2,136,512]{2,1,0:T(8,128)S(1)} %first.1.own1), channel_id=1, source_target_pairs={{0,1},{1,0},{2,3},{3,2},{4,5},{5,4},{6,7},{7,6},{8,9},{9,8},{10,11... | collective-permute-start | bytes 1671176 | tf_op jit(solution)/shard_map/ppermute | solution.py:364
  58.4 9.5 %collective-permute-start.2 = (f32[2,136,256]{2,1,0:T(8,128)S(1)}, f32[2,136,256]{2,1,0:T(8,128)S(1)}, u32[]{:S(2)}, u32[]{:S(2)}) collective-permute-start(f32[2,136,256]{2,1,0:T(8,128)S(1)} %diagonal.1.own0), channel_id=1, source_target_pairs={{0,1},{1,0},{2,3},{3,2},{4,5},{5,4},{6,7},{7,6},{8,9},{9,8},{10,11... | collective-permute-start | bytes 835592 | tf_op jit(solution)/shard_map/ppermute | solution.py:364
  120.0 10.9 %collective-permute-start.8 = (f32[128,256]{1,0:T(8,128)S(1)}, f32[128,256]{1,0:T(8,128)S(1)}, u32[]{:S(2)}, u32[]{:S(2)}) collective-permute-start(f32[128,256]{1,0:T(8,128)S(1)} %get-tuple-element.21), channel_id=1, source_target_pairs={{0,32},{32,64},{64,96},{96,0},{128,160},{160,192},{192,224},{224,1... | collective-permute-start | bytes 393224 | tf_op jit(solution)/shard_map/ppermute | solution.py:394
  120.1 10.8 %collective-permute-start.9 = (f32[128,256]{1,0:T(8,128)S(1)}, f32[128,256]{1,0:T(8,128)S(1)}, u32[]{:S(2)}, u32[]{:S(2)}) collective-permute-start(f32[128,256]{1,0:T(8,128)S(1)} %get-tuple-element.20), channel_id=1, source_target_pairs={{0,224},{32,128},{64,160},{96,192},{128,96},{160,0},{192,32},{224,... | collective-permute-start | bytes 393224 | tf_op jit(solution)/shard_map/ppermute | solution.py:394
  122.7 15.5 %collective-permute-start.7 = (f32[128,1152]{1,0:T(8,128)S(1)}, f32[128,1152]{1,0:T(8,128)S(1)}, u32[]{:S(2)}, u32[]{:S(2)}) collective-permute-start(f32[128,1152]{1,0:T(8,128)S(1)} %bitcast.5), channel_id=1, source_target_pairs={{0,1},{1,0},{2,3},{3,2},{4,5},{5,4},{6,7},{7,6},{8,9},{9,8},{10,11... | collective-permute-start | bytes 1769480 | tf_op jit(solution)/shard_map/ppermute | solution.py:364
  126.8 10.7 %collective-permute-start.11 = (f32[128,128]{1,0:T(8,128)S(1)}, f32[128,128]{1,0:T(8,128)S(1)}, u32[]{:S(2)}, u32[]{:S(2)}) collective-permute-start(f32[128,128]{1,0:T(8,128)S(1)} %slice.19), channel_id=1, source_target_pairs={{0,192},{32,224},{64,128},{96,160},{128,64},{160,96},{192,0},{224,... | collective-permute-start | bytes 196616 | tf_op jit(solution)/shard_map/ppermute | solution.py:394
  129.7 7.8 %collective-permute-start.10 = (f32[128,256]{1,0:T(8,128)S(1)}, f32[128,256]{1,0:T(8,128)S(1)}, u32[]{:S(2)}, u32[]{:S(2)}) collective-permute-start(f32[128,256]{1,0:T(8,128)S(1)} %get-tuple-element.19), channel_id=1, source_target_pairs={{0,64},{32,96},{64,192},{96,224},{128,0},{160,32},{192,128},{224,1... | collective-permute-start | bytes 393224 | tf_op jit(solution)/shard_map/ppermute | solution.py:394
  137.5 2.1 %collective-permute-start.12 = (f32[128,896]{1,0:T(8,128)S(1)}, f32[128,896]{1,0:T(8,128)S(1)}, u32[]{:S(2)}, u32[]{:S(2)}) collective-permute-start(f32[128,896]{1,0:T(8,128)S(1)} %constant_dynamic-update-slice_fusion.own_swapped), channel_id=1, source_target_pairs={{0,1},{1,0},{2,3},{3,2},{4,5},{5,4},{6,7},{7,6},{8,9},{9,8},{10,11... | collective-permute-start | bytes 1376264 | tf_op jit(solution)/shard_map/ppermute | solution.py:364

commit v11 on v10

--- a/solution.py
+++ b/solution.py
@@ -377,8 +377,8 @@
     part0 = diagonal(split, mass_col, wt)
     later = lax.optimization_barrier((wt, part0))[0]
     got += [from_partner(later, n) for n in (2, 3)]
+    received0 = other_core(part0)
     part1 = first(split, mass_col, got[0], got[1])
-    received0 = other_core(lax.optimization_barrier((part0, part1))[0])
     received1 = other_core(part1)
     third = lax.optimization_barrier((got[2], part1))[0]
     sent2 = second[1](split, mass_col, third, got[3])

time: 141 us -> 139 us (0.986)
  waiting for transfers between devices: 8.62 us -> 6.39 us
    ppermute x4, waiting for transfers between devices: 6.47 us -> 4.93 us  [on_device(): lax.ppermute(tile, 'blk', [(b, PARTNERS[n][b]) for b in range(BLOCKS)])]
    ppermute x4, starting transfers between devices: 6.78 us -> 8.26 us  [on_device(): lax.ppermute(tile, 'blk', [(b, PARTNERS[n][b]) for b in range(BLOCKS)])]
  transfers between devices with their start and end apart: 13 -> 13, of which waited for: 3 -> 3; matrix products, arithmetic and copies ran while one was open for 0% -> 0% of each run, Pallas kernels for 30% -> 36%
where the time goes in v11:
time: 139 us
  Pallas kernels  53.1 us (38%)
  blocking collectives  51 us (37%)
  starting transfers between devices  25.8 us (19%)
  waiting for transfers between devices  6.39 us (5%)
  local copies, waits for them, and re-layouts  2.47 us (2%)
    all_to_all x2, blocking collectives, over_chips(): return lax.all_to_all(v, 'branch', 0, 0, axis_index_groups=chips)  51 us
    pallas_call x4, Pallas kernels, call(): pl.pallas_call(kernel, out_shape=jax.ShapeDtypeStruct((halves, 136, width...  50.4 us
    ppermute x4, starting transfers between devices, from_partner(): return lax.ppermute(v, 'blk', [(PARTNERS[n][b], b) for b in range(BLOCKS)])  10.5 us
    ppermute x4, starting transfers between devices, on_device(): lax.ppermute(tile, 'blk', [(b, PARTNERS[n][b]) for b in range(BLOCKS)])  8.26 us
    ppermute x5, starting transfers between devices, other_core(): return lax.ppermute(v, 'branch', [(i, i ^ 1) for i in range(32)])  6.99 us
    ppermute x4, waiting for transfers between devices, on_device(): lax.ppermute(tile, 'blk', [(b, PARTNERS[n][b]) for b in range(BLOCKS)])  4.93 us
  transfers between devices with their start and end apart: 13, of which 3 were waited for; matrix products, arithmetic and copies ran while one was open for 0% of the time, Pallas kernels for 36%

profile of v11, /device:TPU:1, one launch (start us, length us, event | category | flops | bytes accessed | tf_op | source)
XLA Modules:
  0.0 139.0 jit_solution(6026968312557293970)
XLA Ops:
  0.0 1.0 copy-done
  1.0 0.7 copy-done.1
  2.4 0.9 weigh.1
  3.4 3.4 %collective-permute-start.1 = (f32[512,256]{1,0:T(8,128)S(1)}, f32[512,256]{1,0:T(8,128)S(1)}, u32[]{:S(2)}, u32[]{:S(2)}) collective-permute-start(f32[512,256]{1,0:T(8,128)S(1)} %get-tuple-element.14.refs_0_), channel_id=1, source_target_pairs={{32,0},{64,32},{96,64},{0,96},{160,128},{192,160},{224,192},{128,2... | collective-permute-start | bytes 1572872 | tf_op jit(solution)/shard_map/ppermute | solution.py:361
  6.7 1.6 %collective-permute-start.2 = (f32[512,256]{1,0:T(8,128)S(1)}, f32[512,256]{1,0:T(8,128)S(1)}, u32[]{:S(2)}, u32[]{:S(2)}) collective-permute-start(f32[512,256]{1,0:T(8,128)S(1)} %get-tuple-element.14.refs_0_), channel_id=1, source_target_pairs={{224,0},{128,32},{160,64},{192,96},{96,128},{0,160},{32,192},{64,2... | collective-permute-start | bytes 1572872 | tf_op jit(solution)/shard_map/ppermute | solution.py:361
  8.4 12.2 %diagonal.1.own0 = f32[2,136,256]{2,1,0:T(8,128)S(1)} custom-call(bf16[8,512,128]{2,1,0:T(8,128)(2,1)S(1)} %get-tuple-element.11.split_ref, f32[256,128]{1,0:T(8,128)S(1)} %get-tuple-element.12.col_ref, f32[512,256]{1,0:T(8,128)S(1)} %get-tuple-element.14.refs_0_), custom_call_target="tpu_custom_call" | custom-call | flops 8388608000 | bytes 4194304 | tf_op jit(solution)/shard_map/diagonal/pallas_call | solution.py:201
  20.6 1.4 collective-permute-start.4
  22.0 4.1 %collective-permute-start.5 = (f32[512,256]{1,0:T(8,128)S(1)}, f32[512,256]{1,0:T(8,128)S(1)}, u32[]{:S(2)}, u32[]{:S(2)}) collective-permute-start(f32[512,256]{1,0:T(8,128)S(1)} %get-tuple-element.14.refs_0_), channel_id=1, source_target_pairs={{192,0},{224,32},{128,64},{160,96},{64,128},{96,160},{0,192},{32,2... | collective-permute-start | bytes 1572872 | tf_op jit(solution)/shard_map/ppermute | solution.py:361
  26.1 1.8 %collective-permute-start = (f32[2,136,256]{2,1,0:T(8,128)S(1)}, f32[2,136,256]{2,1,0:T(8,128)S(1)}, u32[]{:S(2)}, u32[]{:S(2)}) collective-permute-start(f32[2,136,256]{2,1,0:T(8,128)S(1)} %diagonal.1.own0), channel_id=1, source_target_pairs={{0,1},{1,0},{2,3},{3,2},{4,5},{5,4},{6,7},{7,6},{8,9},{9,8},{10,11... | collective-permute-start | bytes 835592 | tf_op jit(solution)/shard_map/ppermute | solution.py:364
  27.9 20.5 %first.1.own1 = f32[2,136,512]{2,1,0:T(8,128)S(1)} custom-call(bf16[8,512,128]{2,1,0:T(8,128)(2,1)S(1)} %get-tuple-element.11.split_ref, f32[256,128]{1,0:T(8,128)S(1)} %get-tuple-element.12.col_ref, f32[512,256]{1,0:T(8,128)S(1)} %collective-permute-done.1.refs_0_, f32[512,256]{1,0:T(8,128)S(1)} %collective-permute-done.2.refs_1_), custom_call_target="tpu_custom_call" | custom-call | flops 16777216000 | bytes 4194304 | tf_op jit(solution)/shard_map/first/pallas_call | solution.py:201
  48.5 8.5 %second1.1 = f32[1,136,384]{2,1,0:T(8,128)S(1)} custom-call(bf16[8,512,128]{2,1,0:T(8,128)(2,1)S(1)} %get-tuple-element.11.split_ref, f32[256,128]{1,0:T(8,128)S(1)} %get-tuple-element.12.col_ref, f32[512,256]{1,0:T(8,128)S(1)} %collective-permute-done.4.refs_0_, f32[512,256]{1,0:T(8,128)S(1)} %collective-permute-done.5.refs_1_), custom_call_target="tpu_custom_call" | custom-call | flops 6291456000 | bytes 4194304 | tf_op jit(solution)/shard_map/second1/pallas_call | solution.py:201
  57.8 9.1 %second0.1.own2 = f32[1,136,384]{2,1,0:T(8,128)S(1)} custom-call(bf16[8,512,128]{2,1,0:T(8,128)(2,1)S(1)} %get-tuple-element.11.split_ref, f32[256,128]{1,0:T(8,128)S(1)} %get-tuple-element.12.col_ref, f32[512,256]{1,0:T(8,128)S(1)} %collective-permute-done.4.refs_0_, f32[512,256]{1,0:T(8,128)S(1)} %collective-permute-done.5.refs_1_), custom_call_target="tpu_custom_call" | custom-call | flops 6291456000 | bytes 4194304 | tf_op jit(solution)/shard_map/second0/pallas_call | solution.py:201
  67.0 29.3 %all_to_all.10.shards_ref = f32[16,8,1408]{2,1,0:T(8,128)S(1)} all-to-all(f32[16,8,1408]{2,1,0:T(8,128)S(1)} %pack.1), channel_id=1, replica_groups={{0,2,4,6,8,10,12,14,16,18,20,22,24,26,28,30},{1,3,5,7,9,11,13,15,17,19,..., dimensions={0} | all-to-all | bytes 1441792 | tf_op jit(solution)/shard_map/all_to_all | solution.py:369
  96.4 21.7 %all_to_all.11 = f32[16,8,1152]{2,1,0:T(8,128)S(1)} all-to-all(f32[16,8,1152]{2,1,0:T(8,128)S(1)} %normalise.1), channel_id=1, replica_groups={{0,2,4,6,8,10,12,14,16,18,20,22,24,26,28,30},{1,3,5,7,9,11,13,15,17,19,..., dimensions={0} | all-to-all | bytes 1179648 | tf_op jit(solution)/shard_map/all_to_all | solution.py:369
  118.2 1.6 %collective-permute-start.8 = (f32[128,256]{1,0:T(8,128)S(1)}, f32[128,256]{1,0:T(8,128)S(1)}, u32[]{:S(2)}, u32[]{:S(2)}) collective-permute-start(f32[128,256]{1,0:T(8,128)S(1)} %get-tuple-element.19), channel_id=1, source_target_pairs={{0,32},{32,64},{64,96},{96,0},{128,160},{160,192},{192,224},{224,1... | collective-permute-start | bytes 393224 | tf_op jit(solution)/shard_map/ppermute | solution.py:394
  119.8 0.8 collective-permute-start.9
  120.6 3.6 %collective-permute-start.7 = (f32[128,1152]{1,0:T(8,128)S(1)}, f32[128,1152]{1,0:T(8,128)S(1)}, u32[]{:S(2)}, u32[]{:S(2)}) collective-permute-start(f32[128,1152]{1,0:T(8,128)S(1)} %bitcast.5), channel_id=1, source_target_pairs={{0,1},{1,0},{2,3},{3,2},{4,5},{5,4},{6,7},{7,6},{8,9},{9,8},{10,11... | collective-permute-start | bytes 1769480 | tf_op jit(solution)/shard_map/ppermute | solution.py:364
  124.1 1.5 %collective-permute-start.10 = (f32[128,256]{1,0:T(8,128)S(1)}, f32[128,256]{1,0:T(8,128)S(1)}, u32[]{:S(2)}, u32[]{:S(2)}) collective-permute-start(f32[128,256]{1,0:T(8,128)S(1)} %get-tuple-element.17), channel_id=1, source_target_pairs={{0,64},{32,96},{64,192},{96,224},{128,0},{160,32},{192,128},{224,1... | collective-permute-start | bytes 393224 | tf_op jit(solution)/shard_map/ppermute | solution.py:394
  125.6 4.4 %collective-permute-start.11 = (f32[128,128]{1,0:T(8,128)S(1)}, f32[128,128]{1,0:T(8,128)S(1)}, u32[]{:S(2)}, u32[]{:S(2)}) collective-permute-start(f32[128,128]{1,0:T(8,128)S(1)} %slice.19), channel_id=1, source_target_pairs={{0,192},{32,224},{64,128},{96,160},{128,64},{160,96},{192,0},{224,... | collective-permute-start | bytes 196616 | tf_op jit(solution)/shard_map/ppermute | solution.py:394
  130.1 1.9 %collective-permute-done.10 = f32[128,256]{1,0:T(8,128)S(1)} collective-permute-done((f32[128,256]{1,0:T(8,128)S(1)}, f32[128,256]{1,0:T(8,128)S(1)}, u32[]{:S(2)}, u32[]{:S(2)}) %collective-permute-start.10) | collective-permute-done | bytes 131104 | tf_op jit(solution)/shard_map/ppermute | solution.py:394
  132.0 3.1 %collective-permute-done.11 = f32[128,128]{1,0:T(8,128)S(1)} collective-permute-done((f32[128,128]{1,0:T(8,128)S(1)}, f32[128,128]{1,0:T(8,128)S(1)}, u32[]{:S(2)}, u32[]{:S(2)}) %collective-permute-start.11) | collective-permute-done | bytes 65568 | tf_op jit(solution)/shard_map/ppermute | solution.py:394
  135.0 0.9 collective-permute-start.12
  135.9 1.4 %collective-permute-done.12.other_swapped = f32[128,896]{1,0:T(8,128)S(1)} collective-permute-done((f32[128,896]{1,0:T(8,128)S(1)}, f32[128,896]{1,0:T(8,128)S(1)}, u32[]{:S(2)}, u32[]{:S(2)}) %collective-permute-start.12) | collective-permute-done | bytes 458784 | tf_op jit(solution)/shard_map/ppermute | solution.py:364
  137.3 1.5 %assemble.1 = f32[256,2048]{1,0:T(8,128)} custom-call(f32[128,1152]{1,0:T(8,128)S(1)} %bitcast.6, f32[128,1152]{1,0:T(8,128)S(1)} %collective-permute-done.7.other, f32[128,896]{1,0:T(8,128)S(1)} %constant_dynamic-update-slice_fusion.own_swapped, f32[128,896]{1,0:T(8,128)S(1)} %collective-permute-done.12.other_swapped), custom_call_target="tpu_custom_call" | custom-call | tf_op jit(solution)/shard_map/assemble/pallas_call | solution.py:345
  (24 shorter events, 1.8 us)
Async XLA Ops:
  0.0 1.0 copy-start
  1.0 0.7 copy-start.1
  1.7 0.7 copy-start.2
  3.4 24.5 %collective-permute-start.1 = (f32[512,256]{1,0:T(8,128)S(1)}, f32[512,256]{1,0:T(8,128)S(1)}, u32[]{:S(2)}, u32[]{:S(2)}) collective-permute-start(f32[512,256]{1,0:T(8,128)S(1)} %get-tuple-element.14.refs_0_), channel_id=1, source_target_pairs={{32,0},{64,32},{96,64},{0,96},{160,128},{192,160},{224,192},{128,2... | collective-permute-start | bytes 1572872 | tf_op jit(solution)/shard_map/ppermute | solution.py:361
  6.7 21.2 %collective-permute-start.2 = (f32[512,256]{1,0:T(8,128)S(1)}, f32[512,256]{1,0:T(8,128)S(1)}, u32[]{:S(2)}, u32[]{:S(2)}) collective-permute-start(f32[512,256]{1,0:T(8,128)S(1)} %get-tuple-element.14.refs_0_), channel_id=1, source_target_pairs={{224,0},{128,32},{160,64},{192,96},{96,128},{0,160},{32,192},{64,2... | collective-permute-start | bytes 1572872 | tf_op jit(solution)/shard_map/ppermute | solution.py:361
  20.6 27.8 %collective-permute-start.4 = (f32[512,256]{1,0:T(8,128)S(1)}, f32[512,256]{1,0:T(8,128)S(1)}, u32[]{:S(2)}, u32[]{:S(2)}) collective-permute-start(f32[512,256]{1,0:T(8,128)S(1)} %get-tuple-element.14.refs_0_), channel_id=1, source_target_pairs={{64,0},{96,32},{192,64},{224,96},{0,128},{32,160},{128,192},{160,2... | collective-permute-start | bytes 1572872 | tf_op jit(solution)/shard_map/ppermute | solution.py:361
  22.0 26.5 %collective-permute-start.5 = (f32[512,256]{1,0:T(8,128)S(1)}, f32[512,256]{1,0:T(8,128)S(1)}, u32[]{:S(2)}, u32[]{:S(2)}) collective-permute-start(f32[512,256]{1,0:T(8,128)S(1)} %get-tuple-element.14.refs_0_), channel_id=1, source_target_pairs={{192,0},{224,32},{128,64},{160,96},{64,128},{96,160},{0,192},{32,2... | collective-permute-start | bytes 1572872 | tf_op jit(solution)/shard_map/ppermute | solution.py:361
  26.1 40.8 %collective-permute-start = (f32[2,136,256]{2,1,0:T(8,128)S(1)}, f32[2,136,256]{2,1,0:T(8,128)S(1)}, u32[]{:S(2)}, u32[]{:S(2)}) collective-permute-start(f32[2,136,256]{2,1,0:T(8,128)S(1)} %diagonal.1.own0), channel_id=1, source_target_pairs={{0,1},{1,0},{2,3},{3,2},{4,5},{5,4},{6,7},{7,6},{8,9},{9,8},{10,11... | collective-permute-start | bytes 835592 | tf_op jit(solution)/shard_map/ppermute | solution.py:364
  57.0 9.9 %collective-permute-start.6 = (f32[1,136,384]{2,1,0:T(8,128)S(1)}, f32[1,136,384]{2,1,0:T(8,128)S(1)}, u32[]{:S(2)}, u32[]{:S(2)}) collective-permute-start(f32[1,136,384]{2,1,0:T(8,128)S(1)} %second1.1), channel_id=1, source_target_pairs={{0,1},{1,0},{2,3},{3,2},{4,5},{5,4},{6,7},{7,6},{8,9},{9,8},{10,11... | collective-permute-start | bytes 626696 | tf_op jit(solution)/shard_map/ppermute | solution.py:364
  57.7 9.2 %collective-permute-start.3 = (f32[2,136,512]{2,1,0:T(8,128)S(1)}, f32[2,136,512]{2,1,0:T(8,128)S(1)}, u32[]{:S(2)}, u32[]{:S(2)}) collective-permute-start(f32[2,136,512]{2,1,0:T(8,128)S(1)} %first.1.own1), channel_id=1, source_target_pairs={{0,1},{1,0},{2,3},{3,2},{4,5},{5,4},{6,7},{7,6},{8,9},{9,8},{10,11... | collective-permute-start | bytes 1671176 | tf_op jit(solution)/shard_map/ppermute | solution.py:364
  118.2 11.8 %collective-permute-start.8 = (f32[128,256]{1,0:T(8,128)S(1)}, f32[128,256]{1,0:T(8,128)S(1)}, u32[]{:S(2)}, u32[]{:S(2)}) collective-permute-start(f32[128,256]{1,0:T(8,128)S(1)} %get-tuple-element.19), channel_id=1, source_target_pairs={{0,32},{32,64},{64,96},{96,0},{128,160},{160,192},{192,224},{224,1... | collective-permute-start | bytes 393224 | tf_op jit(solution)/shard_map/ppermute | solution.py:394
  119.8 10.3 %collective-permute-start.9 = (f32[128,256]{1,0:T(8,128)S(1)}, f32[128,256]{1,0:T(8,128)S(1)}, u32[]{:S(2)}, u32[]{:S(2)}) collective-permute-start(f32[128,256]{1,0:T(8,128)S(1)} %get-tuple-element.18), channel_id=1, source_target_pairs={{0,224},{32,128},{64,160},{96,192},{128,96},{160,0},{192,32},{224,... | collective-permute-start | bytes 393224 | tf_op jit(solution)/shard_map/ppermute | solution.py:394
  120.6 15.3 %collective-permute-start.7 = (f32[128,1152]{1,0:T(8,128)S(1)}, f32[128,1152]{1,0:T(8,128)S(1)}, u32[]{:S(2)}, u32[]{:S(2)}) collective-permute-start(f32[128,1152]{1,0:T(8,128)S(1)} %bitcast.5), channel_id=1, source_target_pairs={{0,1},{1,0},{2,3},{3,2},{4,5},{5,4},{6,7},{7,6},{8,9},{9,8},{10,11... | collective-permute-start | bytes 1769480 | tf_op jit(solution)/shard_map/ppermute | solution.py:364
  124.1 7.8 %collective-permute-start.10 = (f32[128,256]{1,0:T(8,128)S(1)}, f32[128,256]{1,0:T(8,128)S(1)}, u32[]{:S(2)}, u32[]{:S(2)}) collective-permute-start(f32[128,256]{1,0:T(8,128)S(1)} %get-tuple-element.17), channel_id=1, source_target_pairs={{0,64},{32,96},{64,192},{96,224},{128,0},{160,32},{192,128},{224,1... | collective-permute-start | bytes 393224 | tf_op jit(solution)/shard_map/ppermute | solution.py:394
  125.6 9.4 %collective-permute-start.11 = (f32[128,128]{1,0:T(8,128)S(1)}, f32[128,128]{1,0:T(8,128)S(1)}, u32[]{:S(2)}, u32[]{:S(2)}) collective-permute-start(f32[128,128]{1,0:T(8,128)S(1)} %slice.19), channel_id=1, source_target_pairs={{0,192},{32,224},{64,128},{96,160},{128,64},{160,96},{192,0},{224,... | collective-permute-start | bytes 196616 | tf_op jit(solution)/shard_map/ppermute | solution.py:394
  135.0 2.3 %collective-permute-start.12 = (f32[128,896]{1,0:T(8,128)S(1)}, f32[128,896]{1,0:T(8,128)S(1)}, u32[]{:S(2)}, u32[]{:S(2)}) collective-permute-start(f32[128,896]{1,0:T(8,128)S(1)} %constant_dynamic-update-slice_fusion.own_swapped), channel_id=1, source_target_pairs={{0,1},{1,0},{2,3},{3,2},{4,5},{5,4},{6,7},{7,6},{8,9},{9,8},{10,11... | collective-permute-start | bytes 1376264 | tf_op jit(solution)/shard_map/ppermute | solution.py:364
